TPU v7x, 32 devices: a whole 2x2x4 slice. The times are simulated.
32 devices in a mesh: seq: 8 (over z, y), ch: 4 (over x, core).
Axes of the slice: x: 2, y: 2, z: 4, core: 2. Of those that a mesh axis runs over, the one named last changes fastest.
Arguments:
- genome: int32 [2048, 128], P('seq'), may hold values from 0 to 3
- stem_weight: bfloat16 [768, 512], P('ch'), may hold values from -0.5 to 0.5
- dilated_filter_weight: bfloat16 [5, 3, 768, 768], P(None, None, 'ch'), may hold values from -0.125 to 0.125
- head_weight: bfloat16 [768, 5313], P('ch'), may hold values from -0.21875 to 0.21875
- window_start: int32 [128], replicated, may hold values from 0 to 2032
- window_track: int32 [128], replicated, may hold values from 0 to 5312
- targets: float32 [128], replicated, may hold values from 0 to 3
Outputs:
- window_score: float32 [128], replicated
- conv_grad: float32 [5, 3, 768, 768], P(None, None, 'ch', 'seq')
- stem_grad: float32 [768, 512], P('ch')
- head_grad: float32 [768, 5313], P('ch')
Inputs may be any that keep to these rules, and one draw needn't show every extreme that they name: `window_start`: each window lies inside the sequence.
All inputs are finite; a program needn't handle non-finite values.
Results may differ from a plain program's by a relative error of at most 0.0037.
Values may be sent and summed in bfloat16 or wider, within the bound.
No kernel may reach another device: no remote copies, remote signals or barrier semaphores. Data moves between devices by JAX's collectives and lax.ppermute only.
A program may use at most 128 MiB of HBM per device.

v0:
```python
import jax
import jax.numpy as jnp
from jax import lax
from jax.experimental import pallas as pl
from jax.experimental.pallas import tpu as pltpu
from jax.sharding import PartitionSpec as P

LAYERS = 5
WIN = 16
CORES = 2
VMEM = 12 << 20

bf16 = jnp.bfloat16
f32 = jnp.float32


def dilations(shard_rows):
    return (shard_rows // 8, shard_rows // 2, shard_rows, 2 * shard_rows, 4 * shard_rows)


def core_swap(value):
    count = lax.axis_size("ch")
    return lax.ppermute(value, "ch", [(i, i ^ 1) for i in range(count)])


def chip_shift(value, by):
    count = lax.axis_size("ch")
    return lax.ppermute(value, "ch", [(i, (i + CORES * by) % count) for i in range(count)])


def seq_swap(value, bit):
    count = lax.axis_size("seq")
    return lax.ppermute(value, "seq", [(i, i ^ bit) for i in range(count)])


def choose(index, options):
    picked = options[0]
    for place, option in enumerate(options[1:], 1):
        picked = jnp.where(index == place, option, picked)
    return picked


def rolled(field, by):
    if by == 0:
        return field
    blank = jnp.zeros((abs(by),) + field.shape[1:], field.dtype)
    if by > 0:
        return jnp.concatenate([field[by:], blank], axis=0)
    return jnp.concatenate([blank, field[:by]], axis=0)


def tied(*values):
    return lax.optimization_barrier(values)


def by_strand(strand, own, sibling):
    return [jnp.where(strand == 0, own, sibling), jnp.where(strand == 0, sibling, own)]


def pieces(value):
    high = value.astype(bf16)
    rest = value - high.astype(f32)
    middle = rest.astype(bf16)
    return high, middle, (rest - middle.astype(f32)).astype(bf16)


def run(body, outs, *values, inside=True):
    if not inside:
        return body(jnp.roll, *values)

    def kernel(*refs):
        results = body(pltpu.roll, *[ref[...] for ref in refs[: len(values)]])
        for ref, result in zip(refs[len(values) :], results):
            ref[...] = result

    return pl.pallas_call(
        kernel,
        out_shape=[jax.ShapeDtypeStruct(shape, kind) for shape, kind in outs],
        compiler_params=pltpu.CompilerParams(vmem_limit_bytes=VMEM),
    )(*values)


def moved(roll, field, by):
    if by == 0:
        return field
    rows = field.shape[0]
    row = lax.broadcasted_iota(jnp.int32, field.shape, 0)
    there = (row + by >= 0) & (row + by < rows)
    return jnp.where(there, roll(field, (-by) % rows, 0), 0.0)


def slope_of_gelu(value):
    scale = 0.7978845608028654
    bend = jnp.tanh(scale * (value + 0.044715 * value * value * value))
    return 0.5 * (1.0 + bend) + 0.5 * value * (1.0 - bend * bend) * scale * (
        1.0 + 3 * 0.044715 * value * value
    )


def back_body(reach, chips, first):
    def body(roll, chip, grad, *rest):
        if first:
            (taps,) = rest
        else:
            mine, received, stream, taps = rest
            through = mine
            for part in range(chips - 1):
                through = through + received[part].astype(f32)
            grad = grad + through * slope_of_gelu(stream)
        upstream = grad.astype(bf16)
        wide = upstream.astype(f32)
        fields = [moved(roll, wide, (1 - tap) * reach).astype(bf16) for tap in range(3)]
        back = jnp.dot(
            jnp.concatenate(fields, axis=1),
            taps.reshape(-1, taps.shape[-1]),
            preferred_element_type=f32,
        )
        width = grad.shape[1]
        parts = [back[:, i * width : (i + 1) * width] for i in range(chips)]
        index = chip[0, 0]
        sends = [
            choose((index + by) % chips, parts).astype(bf16)[None] for by in range(1, chips)
        ]
        sends = sends[0] if chips == 2 else jnp.concatenate(sends)
        return grad, upstream, choose(index, parts), sends

    return body


def side_taps(roll, upstream, side, reach, quarter):
    shape = (upstream.shape[1], 3 * quarter)
    source = lax.broadcasted_iota(jnp.int32, shape, 0)
    target = lax.broadcasted_iota(jnp.int32, shape, 1)
    tap = (target >= quarter).astype(jnp.int32) + (target >= 2 * quarter).astype(jnp.int32)
    spread = (source == side * quarter + target - tap * quarter).astype(f32).astype(bf16)
    wide = jnp.dot(upstream, spread, preferred_element_type=f32)
    lane = lax.broadcasted_iota(jnp.int32, wide.shape, 1)
    low, high = moved(roll, wide, reach), moved(roll, wide, -reach)
    return jnp.where(lane < quarter, low, jnp.where(lane < 2 * quarter, wide, high)).astype(bf16)


def filter_theirs(active, upstream, strand, reach, quarter):
    def body(roll, strand, active, upstream):
        taps = side_taps(roll, upstream, 1 - strand[0, 0], reach, quarter)
        return (jnp.dot(active, taps, preferred_element_type=f32).astype(bf16),)

    return run(body, [((active.shape[0], 3 * quarter), bf16)], strand, active, upstream)[0]


def filter_ours(active, upstream, strand, theirs, reach, quarter):
    half = active.shape[0] // 2

    def body(roll, strand, active, upstream, theirs):
        taps = side_taps(roll, upstream, strand[0, 0], reach, quarter)
        keep = jnp.dot(active[:half], taps, preferred_element_type=f32)
        send = jnp.dot(active[half:], taps, preferred_element_type=f32)
        return (
            keep + theirs[:half].astype(f32),
            (send + theirs[half:].astype(f32)).astype(bf16),
        )

    shape = (half, 3 * quarter)
    return run(body, [(shape, f32), (shape, bf16)], strand, active, upstream, theirs)


def last_body(chips, quarter):
    def body(roll, strand, grad, mine, received, stream, letters):
        through = mine
        for part in range(chips - 1):
            through = through + received[part].astype(f32)
        grad = grad + through * slope_of_gelu(stream)
        stem = jnp.dot(grad.T.astype(bf16), letters, preferred_element_type=f32)
        parts = [stem[:quarter], stem[quarter:]]
        return choose(strand[0, 0], parts), choose(1 - strand[0, 0], parts).astype(bf16)

    return body


class BlockSum:
    def __init__(self, kept, sent, slot):
        self.kept, self.sent, self.slot = kept, sent, slot
        self.bit = 1
        self.received = None

    def start(self):
        if self.sent is not None and self.received is None:
            self.received = seq_swap(self.sent, self.bit)

    def last(self):
        return 2 * self.bit >= lax.axis_size("seq")

    def join(self):
        if self.last():
            self.sent = None
            return

        def body(roll, kept, received):
            total = kept + received.astype(f32)
            half = total.shape[0] // 2
            return total[:half], total[half:].astype(bf16)

        shape = (self.kept.shape[0] // 2, self.kept.shape[1])
        self.kept, self.sent = run(body, [(shape, f32), (shape, bf16)], self.kept, self.received)
        self.bit *= 2
        self.received = None


def assemble(sums, quarter):
    block = sums[0].kept.shape[0]
    taps = sums[0].kept.shape[1] // quarter
    count = len(sums)

    def kernel(*refs):
        out = refs[-1]
        for layer in range(count):
            total = refs[layer][...] + refs[count + layer][...].astype(f32)
            out[layer] = total.T.reshape(taps, quarter, block)

    return pl.pallas_call(
        kernel,
        out_shape=jax.ShapeDtypeStruct((count, taps, quarter, block), f32),
        compiler_params=pltpu.CompilerParams(vmem_limit_bytes=VMEM),
    )(*[s.kept for s in sums], *[s.received for s in sums])


def shards(
    genome, stem_weight, dilated_filter_weight, head_weight, window_start, window_track, targets
):
    shard_rows, pool = genome.shape
    seqs = lax.axis_size("seq")
    chips = lax.axis_size("ch") // CORES
    seq = lax.axis_index("seq")
    strand = lax.axis_index("ch") % CORES
    chip = lax.axis_index("ch") // CORES
    spans = dilations(shard_rows)
    classes = spans[0]
    own_classes = classes // seqs
    steps = shard_rows // classes
    reach = tuple(span // classes * own_classes for span in spans)
    quarter = stem_weight.shape[0]
    channels = dilated_filter_weight.shape[3]
    block = channels // seqs
    tracks = head_weight.shape[1]

    blocks = (
        genome.astype(bf16)
        .reshape(steps, seqs, own_classes, pool)
        .transpose(1, 0, 2, 3)
        .reshape(seqs, steps * own_classes, pool)
    )
    blocks = lax.all_to_all(blocks, "seq", 0, 0, tiled=True)

    stem_own = [stem_weight] + [chip_shift(stem_weight, by) for by in range(1, chips)]
    stem_pairs = [
        jnp.concatenate(by_strand(strand, part, core_swap(part))) for part in stem_own
    ]
    stem_full = jnp.concatenate([choose((chip - p) % chips, stem_pairs) for p in range(chips)])

    sibling_filter = core_swap(dilated_filter_weight)

    own_filter = dilated_filter_weight

    def filter_of(layer):
        return jnp.concatenate(
            by_strand(strand, own_filter[layer], sibling_filter[layer]), axis=1
        )

    bases = blocks.reshape(shard_rows, pool)
    row = jnp.arange(shard_rows, dtype=jnp.int32)
    step_of = row // own_classes
    step_of = jnp.where(strand == 0, step_of, shard_rows // own_classes - 1 - step_of)
    class_of = row % own_classes
    source_row = step_of * own_classes + class_of
    order = (source_row[:, None] == row[None, :]).astype(bf16)
    letter = jnp.arange(4 * pool, dtype=jnp.int32)
    place = jnp.where(strand == 0, letter // 4, pool - 1 - letter // 4)
    spread_place = (jnp.arange(pool, dtype=jnp.int32)[:, None] == place[None, :]).astype(bf16)
    base_of = jnp.where(strand == 0, letter % 4, 3 - letter % 4)
    ordered = jnp.dot(order, bases, preferred_element_type=f32).astype(bf16)
    wide = jnp.dot(ordered, spread_place, preferred_element_type=f32)
    letters = (wide == base_of[None, :].astype(f32)).astype(bf16)
    position = step_of * classes + seq * own_classes + class_of

    member = (
        (position[None, :] >= window_start[:, None])
        & (position[None, :] < window_start[:, None] + WIN)
    ).astype(bf16)
    counts = jnp.sum((window_track[:, None] == window_track[None, :]).astype(f32), axis=1)
    at_track = (
        jnp.arange(tracks, dtype=jnp.int32)[None, :] == window_track[:, None]
    ).astype(bf16)

    bits = seqs.bit_length() - 1
    slot = jnp.arange(channels, dtype=jnp.int32) // block
    away = sum(((slot >> (bits - 1 - b)) & 1) << b for b in range(bits))
    wanted = (seq ^ away) * block + jnp.arange(channels, dtype=jnp.int32) % block
    by_distance = (
        jnp.arange(channels, dtype=jnp.int32)[:, None] == wanted[None, :]
    ).astype(bf16)

    whole = lax.dot_general(
        letters, stem_full, (((1,), (1,)), ((), ())), preferred_element_type=f32
    )
    active = jax.nn.gelu(whole).astype(bf16)
    stream = choose(chip, jnp.split(whole, chips, axis=1))
    filters = [filter_of(0)]
    streams = []
    actives = []
    for layer in range(LAYERS):
        streams.append(stream)
        for tap in range(3):
            stream = stream + lax.dot_general(
                rolled(active, (tap - 1) * reach[layer]),
                filters[layer][tap],
                (((1,), (1,)), ((), ())),
                preferred_element_type=f32,
            )
        if layer < LAYERS - 1:
            own = jax.nn.gelu(stream).astype(bf16)
            own, own_filter, sibling_filter, by_distance, at_track = tied(
                own, own_filter, sibling_filter, by_distance, at_track
            )
            parts = [chip_shift(own, by) for by in range(1, chips)]
            beside = [
                filter_of(layer + 1),
                lax.dot_general(
                    by_distance, active, (((0,), (1,)), ((), ())), preferred_element_type=f32
                ).astype(bf16),
            ]
            if layer == 1:
                columns = lax.dot_general(
                    head_weight, at_track, (((1,), (1,)), ((), ())), preferred_element_type=f32
                ).astype(bf16)
                beside.append(columns)
            if layer == 2:
                beside.append(jnp.concatenate(by_strand(strand, columns, core_swap(columns))))
            parts, beside = tied(parts, beside)
            filters.append(beside[0])
            actives.append(beside[1])
            if layer == 1:
                columns = beside[2]
            if layer == 2:
                half_columns = beside[2]
            parts = [own] + list(parts)
            active = jnp.concatenate(
                [choose((chip - p) % chips, parts) for p in range(chips)], axis=1
            )

    pooled = (
        lax.dot_general(
            jnp.concatenate(pieces(stream)),
            jnp.concatenate([member] * 3, axis=1),
            (((0,), (1,)), ((), ())),
            preferred_element_type=f32,
        )
        / WIN
    )
    partial_score = 0.5 * jnp.sum(pooled * half_columns.astype(f32), axis=0)
    everyone = seqs * chips * CORES
    partial_score = jnp.broadcast_to(partial_score, (everyone,) + partial_score.shape)
    partial_score, pooled, active = tied(partial_score, pooled, active)
    scores = lax.all_to_all(partial_score, ("seq", "ch"), 0, 0, tiled=True)
    pooled_parts = [pooled[:quarter], pooled[quarter:]]
    pooled_own = choose(strand, pooled_parts) + core_swap(choose(1 - strand, pooled_parts))
    last_active = lax.dot_general(
        by_distance, active, (((0,), (1,)), ((), ())), preferred_element_type=f32
    ).astype(bf16)
    wide_columns = jnp.concatenate([half_columns] * 3, axis=1)
    scores, pooled_own, last_active, wide_columns = tied(
        scores, pooled_own, last_active, wide_columns
    )
    actives.append(last_active)
    window_score = jnp.sum(scores, axis=0)
    loss_slope = (jnp.exp(window_score) - targets) / counts

    grad = lax.dot_general(
        jnp.concatenate(pieces((0.5 / WIN * loss_slope)[:, None] * member.astype(f32))),
        wide_columns,
        (((0,), (1,)), ((), ())),
        preferred_element_type=f32,
    )
    sums = []
    pooled_bit = 1
    aligned = (channels // chips) % 128 == 0
    shape = (shard_rows, channels // chips)
    back_outs = [(shape, f32), (shape, bf16), (shape, f32), ((chips - 1,) + shape, bf16)]
    chip_word = jnp.reshape(chip, (1, 1))
    strand_word = jnp.reshape(strand, (1, 1))
    state = (grad,)
    for layer in reversed(range(LAYERS)):
        first = layer == LAYERS - 1
        grad, upstream, mine, sends = run(
            back_body(reach[layer], chips, first),
            back_outs,
            chip_word,
            *state,
            filters[layer],
            inside=aligned,
        )
        sends, upstream = tied(sends, upstream)
        received = jnp.stack([chip_shift(sends[by - 1], by) for by in range(1, chips)])
        for s in sums:
            s.start()
        if pooled_bit < seqs:
            pooled_received = seq_swap(pooled_own, pooled_bit)
            pooled_bit *= 2
        else:
            pooled_received = jnp.zeros_like(pooled_own)
        theirs = core_swap(
            filter_theirs(actives[layer], upstream, strand_word, reach[layer], quarter)
        )
        keep, send = filter_ours(
            actives[layer], upstream, strand_word, theirs, reach[layer], quarter
        )
        due = [s for s in sums if s.sent is not None and (s.bit > 1 or layer < LAYERS - 2 - s.slot)]
        received, due_received, pooled_received, keep, send = tied(
            received, [s.received for s in due], pooled_received, keep, send
        )
        for s, got in zip(due, due_received):
            s.received = got
            s.join()
        pooled_own = pooled_own + pooled_received
        sums.append(BlockSum(keep, send, LAYERS - 1 - layer))
        state = (grad, mine, received, streams[layer])

    for s in sums:
        s.start()
    stem_shape = (quarter, letters.shape[1])
    stem_keep, stem_away = run(
        last_body(chips, quarter),
        [(stem_shape, f32), (stem_shape, bf16)],
        strand_word,
        *state,
        letters,
        inside=aligned,
    )
    stem_own = stem_keep + core_swap(stem_away).astype(f32)
    stem_send = stem_own.astype(bf16).reshape(seqs, quarter // seqs, -1)
    stem_blocks = lax.all_to_all(stem_send, "seq", 0, 0, tiled=True)
    stem_blocks, seq_received, pooled_own = tied(
        stem_blocks, [s.received for s in sums], pooled_own
    )
    for s, got in zip(sums, seq_received):
        s.received = got
        if not s.last():
            s.join()
            s.start()
    stem_block = jnp.sum(stem_blocks.astype(f32), axis=0)
    stem_grad = lax.all_to_all(
        jnp.broadcast_to(stem_block, (seqs,) + stem_block.shape), "seq", 0, 0, tiled=True
    ).reshape(quarter, -1)
    while pooled_bit < seqs:
        pooled_own = pooled_own + seq_swap(pooled_own, pooled_bit)
        pooled_bit *= 2
    head_grad = lax.dot_general(
        jnp.concatenate(pieces(0.5 * loss_slope[None, :] * pooled_own), axis=1),
        jnp.concatenate([at_track] * 3),
        (((1,), (0,)), ((), ())),
        preferred_element_type=f32,
    )
    for s in sums:
        while not s.last():
            s.join()
            s.start()
    conv_grad = assemble(sums[::-1], quarter)
    return (window_score, conv_grad, stem_grad, head_grad)


def solution(mesh):
    return jax.shard_map(
        shards,
        mesh=mesh,
        in_specs=(
            P("seq", None),
            P("ch", None),
            P(None, None, "ch", None),
            P("ch", None),
            P(),
            P(),
            P(),
        ),
        out_specs=(P(), P(None, None, "ch", "seq"), P("ch", None), P("ch", None)),
        check_vma=False,
    )
```

profile of v0, /device:TPU:0, one launch (start us, length us, event | category | flops | bytes accessed | tf_op | source)
XLA Modules:
  0.0 246.4 jit_solution(15048877970902692082)
XLA Ops:
  1.2 2.6 %collective-permute-start = (bf16[192,512]{1,0:T(8,128)(2,1)}, bf16[192,512]{1,0:T(8,128)(2,1)}, u32[]{:S(2)}, u32[]{:S(2)}) collective-permute-start(bf16[192,512]{1,0:T(8,128)(2,1)} %param.8), channel_id=1, source_target_pairs={{0,2},{1,3},{2,0},{3,1},{4,6},{5,7},{6,4},{7,5},{8,10},{9,11},{10,... | collective-permute-start | bytes 589832 | tf_op jit(solution)/shard_map/ppermute | solution.py:28
  5.5 5.8 %all-to-all-start = ((bf16[8,32,128]{2,1,0:T(8,128)(2,1)}), bf16[8,32,128]{2,1,0:T(8,128)(2,1)S(1)}, u32[]{:S(2)}, u32[]{:S(2)}) async-start(bf16[8,32,128]{2,1,0:T(8,128)(2,1)} %copy.26), calls=%async_computation | async-start | bytes 131072 | tf_op jit(solution)/shard_map/all_to_all | solution.py:251
  16.1 2.2 all-to-all-done
  29.4 3.7 %collective-permute-done.4 = bf16[256,384]{1,0:T(8,128)(2,1)S(1)} collective-permute-done((bf16[256,384]{1,0:T(8,128)(2,1)S(1)}, bf16[256,384]{1,0:T(8,128)(2,1)S(1)}, u32[]{:S(2)}, u32[]{:S(2)}) %collective-permute-start.4) | collective-permute-done | bytes 196640 | tf_op jit(solution)/shard_map/ppermute | solution.py:28
  38.5 2.1 collective-permute-done.5
  45.3 5.3 %collective-permute-done.6 = bf16[256,384]{1,0:T(8,128)(2,1)S(1)} collective-permute-done((bf16[256,384]{1,0:T(8,128)(2,1)S(1)}, bf16[256,384]{1,0:T(8,128)(2,1)S(1)}, u32[]{:S(2)}, u32[]{:S(2)}) %collective-permute-start.6) | collective-permute-done | bytes 196640 | tf_op jit(solution)/shard_map/ppermute | solution.py:28
  56.0 3.8 %collective-permute-done.8 = bf16[256,384]{1,0:T(8,128)(2,1)S(1)} collective-permute-done((bf16[256,384]{1,0:T(8,128)(2,1)S(1)}, bf16[256,384]{1,0:T(8,128)(2,1)S(1)}, u32[]{:S(2)}, u32[]{:S(2)}) %collective-permute-start.8) | collective-permute-done | bytes 196640 | tf_op jit(solution)/shard_map/ppermute | solution.py:28
  64.3 3.1 %all-to-all-start.1 = ((f32[32,1,128]{2,1,0:T(1,128)}), f32[32,1,128]{2,1,0:T(1,128)S(1)}, u32[]{:S(2)}, u32[]{:S(2)}) async-start(f32[32,1,128]{2,1,0:T(1,128)} %bitcast.30), calls=%async_computation.1 | async-start | bytes 32768 | tf_op jit(solution)/shard_map/all_to_all | solution.py:362
  69.1 5.5 %all-to-all-done.1 = f32[32,1,128]{2,1,0:T(1,128)S(1)} async-done(((f32[32,1,128]{2,1,0:T(1,128)}), f32[32,1,128]{2,1,0:T(1,128)S(1)}, u32[]{:S(2)}, u32[]{:S(2)}) %all-to-all-start.1) | async-done | bytes 16416 | tf_op jit(solution)/shard_map/all_to_all | solution.py:362
  86.6 2.2 copy.28.refs_3_
  94.6 2.5 %shard_map.105 = (f32[256,384]{1,0:T(8,128)S(1)}, bf16[256,384]{1,0:T(8,128)(2,1)S(1)}, f32[256,384]{1,0:T(8,128)S(1)}, bf16[1,256,384]{2,1,0:T(8,128)(2,1)}) custom-call(s32[1,1]{1,0:T(1,128)} %bitcast.32.refs_0_, f32[256,384]{1,0:T(8,128)S(1)} %copy-done.64, f32[256,384]{1,0:T(8,128)S(1)} %copy-done.66, bf16[1,256,384]{2,1,0:T(8,128)(2,1)} %bitcast.34.refs_3_, ...), custom_call_target="tpu_custom_call" | custom-call | tf_op jit(solution)/shard_map/pallas_call | solution.py:76
  109.4 2.5 %shard_map.108 = (f32[256,384]{1,0:T(8,128)S(1)}, bf16[256,384]{1,0:T(8,128)(2,1)S(1)}, f32[256,384]{1,0:T(8,128)S(1)}, bf16[1,256,384]{2,1,0:T(8,128)(2,1)}) custom-call(s32[1,1]{1,0:T(1,128)} %bitcast.32.refs_0_, f32[256,384]{1,0:T(8,128)S(1)} %copy-done.60, f32[256,384]{1,0:T(8,128)S(1)} %copy-done.62, bf16[1,256,384]{2,1,0:T(8,128)(2,1)} %bitcast.37.refs_3_, ...), custom_call_target="tpu_custom_call" | custom-call | tf_op jit(solution)/shard_map/pallas_call | solution.py:76
  123.4 6.3 %collective-permute-done.17.refs_1_ = bf16[384,576]{1,0:T(8,128)(2,1)} collective-permute-done((bf16[384,576]{1,0:T(8,128)(2,1)}, bf16[384,576]{1,0:T(8,128)(2,1)}, u32[]{:S(2)}, u32[]{:S(2)}) %collective-permute-start.17) | collective-permute-done | bytes 442400 | tf_op jit(solution)/shard_map/ppermute | solution.py:33
  130.7 2.5 shard_map.111
  150.9 1.8 shard_map.115
  168.6 2.6 %collective-permute-done.27.refs_1_ = bf16[384,576]{1,0:T(8,128)(2,1)} collective-permute-done((bf16[384,576]{1,0:T(8,128)(2,1)}, bf16[384,576]{1,0:T(8,128)(2,1)}, u32[]{:S(2)}, u32[]{:S(2)}) %collective-permute-start.27) | collective-permute-done | bytes 442400 | tf_op jit(solution)/shard_map/ppermute | solution.py:33
  171.1 2.4 collective-permute-done.25.refs_9_
  180.6 4.0 %all-to-all-start.2 = ((bf16[8,24,512]{2,1,0:T(8,128)(2,1)}), bf16[8,24,512]{2,1,0:T(8,128)(2,1)}, u32[]{:S(2)}, u32[]{:S(2)}) async-start(bf16[8,24,512]{2,1,0:T(8,128)(2,1)} %bitcast.44), calls=%async_computation.2 | async-start | bytes 393216 | tf_op jit(solution)/shard_map/all_to_all | solution.py:439
  185.8 2.0 collective-permute-start.31
  187.8 2.5 collective-permute-start.30
  191.3 2.5 %collective-permute-done.32.refs_1_ = bf16[384,576]{1,0:T(8,128)(2,1)} collective-permute-done((bf16[384,576]{1,0:T(8,128)(2,1)}, bf16[384,576]{1,0:T(8,128)(2,1)}, u32[]{:S(2)}, u32[]{:S(2)}) %collective-permute-start.32) | collective-permute-done | bytes 442400 | tf_op jit(solution)/shard_map/ppermute | solution.py:33
  193.7 2.4 collective-permute-done.30.refs_8_
  196.1 2.7 %collective-permute-done.31.refs_1_ = bf16[192,576]{1,0:T(8,128)(2,1)S(1)} collective-permute-done((bf16[192,576]{1,0:T(8,128)(2,1)S(1)}, bf16[192,576]{1,0:T(8,128)(2,1)S(1)}, u32[]{:S(2)}, u32[]{:S(2)}) %collective-permute-start.31) | collective-permute-done | bytes 221216 | tf_op jit(solution)/shard_map/ppermute | solution.py:33
  199.6 4.6 %collective-permute-done.33.refs_1_ = bf16[384,576]{1,0:T(8,128)(2,1)} collective-permute-done((bf16[384,576]{1,0:T(8,128)(2,1)}, bf16[384,576]{1,0:T(8,128)(2,1)}, u32[]{:S(2)}, u32[]{:S(2)}) %collective-permute-start.33) | collective-permute-done | bytes 442400 | tf_op jit(solution)/shard_map/ppermute | solution.py:33
  206.2 4.1 %all-to-all-start.3 = ((f32[8,24,512]{2,1,0:T(8,128)}), f32[8,24,512]{2,1,0:T(8,128)}, u32[]{:S(2)}, u32[]{:S(2)}) async-start(f32[8,24,512]{2,1,0:T(8,128)} %broadcast_in_dim.5), calls=%async_computation.3 | async-start | bytes 786432 | tf_op jit(solution)/shard_map/all_to_all | solution.py:449
  211.3 2.9 %collective-permute-start.38 = (bf16[96,576]{1,0:T(8,128)(2,1)S(1)}, bf16[96,576]{1,0:T(8,128)(2,1)S(1)}, u32[]{:S(2)}, u32[]{:S(2)}) collective-permute-start(bf16[96,576]{1,0:T(8,128)(2,1)S(1)} %get-tuple-element.270), channel_id=1, source_target_pairs={{0,16},{4,20},{8,24},{12,28},{16,0},{20,4},{24,8},{28,12},{1,17},{... | collective-permute-start | bytes 331784 | tf_op jit(solution)/shard_map/ppermute | solution.py:33
  218.6 9.8 %collective-permute-done.35.refs_1_ = bf16[192,576]{1,0:T(8,128)(2,1)S(1)} collective-permute-done((bf16[192,576]{1,0:T(8,128)(2,1)S(1)}, bf16[192,576]{1,0:T(8,128)(2,1)S(1)}, u32[]{:S(2)}, u32[]{:S(2)}) %collective-permute-start.35) | collective-permute-done | bytes 221216 | tf_op jit(solution)/shard_map/ppermute | solution.py:33
  228.4 2.3 collective-permute-start.37
  230.7 4.1 %collective-permute-done.34.refs_1_ = bf16[192,576]{1,0:T(8,128)(2,1)S(1)} collective-permute-done((bf16[192,576]{1,0:T(8,128)(2,1)S(1)}, bf16[192,576]{1,0:T(8,128)(2,1)S(1)}, u32[]{:S(2)}, u32[]{:S(2)}) %collective-permute-start.34) | collective-permute-done | bytes 221216 | tf_op jit(solution)/shard_map/ppermute | solution.py:33
  236.0 2.8 %fusion = f32[192,5313]{1,0:T(8,128)} fusion(bf16[128,5313]{1,0:T(8,128)(2,1)S(1)} %copy-done.81, bf16[192,128]{1,0:T(8,128)(2,1)S(1)} %get-tuple-element.316, bf16[192,128]{1,0:T(8,128)(2,1)S(1)} %get-tuple-element.317, bf16[192,128]{1,0:T(8,128)(2,1)S(1)} %get-tuple-element.315), kind=kOutput, calls=%fused_computation | convolution fusion | flops 796117248 | bytes 5587968 | tf_op jit(solution)/shard_map/dot_general | solution.py:455
  238.7 3.3 %collective-permute-done.36.refs_5_ = bf16[96,576]{1,0:T(8,128)(2,1)S(1)} collective-permute-done((bf16[96,576]{1,0:T(8,128)(2,1)S(1)}, bf16[96,576]{1,0:T(8,128)(2,1)S(1)}, u32[]{:S(2)}, u32[]{:S(2)}) %collective-permute-start.36) | collective-permute-done | bytes 110624 | tf_op jit(solution)/shard_map/ppermute | solution.py:33
  242.0 2.6 %shard_map.128 = f32[5,3,192,96]{3,2,1,0:T(8,128)} custom-call(f32[96,576]{1,0:T(8,128)S(1)} %get-tuple-element.257.refs_0_, f32[96,576]{1,0:T(8,128)S(1)} %get-tuple-element.262.refs_1_, f32[96,576]{1,0:T(8,128)S(1)} %get-tuple-element.265.refs_2_, f32[96,576]{1,0:T(8,128)S(1)} %get-tuple-element.266.refs_3_, f32[96,576]{1,0:T(8,128)S(1)} %copy-done.69, ...), custom_call_target="tpu_custom_call" | custom-call | tf_op jit(solution)/shard_map/pallas_call | solution.py:219
  (358 shorter events, 135.3 us)
Async XLA Ops:
  0.7 22.2 %collective-permute-start.3 = (bf16[5,3,192,768]{3,2,1,0:T(8,128)(2,1)}, bf16[5,3,192,768]{3,2,1,0:T(8,128)(2,1)}, u32[]{:S(2)}, u32[]{:S(2)}) collective-permute-start(bf16[5,3,192,768]{3,2,1,0:T(8,128)(2,1)} %param.9), channel_id=1, source_target_pairs={{0,1},{1,0},{2,3},{3,2},{4,5},{5,4},{6,7},{7,6},{8,9},{9,8},{10,11... | collective-permute-start | bytes 13271048 | tf_op jit(solution)/shard_map/ppermute | solution.py:23
  1.2 18.2 %collective-permute-start = (bf16[192,512]{1,0:T(8,128)(2,1)}, bf16[192,512]{1,0:T(8,128)(2,1)}, u32[]{:S(2)}, u32[]{:S(2)}) collective-permute-start(bf16[192,512]{1,0:T(8,128)(2,1)} %param.8), channel_id=1, source_target_pairs={{0,2},{1,3},{2,0},{3,1},{4,6},{5,7},{6,4},{7,5},{8,10},{9,11},{10,... | collective-permute-start | bytes 589832 | tf_op jit(solution)/shard_map/ppermute | solution.py:28
  3.7 15.7 %collective-permute-start.2 = (bf16[192,512]{1,0:T(8,128)(2,1)}, bf16[192,512]{1,0:T(8,128)(2,1)}, u32[]{:S(2)}, u32[]{:S(2)}) collective-permute-start(bf16[192,512]{1,0:T(8,128)(2,1)} %param.8), channel_id=1, source_target_pairs={{0,1},{1,0},{2,3},{3,2},{4,5},{5,4},{6,7},{7,6},{8,9},{9,8},{10,11... | collective-permute-start | bytes 589832 | tf_op jit(solution)/shard_map/ppermute | solution.py:23
  5.5 12.7 %all-to-all-start = ((bf16[8,32,128]{2,1,0:T(8,128)(2,1)}), bf16[8,32,128]{2,1,0:T(8,128)(2,1)S(1)}, u32[]{:S(2)}, u32[]{:S(2)}) async-start(bf16[8,32,128]{2,1,0:T(8,128)(2,1)} %copy.26), calls=%async_computation | async-start | bytes 131072 | tf_op jit(solution)/shard_map/all_to_all | solution.py:251
  43.3 7.3 %collective-permute-start.6 = (bf16[256,384]{1,0:T(8,128)(2,1)S(1)}, bf16[256,384]{1,0:T(8,128)(2,1)S(1)}, u32[]{:S(2)}, u32[]{:S(2)}) collective-permute-start(bf16[256,384]{1,0:T(8,128)(2,1)S(1)} %get-tuple-element.154), channel_id=1, source_target_pairs={{0,2},{1,3},{2,0},{3,1},{4,6},{5,7},{6,4},{7,5},{8,10},{9,11},{10,... | collective-permute-start | bytes 589832 | tf_op jit(solution)/shard_map/ppermute | solution.py:28
  64.3 10.2 %all-to-all-start.1 = ((f32[32,1,128]{2,1,0:T(1,128)}), f32[32,1,128]{2,1,0:T(1,128)S(1)}, u32[]{:S(2)}, u32[]{:S(2)}) async-start(f32[32,1,128]{2,1,0:T(1,128)} %bitcast.30), calls=%async_computation.1 | async-start | bytes 32768 | tf_op jit(solution)/shard_map/all_to_all | solution.py:362
  83.8 10.7 %collective-permute-start.10 = (bf16[256,384]{1,0:T(8,128)(2,1)}, bf16[256,384]{1,0:T(8,128)(2,1)}, u32[]{:S(2)}, u32[]{:S(2)}) collective-permute-start(bf16[256,384]{1,0:T(8,128)(2,1)} %bitcast.113), channel_id=1, source_target_pairs={{0,2},{1,3},{2,0},{3,1},{4,6},{5,7},{6,4},{7,5},{8,10},{9,11},{10,... | collective-permute-start | bytes 589832 | tf_op jit(solution)/shard_map/ppermute | solution.py:28
  84.3 10.2 %collective-permute-start.11 = (f32[192,128]{1,0:T(8,128)}, f32[192,128]{1,0:T(8,128)}, u32[]{:S(2)}, u32[]{:S(2)}) collective-permute-start(f32[192,128]{1,0:T(8,128)} %select_add_fusion), channel_id=1, source_target_pairs={{0,4},{4,0},{8,12},{12,8},{16,20},{20,16},{24,28},{28,24},{1,5},{5... | collective-permute-start | bytes 294920 | tf_op jit(solution)/shard_map/ppermute | solution.py:33
  101.7 7.7 %collective-permute-start.13 = (bf16[256,384]{1,0:T(8,128)(2,1)}, bf16[256,384]{1,0:T(8,128)(2,1)}, u32[]{:S(2)}, u32[]{:S(2)}) collective-permute-start(bf16[256,384]{1,0:T(8,128)(2,1)} %bitcast.36), channel_id=1, source_target_pairs={{0,2},{1,3},{2,0},{3,1},{4,6},{5,7},{6,4},{7,5},{8,10},{9,11},{10,... | collective-permute-start | bytes 589832 | tf_op jit(solution)/shard_map/ppermute | solution.py:28
  115.8 13.9 %collective-permute-start.17 = (bf16[384,576]{1,0:T(8,128)(2,1)}, bf16[384,576]{1,0:T(8,128)(2,1)}, u32[]{:S(2)}, u32[]{:S(2)}) collective-permute-start(bf16[384,576]{1,0:T(8,128)(2,1)} %get-tuple-element.201), channel_id=1, source_target_pairs={{0,4},{4,0},{8,12},{12,8},{16,20},{20,16},{24,28},{28,24},{1,5},{5... | collective-permute-start | bytes 1327112 | tf_op jit(solution)/shard_map/ppermute | solution.py:33
  116.4 13.3 %collective-permute-start.16 = (bf16[256,384]{1,0:T(8,128)(2,1)}, bf16[256,384]{1,0:T(8,128)(2,1)}, u32[]{:S(2)}, u32[]{:S(2)}) collective-permute-start(bf16[256,384]{1,0:T(8,128)(2,1)} %bitcast.38), channel_id=1, source_target_pairs={{0,2},{1,3},{2,0},{3,1},{4,6},{5,7},{6,4},{7,5},{8,10},{9,11},{10,... | collective-permute-start | bytes 589832 | tf_op jit(solution)/shard_map/ppermute | solution.py:28
  119.5 10.2 %collective-permute-start.18 = (f32[192,128]{1,0:T(8,128)}, f32[192,128]{1,0:T(8,128)}, u32[]{:S(2)}, u32[]{:S(2)}) collective-permute-start(f32[192,128]{1,0:T(8,128)} %add.293), channel_id=1, source_target_pairs={{0,16},{4,20},{8,24},{12,28},{16,0},{20,4},{24,8},{28,12},{1,17},{... | collective-permute-start | bytes 294920 | tf_op jit(solution)/shard_map/ppermute | solution.py:33
  136.9 7.4 %collective-permute-start.23 = (bf16[768,576]{0,1:T(8,128)(2,1)}, bf16[768,576]{0,1:T(8,128)(2,1)}, u32[]{:S(2)}, u32[]{:S(2)}) collective-permute-start(bf16[768,576]{0,1:T(8,128)(2,1)} %copy.33), channel_id=1, source_target_pairs={{0,1},{1,0},{2,3},{3,2},{4,5},{5,4},{6,7},{7,6},{8,9},{9,8},{10,11... | collective-permute-start | bytes 2654216 | tf_op jit(solution)/shard_map/ppermute | solution.py:23
  136.9 13.9 %collective-permute-start.22 = (bf16[384,576]{1,0:T(8,128)(2,1)}, bf16[384,576]{1,0:T(8,128)(2,1)}, u32[]{:S(2)}, u32[]{:S(2)}) collective-permute-start(bf16[384,576]{1,0:T(8,128)(2,1)} %get-tuple-element.216), channel_id=1, source_target_pairs={{0,4},{4,0},{8,12},{12,8},{16,20},{20,16},{24,28},{28,24},{1,5},{5... | collective-permute-start | bytes 1327112 | tf_op jit(solution)/shard_map/ppermute | solution.py:33
  140.1 10.7 %collective-permute-start.21 = (bf16[192,576]{1,0:T(8,128)(2,1)}, bf16[192,576]{1,0:T(8,128)(2,1)}, u32[]{:S(2)}, u32[]{:S(2)}) collective-permute-start(bf16[192,576]{1,0:T(8,128)(2,1)} %get-tuple-element.215), channel_id=1, source_target_pairs={{0,8},{4,12},{8,0},{12,4},{16,24},{20,28},{24,16},{28,20},{1,9},{5... | collective-permute-start | bytes 663560 | tf_op jit(solution)/shard_map/ppermute | solution.py:33
  141.6 9.3 %collective-permute-start.20 = (bf16[256,384]{1,0:T(8,128)(2,1)}, bf16[256,384]{1,0:T(8,128)(2,1)}, u32[]{:S(2)}, u32[]{:S(2)}) collective-permute-start(bf16[256,384]{1,0:T(8,128)(2,1)} %bitcast.40), channel_id=1, source_target_pairs={{0,2},{1,3},{2,0},{3,1},{4,6},{5,7},{6,4},{7,5},{8,10},{9,11},{10,... | collective-permute-start | bytes 589832 | tf_op jit(solution)/shard_map/ppermute | solution.py:28
  157.2 8.2 %collective-permute-start.28 = (bf16[768,576]{0,1:T(8,128)(2,1)}, bf16[768,576]{0,1:T(8,128)(2,1)}, u32[]{:S(2)}, u32[]{:S(2)}) collective-permute-start(bf16[768,576]{0,1:T(8,128)(2,1)} %copy.35), channel_id=1, source_target_pairs={{0,1},{1,0},{2,3},{3,2},{4,5},{5,4},{6,7},{7,6},{8,9},{9,8},{10,11... | collective-permute-start | bytes 2654216 | tf_op jit(solution)/shard_map/ppermute | solution.py:23
  157.2 13.9 %collective-permute-start.27 = (bf16[384,576]{1,0:T(8,128)(2,1)}, bf16[384,576]{1,0:T(8,128)(2,1)}, u32[]{:S(2)}, u32[]{:S(2)}) collective-permute-start(bf16[384,576]{1,0:T(8,128)(2,1)} %copy-done.74), channel_id=1, source_target_pairs={{0,4},{4,0},{8,12},{12,8},{16,20},{20,16},{24,28},{28,24},{1,5},{5... | collective-permute-start | bytes 1327112 | tf_op jit(solution)/shard_map/ppermute | solution.py:33
  159.6 14.0 %collective-permute-start.26 = (bf16[192,576]{1,0:T(8,128)(2,1)}, bf16[192,576]{1,0:T(8,128)(2,1)S(1)}, u32[]{:S(2)}, u32[]{:S(2)}) collective-permute-start(bf16[192,576]{1,0:T(8,128)(2,1)} %get-tuple-element.230), channel_id=1, source_target_pairs={{0,8},{4,12},{8,0},{12,4},{16,24},{20,28},{24,16},{28,20},{1,9},{5... | collective-permute-start | bytes 663560 | tf_op jit(solution)/shard_map/ppermute | solution.py:33
  161.0 12.5 %collective-permute-start.24 = (bf16[256,384]{1,0:T(8,128)(2,1)}, bf16[256,384]{1,0:T(8,128)(2,1)S(1)}, u32[]{:S(2)}, u32[]{:S(2)}) collective-permute-start(bf16[256,384]{1,0:T(8,128)(2,1)} %bitcast.112), channel_id=1, source_target_pairs={{0,2},{1,3},{2,0},{3,1},{4,6},{5,7},{6,4},{7,5},{8,10},{9,11},{10,... | collective-permute-start | bytes 589832 | tf_op jit(solution)/shard_map/ppermute | solution.py:28
  164.8 8.7 %collective-permute-start.25 = (bf16[96,576]{1,0:T(8,128)(2,1)}, bf16[96,576]{1,0:T(8,128)(2,1)}, u32[]{:S(2)}, u32[]{:S(2)}) collective-permute-start(bf16[96,576]{1,0:T(8,128)(2,1)} %get-tuple-element.227), channel_id=1, source_target_pairs={{0,16},{4,20},{8,24},{12,28},{16,0},{20,4},{24,8},{28,12},{1,17},{... | collective-permute-start | bytes 331784 | tf_op jit(solution)/shard_map/ppermute | solution.py:33
  177.8 15.9 %collective-permute-start.32 = (bf16[384,576]{1,0:T(8,128)(2,1)}, bf16[384,576]{1,0:T(8,128)(2,1)}, u32[]{:S(2)}, u32[]{:S(2)}) collective-permute-start(bf16[384,576]{1,0:T(8,128)(2,1)} %get-tuple-element.249), channel_id=1, source_target_pairs={{0,4},{4,0},{8,12},{12,8},{16,20},{20,16},{24,28},{28,24},{1,5},{5... | collective-permute-start | bytes 1327112 | tf_op jit(solution)/shard_map/ppermute | solution.py:33
  179.4 24.8 %collective-permute-start.33 = (bf16[384,576]{1,0:T(8,128)(2,1)}, bf16[384,576]{1,0:T(8,128)(2,1)}, u32[]{:S(2)}, u32[]{:S(2)}) collective-permute-start(bf16[384,576]{1,0:T(8,128)(2,1)} %get-tuple-element.250), channel_id=1, source_target_pairs={{0,4},{4,0},{8,12},{12,8},{16,20},{20,16},{24,28},{28,24},{1,5},{5... | collective-permute-start | bytes 1327112 | tf_op jit(solution)/shard_map/ppermute | solution.py:33
  180.6 23.8 %all-to-all-start.2 = ((bf16[8,24,512]{2,1,0:T(8,128)(2,1)}), bf16[8,24,512]{2,1,0:T(8,128)(2,1)}, u32[]{:S(2)}, u32[]{:S(2)}) async-start(bf16[8,24,512]{2,1,0:T(8,128)(2,1)} %bitcast.44), calls=%async_computation.2 | async-start | bytes 393216 | tf_op jit(solution)/shard_map/all_to_all | solution.py:439
  185.8 13.0 %collective-permute-start.31 = (bf16[192,576]{1,0:T(8,128)(2,1)S(1)}, bf16[192,576]{1,0:T(8,128)(2,1)S(1)}, u32[]{:S(2)}, u32[]{:S(2)}) collective-permute-start(bf16[192,576]{1,0:T(8,128)(2,1)S(1)} %get-tuple-element.248), channel_id=1, source_target_pairs={{0,8},{4,12},{8,0},{12,4},{16,24},{20,28},{24,16},{28,20},{1,9},{5... | collective-permute-start | bytes 663560 | tf_op jit(solution)/shard_map/ppermute | solution.py:33
  187.8 8.3 %collective-permute-start.30 = (bf16[96,576]{1,0:T(8,128)(2,1)S(1)}, bf16[96,576]{1,0:T(8,128)(2,1)S(1)}, u32[]{:S(2)}, u32[]{:S(2)}) collective-permute-start(bf16[96,576]{1,0:T(8,128)(2,1)S(1)} %get-tuple-element.245), channel_id=1, source_target_pairs={{0,16},{4,20},{8,24},{12,28},{16,0},{20,4},{24,8},{28,12},{1,17},{... | collective-permute-start | bytes 331784 | tf_op jit(solution)/shard_map/ppermute | solution.py:33
  206.2 38.5 %all-to-all-start.3 = ((f32[8,24,512]{2,1,0:T(8,128)}), f32[8,24,512]{2,1,0:T(8,128)}, u32[]{:S(2)}, u32[]{:S(2)}) async-start(f32[8,24,512]{2,1,0:T(8,128)} %broadcast_in_dim.5), calls=%async_computation.3 | async-start | bytes 786432 | tf_op jit(solution)/shard_map/all_to_all | solution.py:449
  211.3 27.5 %collective-permute-start.38 = (bf16[96,576]{1,0:T(8,128)(2,1)S(1)}, bf16[96,576]{1,0:T(8,128)(2,1)S(1)}, u32[]{:S(2)}, u32[]{:S(2)}) collective-permute-start(bf16[96,576]{1,0:T(8,128)(2,1)S(1)} %get-tuple-element.270), channel_id=1, source_target_pairs={{0,16},{4,20},{8,24},{12,28},{16,0},{20,4},{24,8},{28,12},{1,17},{... | collective-permute-start | bytes 331784 | tf_op jit(solution)/shard_map/ppermute | solution.py:33
  215.3 13.1 %collective-permute-start.35 = (bf16[192,576]{1,0:T(8,128)(2,1)S(1)}, bf16[192,576]{1,0:T(8,128)(2,1)S(1)}, u32[]{:S(2)}, u32[]{:S(2)}) collective-permute-start(bf16[192,576]{1,0:T(8,128)(2,1)S(1)} %get-tuple-element.261), channel_id=1, source_target_pairs={{0,8},{4,12},{8,0},{12,4},{16,24},{20,28},{24,16},{28,20},{1,9},{5... | collective-permute-start | bytes 663560 | tf_op jit(solution)/shard_map/ppermute | solution.py:33
  217.9 16.9 %collective-permute-start.34 = (bf16[192,576]{1,0:T(8,128)(2,1)S(1)}, bf16[192,576]{1,0:T(8,128)(2,1)S(1)}, u32[]{:S(2)}, u32[]{:S(2)}) collective-permute-start(bf16[192,576]{1,0:T(8,128)(2,1)S(1)} %get-tuple-element.256), channel_id=1, source_target_pairs={{0,8},{4,12},{8,0},{12,4},{16,24},{20,28},{24,16},{28,20},{1,9},{5... | collective-permute-start | bytes 663560 | tf_op jit(solution)/shard_map/ppermute | solution.py:33
  228.4 10.3 %collective-permute-start.37 = (bf16[96,576]{1,0:T(8,128)(2,1)S(1)}, bf16[96,576]{1,0:T(8,128)(2,1)S(1)}, u32[]{:S(2)}, u32[]{:S(2)}) collective-permute-start(bf16[96,576]{1,0:T(8,128)(2,1)S(1)} %get-tuple-element.269), channel_id=1, source_target_pairs={{0,16},{4,20},{8,24},{12,28},{16,0},{20,4},{24,8},{28,12},{1,17},{... | collective-permute-start | bytes 331784 | tf_op jit(solution)/shard_map/ppermute | solution.py:33
  234.9 7.1 %collective-permute-start.36 = (bf16[96,576]{1,0:T(8,128)(2,1)S(1)}, bf16[96,576]{1,0:T(8,128)(2,1)S(1)}, u32[]{:S(2)}, u32[]{:S(2)}) collective-permute-start(bf16[96,576]{1,0:T(8,128)(2,1)S(1)} %get-tuple-element.268), channel_id=1, source_target_pairs={{0,16},{4,20},{8,24},{12,28},{16,0},{20,4},{24,8},{28,12},{1,17},{... | collective-permute-start | bytes 331784 | tf_op jit(solution)/shard_map/ppermute | solution.py:33
  (103 other events, 502.3 us)
where the time goes:
time: 248 us; the launch traced here: 246 us
  waiting for transfers between devices  66.9 us (27%)
  starting transfers between devices  50.3 us (20%)
  local copies, waits for them, and re-layouts  46.2 us (19%)
  Pallas kernels  33.8 us (14%)
  other arithmetic  27.8 us (11%)
  matrix products  19.5 us (8%)
    ppermute x18, waiting for transfers between devices, seq_swap(): return lax.ppermute(value, 'seq', [(i, i ^ bit) for i in range(count)])  41.9 us
    pallas_call x26, Pallas kernels, run(): pl.pallas_call(kernel, out_shape=[jax.ShapeDtypeStruct(shape, kind) for s...  31.2 us
    unnamed x185, local copies, waits for them, and re-layouts  29.7 us
    ppermute x18, starting transfers between devices, seq_swap(): return lax.ppermute(value, 'seq', [(i, i ^ bit) for i in range(count)])  22 us
    ppermute x10, waiting for transfers between devices, chip_shift(): lax.ppermute(value, 'ch', [(i, (i + CORES * by) % count) for i in range(c...  14.9 us
    ppermute x10, starting transfers between devices, chip_shift(): lax.ppermute(value, 'ch', [(i, (i + CORES * by) % count) for i in range(c...  10.2 us
    ppermute x5, local copies, waits for them, and re-layouts, core_swap(): return lax.ppermute(value, 'ch', [(i, i ^ 1) for i in range(count)])  8.66 us
    select_n x7, other arithmetic, by_strand(): jnp.where(strand == 0, own, sibling)  7.23 us
  transfers between devices with their start and end apart: 43, of which 20 were waited for; matrix products, arithmetic and copies ran while one was open for 18% of the time, Pallas kernels for 8%

commit v1 on v0

v1 whole, which is shorter than its diff:
```python
import jax
import jax.numpy as jnp
from jax import lax
from jax.experimental import pallas as pl
from jax.experimental.pallas import tpu as pltpu
from jax.sharding import PartitionSpec as P

LAYERS = 5
WIN = 16
CORES = 2
VMEM = 12 << 20

bf16 = jnp.bfloat16
f32 = jnp.float32


def dilations(shard_rows):
    return (shard_rows // 8, shard_rows // 2, shard_rows, 2 * shard_rows, 4 * shard_rows)


def core_swap(value):
    count = lax.axis_size("ch")
    return lax.ppermute(value, "ch", [(i, i ^ 1) for i in range(count)])


def chip_shift(value, by):
    count = lax.axis_size("ch")
    return lax.ppermute(value, "ch", [(i, (i + CORES * by) % count) for i in range(count)])


def seq_swap(value, bit):
    count = lax.axis_size("seq")
    return lax.ppermute(value, "seq", [(i, i ^ bit) for i in range(count)])


def choose(index, options):
    picked = options[0]
    for place, option in enumerate(options[1:], 1):
        picked = jnp.where(index == place, option, picked)
    return picked


def rolled(field, by):
    if by == 0:
        return field
    blank = jnp.zeros((abs(by),) + field.shape[1:], field.dtype)
    if by > 0:
        return jnp.concatenate([field[by:], blank], axis=0)
    return jnp.concatenate([blank, field[:by]], axis=0)


def tied(*values):
    return lax.optimization_barrier(values)


def by_strand(strand, own, sibling):
    return [jnp.where(strand == 0, own, sibling), jnp.where(strand == 0, sibling, own)]


def pieces(value):
    high = value.astype(bf16)
    rest = value - high.astype(f32)
    middle = rest.astype(bf16)
    return high, middle, (rest - middle.astype(f32)).astype(bf16)


def run(body, outs, *values, inside=True):
    if not inside:
        return body(jnp.roll, *values)

    def kernel(*refs):
        results = body(pltpu.roll, *[ref[...] for ref in refs[: len(values)]])
        for ref, result in zip(refs[len(values) :], results):
            ref[...] = result

    return pl.pallas_call(
        kernel,
        out_shape=[jax.ShapeDtypeStruct(shape, kind) for shape, kind in outs],
        compiler_params=pltpu.CompilerParams(vmem_limit_bytes=VMEM),
        cost_estimate=pl.CostEstimate(flops=1, bytes_accessed=1, transcendentals=0),
    )(*values)


def moved(roll, field, by):
    if by == 0:
        return field
    rows = field.shape[0]
    row = lax.broadcasted_iota(jnp.int32, field.shape, 0)
    there = (row + by >= 0) & (row + by < rows)
    return jnp.where(there, roll(field, (-by) % rows, 0), 0.0)


def slope_of_gelu(value):
    scale = 0.7978845608028654
    bend = jnp.tanh(scale * (value + 0.044715 * value * value * value))
    return 0.5 * (1.0 + bend) + 0.5 * value * (1.0 - bend * bend) * scale * (
        1.0 + 3 * 0.044715 * value * value
    )


def back_body(reach, chips, quarter, first):
    def body(roll, chip, strand, grad, *rest):
        if first:
            (taps,) = rest
        else:
            mine, received, stream, taps = rest
            through = mine
            for part in range(chips - 1):
                through = through + received[part].astype(f32)
            grad = grad + through * slope_of_gelu(stream)
        upstream = grad.astype(bf16)
        wide = upstream.astype(f32)
        fields = [moved(roll, wide, (1 - tap) * reach).astype(bf16) for tap in range(3)]
        back = jnp.dot(
            jnp.concatenate(fields, axis=1),
            taps.reshape(-1, taps.shape[-1]),
            preferred_element_type=f32,
        )
        width = grad.shape[1]
        parts = [back[:, i * width : (i + 1) * width] for i in range(chips)]
        index = chip[0, 0]
        sends = [
            choose((index + by) % chips, parts).astype(bf16)[None] for by in range(1, chips)
        ]
        sends = sends[0] if chips == 2 else jnp.concatenate(sends)
        source = lax.broadcasted_iota(jnp.int32, (width, quarter), 0)
        target = lax.broadcasted_iota(jnp.int32, (width, quarter), 1)
        theirs = (source == target + (1 - strand[0, 0]) * quarter).astype(f32).astype(bf16)
        theirs = jnp.dot(upstream, theirs, preferred_element_type=f32).astype(bf16)
        return grad, upstream, choose(index, parts), sends, theirs

    return body


def score_body(quarter, everyone):
    def body(roll, strand, stream, member, columns):
        pooled = sum(
            jnp.dot(term, member, preferred_element_type=f32) for term in pieces(stream.T)
        ) / WIN
        partial = 0.5 * jnp.sum(pooled * columns.astype(f32), axis=0, keepdims=True)
        parts = [pooled[:quarter], pooled[quarter:]]
        return (
            jnp.broadcast_to(partial, (everyone, partial.shape[1])),
            choose(strand[0, 0], parts),
            choose(1 - strand[0, 0], parts),
        )

    return body


def loss_body(reach, chips, quarter):
    back = back_body(reach, chips, quarter, True)

    def body(roll, chip, strand, scores, targets, counts, member, columns, taps):
        score = jnp.sum(scores, axis=0, keepdims=True)
        slope = (jnp.exp(score) - targets) / counts
        grad = sum(
            lax.dot_general(
                term, columns, (((1,), (1,)), ((), ())), preferred_element_type=f32
            )
            for term in pieces(0.5 / WIN * slope * member.astype(f32))
        )
        return (score, slope, *back(roll, chip, strand, grad, taps))

    return body


def genome_body(steps, seqs, own_classes):
    def body(roll, genome):
        rows = genome.shape[0]
        target = lax.broadcasted_iota(jnp.int32, (rows, rows), 0)
        source = lax.broadcasted_iota(jnp.int32, (rows, rows), 1)
        owner, local = target // (steps * own_classes), target % (steps * own_classes)
        step, kind = local // own_classes, local % own_classes
        wanted = step * (seqs * own_classes) + owner * own_classes + kind
        order = (source == wanted).astype(f32).astype(bf16)
        bases = genome.astype(f32).astype(bf16)
        return (jnp.dot(order, bases, preferred_element_type=f32).astype(bf16),)

    return body


def stem(strand, chip, bases, quarters, chips, own_classes):
    rows, pool = bases.shape
    quarter = quarters[0].shape[0]
    width = chips * CORES * quarter

    def kernel(strand_ref, chip_ref, bases_ref, *refs):
        letters_ref, active_ref, stream_ref, weight_ref = refs[len(quarters) :]
        strand, chip = strand_ref[0, 0], chip_ref[0, 0]
        for by in range(chips):
            for core in range(CORES):
                at = (chip + chips - by) % chips * CORES + (strand + core) % CORES
                weight_ref[pl.ds(at * quarter, quarter), :] = refs[by * CORES + core][...]
        target = lax.broadcasted_iota(jnp.int32, (rows, rows), 0)
        source = lax.broadcasted_iota(jnp.int32, (rows, rows), 1)
        step = target // own_classes
        step = jnp.where(strand == 0, step, rows // own_classes - 1 - step)
        order = (source == step * own_classes + target % own_classes).astype(f32).astype(bf16)
        position = lax.broadcasted_iota(jnp.int32, (pool, 4 * pool), 0)
        letter = lax.broadcasted_iota(jnp.int32, (pool, 4 * pool), 1)
        place = jnp.where(strand == 0, letter // 4, pool - 1 - letter // 4)
        spread = (position == place).astype(f32).astype(bf16)
        ordered = jnp.dot(order, bases_ref[...], preferred_element_type=f32).astype(bf16)
        wide = jnp.dot(ordered, spread, preferred_element_type=f32)
        letter = lax.broadcasted_iota(jnp.int32, (rows, 4 * pool), 1) % 4
        base = jnp.where(strand == 0, letter, 3 - letter).astype(f32)
        letters = (wide == base).astype(f32).astype(bf16)
        letters_ref[...] = letters
        whole = lax.dot_general(
            letters, weight_ref[...], (((1,), (1,)), ((), ())), preferred_element_type=f32
        )
        active_ref[...] = jax.nn.gelu(whole).astype(bf16)
        each = width // chips
        stream_ref[...] = choose(chip, [whole[:, i * each : (i + 1) * each] for i in range(chips)])

    return pl.pallas_call(
        kernel,
        out_shape=[
            jax.ShapeDtypeStruct((rows, 4 * pool), bf16),
            jax.ShapeDtypeStruct((rows, width), bf16),
            jax.ShapeDtypeStruct((rows, width // chips), f32),
        ],
        in_specs=[pl.BlockSpec(memory_space=pltpu.SMEM)] * 2
        + [pl.BlockSpec(memory_space=pltpu.VMEM)] * (1 + len(quarters)),
        scratch_shapes=[pltpu.VMEM((width, 4 * pool), bf16)],
        compiler_params=pltpu.CompilerParams(vmem_limit_bytes=VMEM),
        cost_estimate=pl.CostEstimate(flops=1, bytes_accessed=1, transcendentals=0),
    )(strand, chip, bases, *quarters)


def join_filters(strand, own, sibling, layer):
    taps, quarter, channels = own.shape[1:]

    def kernel(strand_ref, own_ref, sibling_ref, out_ref, sems):
        copies = [
            pltpu.make_async_copy(
                ref.at[layer], out_ref.at[:, pl.ds(at * quarter, quarter), :], sems.at[core]
            )
            for core, (ref, at) in enumerate(
                [(own_ref, strand_ref[0, 0]), (sibling_ref, 1 - strand_ref[0, 0])]
            )
        ]
        for copy in copies:
            copy.start()
        for copy in copies:
            copy.wait()

    return pl.pallas_call(
        kernel,
        out_shape=jax.ShapeDtypeStruct((taps, CORES * quarter, channels), bf16),
        in_specs=[
            pl.BlockSpec(memory_space=pltpu.SMEM),
            pl.BlockSpec(memory_space=pl.ANY),
            pl.BlockSpec(memory_space=pl.ANY),
        ],
        out_specs=pl.BlockSpec(memory_space=pl.ANY),
        scratch_shapes=[pltpu.SemaphoreType.DMA((CORES,))],
        compiler_params=pltpu.CompilerParams(vmem_limit_bytes=VMEM),
        cost_estimate=pl.CostEstimate(flops=1, bytes_accessed=1, transcendentals=0),
    )(strand, own, sibling)


def placed(order, active):
    def body(roll, order, active):
        return (
            lax.dot_general(
                order, active, (((1,), (1,)), ((), ())), preferred_element_type=f32
            ).astype(bf16),
        )

    return run(body, [((order.shape[0], active.shape[0]), bf16)], order, active)[0]


def tap_rows(roll, upstream, offset, reach, quarter):
    width = 3 * quarter
    shape = (upstream.shape[1], 2 * width)
    source = lax.broadcasted_iota(jnp.int32, shape, 0)
    target = lax.broadcasted_iota(jnp.int32, shape, 1)
    target = jnp.where(target >= width, target - width, target)
    tap = (target >= quarter).astype(jnp.int32) + (target >= 2 * quarter).astype(jnp.int32)
    spread = (source == offset + target - tap * quarter).astype(f32).astype(bf16)
    wide = jnp.dot(upstream, spread, preferred_element_type=f32)
    lane = lax.broadcasted_iota(jnp.int32, wide.shape, 1)
    late = lane >= width
    lane = jnp.where(late, lane - width, lane)
    low, high = moved(roll, wide, reach), moved(roll, wide, -reach)
    taps = jnp.where(lane < quarter, low, jnp.where(lane < 2 * quarter, wide, high))
    return [jnp.where(late, 0.0, taps).astype(bf16), jnp.where(late, taps, 0.0).astype(bf16)]


def filter_product(strand, active, upstream, active_sibling, upstream_sibling, reach, quarter):
    half = active.shape[0] // 2
    rows = half // 2

    def body(roll, strand, active, upstream, active_sibling, upstream_sibling):
        fields = [active[:half], active[half:], active_sibling[:half], active_sibling[half:]]
        taps = tap_rows(roll, upstream, strand[0, 0] * quarter, reach, quarter)
        taps = taps + tap_rows(roll, upstream_sibling, 0, reach, quarter)
        total = jnp.dot(
            jnp.concatenate(fields, axis=1), jnp.concatenate(taps), preferred_element_type=f32
        )
        return total[:rows], total[rows:].astype(bf16)

    shape = (rows, 6 * quarter)
    return run(
        body,
        [(shape, f32), (shape, bf16)],
        strand,
        active,
        upstream,
        active_sibling,
        upstream_sibling,
    )


def last_body(chips, quarter):
    def body(roll, strand, grad, mine, received, stream, letters):
        through = mine
        for part in range(chips - 1):
            through = through + received[part].astype(f32)
        grad = grad + through * slope_of_gelu(stream)
        stem = jnp.dot(grad.T.astype(bf16), letters, preferred_element_type=f32)
        parts = [stem[:quarter], stem[quarter:]]
        return choose(strand[0, 0], parts), choose(1 - strand[0, 0], parts).astype(bf16)

    return body


class BlockSum:
    def __init__(self, kept, sent, slot):
        self.kept, self.sent, self.slot = kept, sent, slot
        self.bit = 1
        self.received = None

    def start(self):
        if self.sent is not None and self.received is None:
            self.received = seq_swap(self.sent, self.bit)

    def last(self):
        return 2 * self.bit >= lax.axis_size("seq")

    def join(self):
        rows, width = self.kept.shape
        axis = 1 if 4 * self.bit >= lax.axis_size("seq") else 0
        half = (rows, width // 2) if axis else (rows // 2, width)

        def body(roll, kept, received):
            total = kept + received.astype(f32)
            if axis:
                return total[:, : half[1]], total[:, half[1] :].astype(bf16)
            return total[: half[0]], total[half[0] :].astype(bf16)

        self.kept, self.sent = run(body, [(half, f32), (half, bf16)], self.kept, self.received)
        self.bit *= 2
        self.received = None


def settle(sums, value):
    value, received = tied(value, [s.received for s in sums])
    for s, got in zip(sums, received):
        s.received = got
        s.join()
        s.start()
    return value


def assemble(sums, quarter):
    block = sums[0].kept.shape[0]
    taps = sums[0].kept.shape[1] // quarter
    count = len(sums)

    def kernel(*refs):
        out = refs[-1]
        for layer in range(count):
            total = refs[layer][...] + refs[count + layer][...].astype(f32)
            out[layer] = total.T.reshape(taps, quarter, block)

    return pl.pallas_call(
        kernel,
        out_shape=jax.ShapeDtypeStruct((count, taps, quarter, block), f32),
        compiler_params=pltpu.CompilerParams(vmem_limit_bytes=VMEM),
    )(*[s.kept for s in sums], *[s.received for s in sums])


def shards(
    genome, stem_weight, dilated_filter_weight, head_weight, window_start, window_track, targets
):
    shard_rows, pool = genome.shape
    seqs = lax.axis_size("seq")
    chips = lax.axis_size("ch") // CORES
    seq = lax.axis_index("seq")
    strand = lax.axis_index("ch") % CORES
    chip = lax.axis_index("ch") // CORES
    spans = dilations(shard_rows)
    classes = spans[0]
    own_classes = classes // seqs
    steps = shard_rows // classes
    reach = tuple(span // classes * own_classes for span in spans)
    quarter = stem_weight.shape[0]
    channels = dilated_filter_weight.shape[3]
    block = channels // seqs
    tracks = head_weight.shape[1]

    chip_word = jnp.reshape(chip, (1, 1))
    strand_word = jnp.reshape(strand, (1, 1))

    stem_own = [stem_weight] + [chip_shift(stem_weight, by) for by in range(1, chips)]
    quarters = [part for own in stem_own for part in (own, core_swap(own))]

    (blocks,) = run(
        genome_body(steps, seqs, own_classes), [((shard_rows, pool), bf16)], genome
    )
    blocks = lax.all_to_all(
        blocks.reshape(seqs, steps * own_classes, pool), "seq", 0, 0, tiled=True
    )

    sibling_filter = core_swap(dilated_filter_weight)

    own_filter = dilated_filter_weight

    def filter_of(layer):
        return join_filters(strand_word, own_filter, sibling_filter, layer)

    letters, active, stream = stem(
        strand_word, chip_word, blocks.reshape(shard_rows, pool), quarters, chips, own_classes
    )
    row = jnp.arange(shard_rows, dtype=jnp.int32)
    step_of = row // own_classes
    step_of = jnp.where(strand == 0, step_of, shard_rows // own_classes - 1 - step_of)
    class_of = row % own_classes
    position = step_of * classes + seq * own_classes + class_of

    member = (
        (position[:, None] >= window_start[None, :])
        & (position[:, None] < window_start[None, :] + WIN)
    ).astype(bf16)
    counts = jnp.sum((window_track[:, None] == window_track[None, :]).astype(f32), axis=1)
    at_track = (
        jnp.arange(tracks, dtype=jnp.int32)[None, :] == window_track[:, None]
    ).astype(bf16)

    bits = seqs.bit_length() - 1
    slot = jnp.arange(channels, dtype=jnp.int32) // block
    away = (slot >> (bits - 1)) << (bits - 1)
    for b in range(bits - 1):
        away = away + (((slot >> (bits - 2 - b)) & 1) << b)
    wanted = (seq ^ away) * block + jnp.arange(channels, dtype=jnp.int32) % block
    by_distance = (
        wanted[:, None] == jnp.arange(channels, dtype=jnp.int32)[None, :]
    ).astype(bf16)

    filters = [filter_of(0)]
    streams = []
    actives = []
    sibling_actives = []
    for layer in range(LAYERS):
        streams.append(stream)
        for tap in range(3):
            stream = stream + lax.dot_general(
                rolled(active, (tap - 1) * reach[layer]),
                filters[layer][tap],
                (((1,), (1,)), ((), ())),
                preferred_element_type=f32,
            )
        if layer < LAYERS - 1:
            own = jax.nn.gelu(stream).astype(bf16)
            own, own_filter, sibling_filter, by_distance, at_track = tied(
                own, own_filter, sibling_filter, by_distance, at_track
            )
            parts = [chip_shift(own, by) for by in range(1, chips)]
            beside = [
                filter_of(layer + 1),
                placed(by_distance, active),
            ]
            if layer == 1:
                columns = lax.dot_general(
                    head_weight, at_track, (((1,), (1,)), ((), ())), preferred_element_type=f32
                ).astype(bf16)
                beside.append(columns)
            if layer == 2:
                beside.append(jnp.concatenate(by_strand(strand, columns, core_swap(columns))))
            if layer > 0:
                beside.append(core_swap(actives[-1]))
            parts, beside = tied(parts, beside)
            filters.append(beside[0])
            actives.append(beside[1])
            if layer > 0:
                sibling_actives.append(beside[-1])
            if layer == 1:
                columns = beside[2]
            if layer == 2:
                half_columns = beside[2]
            parts = [own] + list(parts)
            active = jnp.concatenate(
                [choose((chip - p) % chips, parts) for p in range(chips)], axis=1
            )

    windows = window_start.shape[0]
    everyone = seqs * chips * CORES
    partial_score, pooled_own, pooled_sent = run(
        score_body(quarter, everyone),
        [((everyone, windows), f32), ((quarter, windows), f32), ((quarter, windows), f32)],
        strand_word,
        stream,
        member,
        half_columns,
    )
    scores = lax.all_to_all(partial_score[:, None], ("seq", "ch"), 0, 0, tiled=True)
    pooled_own = pooled_own + core_swap(pooled_sent)
    pooled_bit = 1
    if pooled_bit < seqs:
        pooled_own = pooled_own + seq_swap(pooled_own, pooled_bit)
        pooled_bit *= 2
    last_active = placed(by_distance, active)
    sibling_active = core_swap(actives[-1])
    scores, pooled_own, last_active, sibling_active = tied(
        scores, pooled_own, last_active, sibling_active
    )
    actives.append(last_active)
    sibling_actives.append(sibling_active)
    sibling_actives.append(core_swap(last_active))

    sums = []
    aligned = (channels // chips) % 128 == 0
    shape = (shard_rows, channels // chips)
    back_outs = [
        (shape, f32),
        (shape, bf16),
        (shape, f32),
        ((chips - 1,) + shape, bf16),
        ((shard_rows, quarter), bf16),
    ]
    state = ()
    for layer in reversed(range(LAYERS)):
        first = layer == LAYERS - 1
        if first:
            window_score, loss_slope, grad, upstream, mine, sends, theirs = run(
                loss_body(reach[layer], chips, quarter),
                [((1, windows), f32)] * 2 + back_outs,
                chip_word,
                strand_word,
                scores[:, 0],
                targets[None],
                counts[None],
                member,
                half_columns,
                filters[layer],
                inside=aligned,
            )
        else:
            grad, upstream, mine, sends, theirs = run(
                back_body(reach[layer], chips, quarter, False),
                back_outs,
                chip_word,
                strand_word,
                *state,
                filters[layer],
                inside=aligned,
            )
        received = jnp.stack([chip_shift(sends[by - 1], by) for by in range(1, chips)])
        upstream = settle(
            [s for s in sums if not s.last() and s.slot < LAYERS - 2 - layer], upstream
        )
        if pooled_bit < seqs:
            pooled_received = seq_swap(pooled_own, pooled_bit)
            pooled_bit *= 2
        else:
            pooled_received = jnp.zeros_like(pooled_own)
        keep, send = filter_product(
            strand_word,
            actives[layer],
            upstream,
            sibling_actives[layer],
            core_swap(theirs),
            reach[layer],
            quarter,
        )
        received, pooled_received, keep, send = tied(received, pooled_received, keep, send)
        pooled_own = pooled_own + pooled_received
        sums.append(BlockSum(keep, send, LAYERS - 1 - layer))
        sums[-1].start()
        state = (grad, mine, received, streams[layer])

    stem_shape = (quarter, letters.shape[1])
    stem_keep, stem_away = run(
        last_body(chips, quarter),
        [(stem_shape, f32), (stem_shape, bf16)],
        strand_word,
        *state,
        letters,
        inside=aligned,
    )
    stem_own = stem_keep + core_swap(stem_away).astype(f32)
    stem_send = stem_own.astype(bf16).reshape(seqs, quarter // seqs, -1)
    stem_send = settle([s for s in sums if not s.last() and s.slot < LAYERS - 1], stem_send)
    stem_blocks = lax.all_to_all(stem_send, "seq", 0, 0, tiled=True)
    stem_blocks = settle([s for s in sums if not s.last() and s.slot < LAYERS - 1], stem_blocks)
    stem_block = jnp.sum(stem_blocks.astype(f32), axis=0)
    stem_grad = lax.all_to_all(
        jnp.broadcast_to(stem_block, (seqs,) + stem_block.shape), "seq", 0, 0, tiled=True
    ).reshape(quarter, -1)
    while pooled_bit < seqs:
        pooled_own = pooled_own + seq_swap(pooled_own, pooled_bit)
        pooled_bit *= 2
    head_grad = lax.dot_general(
        jnp.concatenate(pieces(0.5 * loss_slope * pooled_own), axis=1),
        jnp.concatenate([at_track] * 3),
        (((1,), (0,)), ((), ())),
        preferred_element_type=f32,
    )
    while any(not s.last() for s in sums):
        for s in sums:
            if not s.last():
                s.join()
                s.start()
    conv_grad = assemble(sums[::-1], quarter)
    return (window_score[0], conv_grad, stem_grad, head_grad)


def solution(mesh):
    return jax.shard_map(
        shards,
        mesh=mesh,
        in_specs=(
            P("seq", None),
            P("ch", None),
            P(None, None, "ch", None),
            P("ch", None),
            P(),
            P(),
            P(),
        ),
        out_specs=(P(), P(None, None, "ch", "seq"), P("ch", None), P("ch", None)),
        check_vma=False,
    )
```

time: 248 us -> 185 us (0.75)
  local copies, waits for them, and re-layouts: 46.2 us -> 21.9 us
  other arithmetic: 27.8 us -> 8.09 us
  waiting for transfers between devices: 66.9 us -> 54 us
  matrix products: 19.5 us -> 9.57 us
  starting transfers between devices: 50.3 us -> 54.2 us
    ppermute x18, waiting for transfers between devices: 41.9 us -> 30.5 us  [seq_swap(): return lax.ppermute(value, 'seq', [(i, i ^ bit) for i in range(count)])]
    dot_general x10 -> x1, matrix products: 12.7 us -> 2.78 us  [shards(): lax.dot_general(jnp.concatenate(pieces(0.5 * loss_slope * pooled_own), ax...]
    unnamed x185 -> x141, local copies, waits for them, and re-layouts: 29.7 us -> 21 us
    ppermute x5 -> x0, local copies, waits for them, and re-layouts: 8.66 us -> none  [core_swap(): return lax.ppermute(value, 'ch', [(i, i ^ 1) for i in range(count)])]
    pallas_call x0 -> x6, Pallas kernels: none -> 8.46 us  [the longest x5 6.6 us: join_filters(): pl.pallas_call(kernel, out_shape=jax.ShapeDtypeStruct((taps, CORES * quar...]
    select_n x7 -> x1, other arithmetic: 7.23 us -> 0.01 us  [by_strand(): jnp.where(strand == 0, own, sibling)]
    pallas_call x26 -> x28, Pallas kernels: 31.2 us -> 24.3 us  [run(): pl.pallas_call(kernel, out_shape=[jax.ShapeDtypeStruct(shape, kind) for s...]
    pallas_call x5 -> x0, local copies, waits for them, and re-layouts: 5.69 us -> none  [run(): pl.pallas_call(kernel, out_shape=[jax.ShapeDtypeStruct(shape, kind) for s...]
  transfers between devices with their start and end apart: 43 -> 48, of which waited for: 20 -> 23; matrix products, arithmetic and copies ran while one was open for 18% -> 8% of each run, Pallas kernels for 8% -> 18%
where the time goes in v1:
time: 185 us; the launch traced here: 184 us
  starting transfers between devices  54.2 us (29%)
  waiting for transfers between devices  54 us (29%)
  Pallas kernels  34.3 us (19%)
  local copies, waits for them, and re-layouts  21.9 us (12%)
  matrix products  9.57 us (5%)
  other arithmetic  8.09 us (4%)
    ppermute x18, waiting for transfers between devices, seq_swap(): return lax.ppermute(value, 'seq', [(i, i ^ bit) for i in range(count)])  30.5 us
    pallas_call x28, Pallas kernels, run(): pl.pallas_call(kernel, out_shape=[jax.ShapeDtypeStruct(shape, kind) for s...  24.3 us
    ppermute x18, starting transfers between devices, seq_swap(): return lax.ppermute(value, 'seq', [(i, i ^ bit) for i in range(count)])  23.3 us
    unnamed x141, local copies, waits for them, and re-layouts  21 us
    ppermute x10, waiting for transfers between devices, chip_shift(): lax.ppermute(value, 'ch', [(i, (i + CORES * by) % count) for i in range(c...  16.3 us
    ppermute x10, starting transfers between devices, chip_shift(): lax.ppermute(value, 'ch', [(i, (i + CORES * by) % count) for i in range(c...  9.94 us
    pallas_call x5, Pallas kernels, join_filters(): pl.pallas_call(kernel, out_shape=jax.ShapeDtypeStruct((taps, CORES * quar...  6.6 us
    dot_general x15, matrix products, shards(): lax.dot_general(rolled(active, (tap - 1) * reach[layer]), filters[layer][...  6.1 us
  transfers between devices with their start and end apart: 48, of which 23 were waited for; matrix products, arithmetic and copies ran while one was open for 8% of the time, Pallas kernels for 18%

profile of v1, /device:TPU:0, one launch (start us, length us, event | category | flops | bytes accessed | tf_op | source)
XLA Modules:
  0.0 183.8 jit_solution(8609386658281428211)
XLA Ops:
  1.2 2.6 %collective-permute-start.1 = (bf16[192,512]{1,0:T(8,128)(2,1)}, bf16[192,512]{1,0:T(8,128)(2,1)}, u32[]{:S(2)}, u32[]{:S(2)}) collective-permute-start(bf16[192,512]{1,0:T(8,128)(2,1)} %refs_0_.3), channel_id=1, source_target_pairs={{0,2},{1,3},{2,0},{3,1},{4,6},{5,7},{6,4},{7,5},{8,10},{9,11},{10,... | collective-permute-start | bytes 589832 | tf_op jit(solution)/shard_map/ppermute | solution.py:28
  5.6 5.8 %all-to-all-start = ((bf16[8,32,128]{2,1,0:T(8,128)(2,1)}), bf16[8,32,128]{2,1,0:T(8,128)(2,1)S(1)}, u32[]{:S(2)}, u32[]{:S(2)}) async-start(bf16[8,32,128]{2,1,0:T(8,128)(2,1)} %bitcast.2), calls=%async_computation | async-start | bytes 131072 | tf_op jit(solution)/shard_map/all_to_all | solution.py:414
  11.5 2.0 %fusion.6 = bf16[128,5313]{1,0:T(8,128)(2,1)} fusion(s32[128]{0:T(128)} %param.12), kind=kLoop, calls=%fused_computation.7 | loop fusion | flops 1360128 | bytes 1360640 | tf_op jit(solution)/shard_map/convert_element_type | solution.py:441
  14.0 4.4 %all-to-all-done = bf16[8,32,128]{2,1,0:T(8,128)(2,1)S(1)} async-done(((bf16[8,32,128]{2,1,0:T(8,128)(2,1)}), bf16[8,32,128]{2,1,0:T(8,128)(2,1)S(1)}, u32[]{:S(2)}, u32[]{:S(2)}) %all-to-all-start) | async-done | bytes 65568 | tf_op jit(solution)/shard_map/all_to_all | solution.py:414
  18.4 1.9 %shard_map.103 = (bf16[256,512]{1,0:T(8,128)(2,1)S(1)}, bf16[256,768]{1,0:T(8,128)(2,1)S(1)}, f32[256,384]{1,0:T(8,128)S(1)}) custom-call(s32[1,1]{1,0:T(1,128)} %bitcast.1.strand_ref.refs_0_.refs_1_, s32[1,1]{1,0:T(1,128)} %bitcast.chip_ref.refs_0_, bf16[256,128]{1,0:T(8,128)(2,1)S(1)} %bitcast.83, bf16[192,512]{1,0:T(8,128)(2,1)S(1)} %copy-done.54, ...), custom_call_target="tpu_custom_call" | custom-call | flops 1 | bytes 1 | tf_op jit(solution)/shard_map/pallas_call | solution.py:217
  21.1 2.3 %copy-done.2 = bf16[5,3,192,768]{3,2,1,0:T(8,128)(2,1)S(1)} copy-done((bf16[5,3,192,768]{3,2,1,0:T(8,128)(2,1)S(1)}, bf16[5,3,192,768]{3,2,1,0:T(8,128)(2,1)}, u32[]{:S(2)}) %copy-start.2) | copy-done | bytes 4423704
  29.2 2.6 %collective-permute-done.4 = bf16[256,384]{1,0:T(8,128)(2,1)S(1)} collective-permute-done((bf16[256,384]{1,0:T(8,128)(2,1)S(1)}, bf16[256,384]{1,0:T(8,128)(2,1)S(1)}, u32[]{:S(2)}, u32[]{:S(2)}) %collective-permute-start.4) | collective-permute-done | bytes 196640 | tf_op jit(solution)/shard_map/ppermute | solution.py:28
  36.8 2.1 %collective-permute-done.5 = bf16[256,384]{1,0:T(8,128)(2,1)S(1)} collective-permute-done((bf16[256,384]{1,0:T(8,128)(2,1)S(1)}, bf16[256,384]{1,0:T(8,128)(2,1)S(1)}, u32[]{:S(2)}, u32[]{:S(2)}) %collective-permute-start.5) | collective-permute-done | bytes 196640 | tf_op jit(solution)/shard_map/ppermute | solution.py:28
  43.4 4.6 %collective-permute-done.7 = bf16[256,384]{1,0:T(8,128)(2,1)S(1)} collective-permute-done((bf16[256,384]{1,0:T(8,128)(2,1)S(1)}, bf16[256,384]{1,0:T(8,128)(2,1)S(1)}, u32[]{:S(2)}, u32[]{:S(2)}) %collective-permute-start.7) | collective-permute-done | bytes 196640 | tf_op jit(solution)/shard_map/ppermute | solution.py:28
  52.8 4.1 %collective-permute-done.10 = bf16[256,384]{1,0:T(8,128)(2,1)S(1)} collective-permute-done((bf16[256,384]{1,0:T(8,128)(2,1)S(1)}, bf16[256,384]{1,0:T(8,128)(2,1)S(1)}, u32[]{:S(2)}, u32[]{:S(2)}) %collective-permute-start.10) | collective-permute-done | bytes 196640 | tf_op jit(solution)/shard_map/ppermute | solution.py:28
  59.8 3.9 %all-to-all-start.1 = ((f32[32,1,128]{2,1,0:T(1,128)}), f32[32,1,128]{2,1,0:T(1,128)S(1)}, u32[]{:S(2)}, u32[]{:S(2)}) async-start(f32[32,1,128]{2,1,0:T(1,128)} %bitcast.21), calls=%async_computation.1 | async-start | bytes 32768 | tf_op jit(solution)/shard_map/all_to_all | solution.py:509
  63.8 1.8 collective-permute-start.13
  78.8 1.8 shard_map.116
  86.0 2.4 %collective-permute-start.20 = (f32[192,128]{1,0:T(8,128)S(1)}, f32[192,128]{1,0:T(8,128)S(1)}, u32[]{:S(2)}, u32[]{:S(2)}) collective-permute-start(f32[192,128]{1,0:T(8,128)S(1)} %add.244), channel_id=1, source_target_pairs={{0,16},{4,20},{8,24},{12,28},{16,0},{20,4},{24,8},{28,12},{1,17},{... | collective-permute-start | bytes 294920 | tf_op jit(solution)/shard_map/ppermute | solution.py:33
  88.3 2.9 %shard_map.118 = (f32[192,1152]{1,0:T(8,128)S(1)}, bf16[192,1152]{1,0:T(8,128)(2,1)S(1)}) custom-call(s32[1,1]{1,0:T(1,128)} %bitcast.1.strand_ref.refs_0_.refs_1_, bf16[768,256]{1,0:T(8,128)(2,1)} %shard_map.112.refs_1_, bf16[256,384]{1,0:T(8,128)(2,1)S(1)} %get-tuple-element.197.refs_2_, bf16[768,256]{1,0:T(8,128)(2,1)} %collective-permute-done.14.refs_3_, ...), custom_call_target="tpu_custom_call" | custom-call | flops 1 | bytes 1 | tf_op jit(solution)/shard_map/pallas_call | solution.py:76
  91.2 3.0 %collective-permute-done.20 = f32[192,128]{1,0:T(8,128)S(1)} collective-permute-done((f32[192,128]{1,0:T(8,128)S(1)}, f32[192,128]{1,0:T(8,128)S(1)}, u32[]{:S(2)}, u32[]{:S(2)}) %collective-permute-start.20) | collective-permute-done | bytes 98336 | tf_op jit(solution)/shard_map/ppermute | solution.py:33
  98.7 1.8 shard_map.120
  105.3 2.1 %collective-permute-done.27.refs_1_ = bf16[192,1152]{1,0:T(8,128)(2,1)S(1)} collective-permute-done((bf16[192,1152]{1,0:T(8,128)(2,1)S(1)}, bf16[192,1152]{1,0:T(8,128)(2,1)S(1)}, u32[]{:S(2)}, u32[]{:S(2)}) %collective-permute-start.27) | collective-permute-done | bytes 442400 | tf_op jit(solution)/shard_map/ppermute | solution.py:33
  108.6 1.8 shard_map.123
  115.5 2.6 %shard_map.126 = (f32[192,1152]{1,0:T(8,128)S(1)}, bf16[192,1152]{1,0:T(8,128)(2,1)}) custom-call(s32[1,1]{1,0:T(1,128)} %bitcast.1.strand_ref.refs_0_.refs_1_, bf16[768,256]{1,0:T(8,128)(2,1)S(1)} %copy-done.17, bf16[256,384]{1,0:T(8,128)(2,1)S(1)} %get-tuple-element.234.refs_2_, bf16[768,256]{1,0:T(8,128)(2,1)S(1)} %copy-done.37, ...), custom_call_target="tpu_custom_call" | custom-call | flops 1 | bytes 1 | tf_op jit(solution)/shard_map/pallas_call | solution.py:76
  120.9 4.1 %collective-permute-done.37.refs_1_ = bf16[192,1152]{1,0:T(8,128)(2,1)S(1)} collective-permute-done((bf16[192,1152]{1,0:T(8,128)(2,1)S(1)}, bf16[192,1152]{1,0:T(8,128)(2,1)S(1)}, u32[]{:S(2)}, u32[]{:S(2)}) %collective-permute-start.37) | collective-permute-done | bytes 442400 | tf_op jit(solution)/shard_map/ppermute | solution.py:33
  127.5 5.0 %all-to-all-start.2 = ((bf16[8,24,512]{2,1,0:T(8,128)(2,1)}), bf16[8,24,512]{2,1,0:T(8,128)(2,1)}, u32[]{:S(2)}, u32[]{:S(2)}) async-start(bf16[8,24,512]{2,1,0:T(8,128)(2,1)} %bitcast.36), calls=%async_computation.2 | async-start | bytes 393216 | tf_op jit(solution)/shard_map/all_to_all | solution.py:597
  132.5 2.0 %collective-permute-start.33 = (bf16[192,1152]{1,0:T(8,128)(2,1)}, bf16[192,1152]{1,0:T(8,128)(2,1)}, u32[]{:S(2)}, u32[]{:S(2)}) collective-permute-start(bf16[192,1152]{1,0:T(8,128)(2,1)} %get-tuple-element.240), channel_id=1, source_target_pairs={{0,4},{4,0},{8,12},{12,8},{16,20},{20,16},{24,28},{28,24},{1,5},{5... | collective-permute-start | bytes 1327112 | tf_op jit(solution)/shard_map/ppermute | solution.py:33
  138.9 2.4 %collective-permute-start.43 = (bf16[96,576]{1,0:T(8,128)(2,1)S(1)}, bf16[96,576]{1,0:T(8,128)(2,1)S(1)}, u32[]{:S(2)}, u32[]{:S(2)}) collective-permute-start(bf16[96,576]{1,0:T(8,128)(2,1)S(1)} %get-tuple-element.274), channel_id=1, source_target_pairs={{0,16},{4,20},{8,24},{12,28},{16,0},{20,4},{24,8},{28,12},{1,17},{... | collective-permute-start | bytes 331784 | tf_op jit(solution)/shard_map/ppermute | solution.py:33
  143.6 2.6 %collective-permute-done.38.refs_1_ = bf16[96,1152]{1,0:T(8,128)(2,1)S(1)} collective-permute-done((bf16[96,1152]{1,0:T(8,128)(2,1)S(1)}, bf16[96,1152]{1,0:T(8,128)(2,1)S(1)}, u32[]{:S(2)}, u32[]{:S(2)}) %collective-permute-start.38) | collective-permute-done | bytes 221216 | tf_op jit(solution)/shard_map/ppermute | solution.py:33
  147.9 4.1 %all-to-all-start.3 = ((f32[8,24,512]{2,1,0:T(8,128)}), f32[8,24,512]{2,1,0:T(8,128)}, u32[]{:S(2)}, u32[]{:S(2)}) async-start(f32[8,24,512]{2,1,0:T(8,128)} %broadcast_in_dim.11), calls=%async_computation.3 | async-start | bytes 786432 | tf_op jit(solution)/shard_map/all_to_all | solution.py:600
  154.2 2.0 %collective-permute-start.34 = (bf16[96,1152]{1,0:T(8,128)(2,1)S(1)}, bf16[96,1152]{1,0:T(8,128)(2,1)S(1)}, u32[]{:S(2)}, u32[]{:S(2)}) collective-permute-start(bf16[96,1152]{1,0:T(8,128)(2,1)S(1)} %get-tuple-element.242), channel_id=1, source_target_pairs={{0,8},{4,12},{8,0},{12,4},{16,24},{20,28},{24,16},{28,20},{1,9},{5... | collective-permute-start | bytes 663560 | tf_op jit(solution)/shard_map/ppermute | solution.py:33
  156.4 2.5 %collective-permute-start.41 = (bf16[96,576]{1,0:T(8,128)(2,1)S(1)}, bf16[96,576]{1,0:T(8,128)(2,1)S(1)}, u32[]{:S(2)}, u32[]{:S(2)}) collective-permute-start(bf16[96,576]{1,0:T(8,128)(2,1)S(1)} %get-tuple-element.272), channel_id=1, source_target_pairs={{0,16},{4,20},{8,24},{12,28},{16,0},{20,4},{24,8},{28,12},{1,17},{... | collective-permute-start | bytes 331784 | tf_op jit(solution)/shard_map/ppermute | solution.py:33
  159.5 9.3 %collective-permute-done.34.refs_1_ = bf16[96,1152]{1,0:T(8,128)(2,1)S(1)} collective-permute-done((bf16[96,1152]{1,0:T(8,128)(2,1)S(1)}, bf16[96,1152]{1,0:T(8,128)(2,1)S(1)}, u32[]{:S(2)}, u32[]{:S(2)}) %collective-permute-start.34) | collective-permute-done | bytes 221216 | tf_op jit(solution)/shard_map/ppermute | solution.py:33
  169.4 2.8 %fusion = f32[192,5313]{1,0:T(8,128)} fusion(bf16[128,5313]{1,0:T(8,128)(2,1)S(1)} %copy-done.64, bf16[192,128]{1,0:T(8,128)(2,1)S(1)} %get-tuple-element.303, bf16[192,128]{1,0:T(8,128)(2,1)S(1)} %get-tuple-element.302, bf16[192,128]{1,0:T(8,128)(2,1)S(1)} %get-tuple-element.282), kind=kOutput, calls=%fused_computation | convolution fusion | flops 796117248 | bytes 5587968 | tf_op jit(solution)/shard_map/dot_general | solution.py:606
  174.8 2.3 %collective-permute-done.40.refs_6_ = bf16[96,576]{1,0:T(8,128)(2,1)S(1)} collective-permute-done((bf16[96,576]{1,0:T(8,128)(2,1)S(1)}, bf16[96,576]{1,0:T(8,128)(2,1)S(1)}, u32[]{:S(2)}, u32[]{:S(2)}) %collective-permute-start.40) | collective-permute-done | bytes 110624 | tf_op jit(solution)/shard_map/ppermute | solution.py:33
  182.0 1.8 copy.14
  (289 shorter events, 84.9 us)
Async XLA Ops:
  0.7 20.4 %collective-permute-start.3 = (bf16[5,3,192,768]{3,2,1,0:T(8,128)(2,1)}, bf16[5,3,192,768]{3,2,1,0:T(8,128)(2,1)}, u32[]{:S(2)}, u32[]{:S(2)}) collective-permute-start(bf16[5,3,192,768]{3,2,1,0:T(8,128)(2,1)} %own_ref.5), channel_id=1, source_target_pairs={{0,1},{1,0},{2,3},{3,2},{4,5},{5,4},{6,7},{7,6},{8,9},{9,8},{10,11... | collective-permute-start | bytes 13271048 | tf_op jit(solution)/shard_map/ppermute | solution.py:23
  1.2 12.3 %collective-permute-start.1 = (bf16[192,512]{1,0:T(8,128)(2,1)}, bf16[192,512]{1,0:T(8,128)(2,1)}, u32[]{:S(2)}, u32[]{:S(2)}) collective-permute-start(bf16[192,512]{1,0:T(8,128)(2,1)} %refs_0_.3), channel_id=1, source_target_pairs={{0,2},{1,3},{2,0},{3,1},{4,6},{5,7},{6,4},{7,5},{8,10},{9,11},{10,... | collective-permute-start | bytes 589832 | tf_op jit(solution)/shard_map/ppermute | solution.py:28
  3.7 14.6 %collective-permute-start = (bf16[192,512]{1,0:T(8,128)(2,1)}, bf16[192,512]{1,0:T(8,128)(2,1)}, u32[]{:S(2)}, u32[]{:S(2)}) collective-permute-start(bf16[192,512]{1,0:T(8,128)(2,1)} %refs_0_.3), channel_id=1, source_target_pairs={{0,1},{1,0},{2,3},{3,2},{4,5},{5,4},{6,7},{7,6},{8,9},{9,8},{10,11... | collective-permute-start | bytes 589832 | tf_op jit(solution)/shard_map/ppermute | solution.py:23
  5.6 12.7 %all-to-all-start = ((bf16[8,32,128]{2,1,0:T(8,128)(2,1)}), bf16[8,32,128]{2,1,0:T(8,128)(2,1)S(1)}, u32[]{:S(2)}, u32[]{:S(2)}) async-start(bf16[8,32,128]{2,1,0:T(8,128)(2,1)} %bitcast.2), calls=%async_computation | async-start | bytes 131072 | tf_op jit(solution)/shard_map/all_to_all | solution.py:414
  40.1 8.0 %collective-permute-start.9 = (bf16[768,256]{1,0:T(8,128)(2,1)S(1)}, bf16[768,256]{1,0:T(8,128)(2,1)S(1)}, u32[]{:S(2)}, u32[]{:S(2)}) collective-permute-start(bf16[768,256]{1,0:T(8,128)(2,1)S(1)} %shard_map.108.refs_1_), channel_id=1, source_target_pairs={{0,1},{1,0},{2,3},{3,2},{4,5},{5,4},{6,7},{7,6},{8,9},{9,8},{10,11... | collective-permute-start | bytes 1179656 | tf_op jit(solution)/shard_map/ppermute | solution.py:23
  40.9 7.1 %collective-permute-start.7 = (bf16[256,384]{1,0:T(8,128)(2,1)S(1)}, bf16[256,384]{1,0:T(8,128)(2,1)S(1)}, u32[]{:S(2)}, u32[]{:S(2)}) collective-permute-start(bf16[256,384]{1,0:T(8,128)(2,1)S(1)} %get-tuple-element.160), channel_id=1, source_target_pairs={{0,2},{1,3},{2,0},{3,1},{4,6},{5,7},{6,4},{7,5},{8,10},{9,11},{10,... | collective-permute-start | bytes 589832 | tf_op jit(solution)/shard_map/ppermute | solution.py:28
  49.0 7.9 %collective-permute-start.11 = (bf16[768,256]{1,0:T(8,128)(2,1)S(1)}, bf16[768,256]{1,0:T(8,128)(2,1)S(1)}, u32[]{:S(2)}, u32[]{:S(2)}) collective-permute-start(bf16[768,256]{1,0:T(8,128)(2,1)S(1)} %shard_map.110.refs_1_), channel_id=1, source_target_pairs={{0,1},{1,0},{2,3},{3,2},{4,5},{5,4},{6,7},{7,6},{8,9},{9,8},{10,11... | collective-permute-start | bytes 1179656 | tf_op jit(solution)/shard_map/ppermute | solution.py:23
  49.5 7.4 %collective-permute-start.10 = (bf16[256,384]{1,0:T(8,128)(2,1)S(1)}, bf16[256,384]{1,0:T(8,128)(2,1)S(1)}, u32[]{:S(2)}, u32[]{:S(2)}) collective-permute-start(bf16[256,384]{1,0:T(8,128)(2,1)S(1)} %get-tuple-element.169), channel_id=1, source_target_pairs={{0,2},{1,3},{2,0},{3,1},{4,6},{5,7},{6,4},{7,5},{8,10},{9,11},{10,... | collective-permute-start | bytes 589832 | tf_op jit(solution)/shard_map/ppermute | solution.py:28
  57.8 12.9 %collective-permute-start.14 = (bf16[768,256]{1,0:T(8,128)(2,1)}, bf16[768,256]{1,0:T(8,128)(2,1)}, u32[]{:S(2)}, u32[]{:S(2)}) collective-permute-start(bf16[768,256]{1,0:T(8,128)(2,1)} %shard_map.112.refs_1_), channel_id=1, source_target_pairs={{0,1},{1,0},{2,3},{3,2},{4,5},{5,4},{6,7},{7,6},{8,9},{9,8},{10,11... | collective-permute-start | bytes 1179656 | tf_op jit(solution)/shard_map/ppermute | solution.py:23
  59.8 10.9 %all-to-all-start.1 = ((f32[32,1,128]{2,1,0:T(1,128)}), f32[32,1,128]{2,1,0:T(1,128)S(1)}, u32[]{:S(2)}, u32[]{:S(2)}) async-start(f32[32,1,128]{2,1,0:T(1,128)} %bitcast.21), calls=%async_computation.1 | async-start | bytes 32768 | tf_op jit(solution)/shard_map/all_to_all | solution.py:509
  70.7 7.1 %collective-permute-start.17 = (bf16[768,256]{1,0:T(8,128)(2,1)}, bf16[768,256]{1,0:T(8,128)(2,1)S(1)}, u32[]{:S(2)}, u32[]{:S(2)}) collective-permute-start(bf16[768,256]{1,0:T(8,128)(2,1)} %copy-done.28), channel_id=1, source_target_pairs={{0,1},{1,0},{2,3},{3,2},{4,5},{5,4},{6,7},{7,6},{8,9},{9,8},{10,11... | collective-permute-start | bytes 1179656 | tf_op jit(solution)/shard_map/ppermute | solution.py:23
  75.5 7.3 %collective-permute-start.15 = (bf16[256,384]{1,0:T(8,128)(2,1)S(1)}, bf16[256,384]{1,0:T(8,128)(2,1)S(1)}, u32[]{:S(2)}, u32[]{:S(2)}) collective-permute-start(bf16[256,384]{1,0:T(8,128)(2,1)S(1)} %bitcast.95), channel_id=1, source_target_pairs={{0,2},{1,3},{2,0},{3,1},{4,6},{5,7},{6,4},{7,5},{8,10},{9,11},{10,... | collective-permute-start | bytes 589832 | tf_op jit(solution)/shard_map/ppermute | solution.py:28
  82.8 14.5 %collective-permute-start.23 = (bf16[192,1152]{1,0:T(8,128)(2,1)S(1)}, bf16[192,1152]{1,0:T(8,128)(2,1)S(1)}, u32[]{:S(2)}, u32[]{:S(2)}) collective-permute-start(bf16[192,1152]{1,0:T(8,128)(2,1)S(1)} %get-tuple-element.207), channel_id=1, source_target_pairs={{0,4},{4,0},{8,12},{12,8},{16,20},{20,16},{24,28},{28,24},{1,5},{5... | collective-permute-start | bytes 1327112 | tf_op jit(solution)/shard_map/ppermute | solution.py:33
  84.4 9.8 %collective-permute-start.19 = (bf16[256,384]{1,0:T(8,128)(2,1)S(1)}, bf16[256,384]{1,0:T(8,128)(2,1)S(1)}, u32[]{:S(2)}, u32[]{:S(2)}) collective-permute-start(bf16[256,384]{1,0:T(8,128)(2,1)S(1)} %bitcast.96), channel_id=1, source_target_pairs={{0,2},{1,3},{2,0},{3,1},{4,6},{5,7},{6,4},{7,5},{8,10},{9,11},{10,... | collective-permute-start | bytes 589832 | tf_op jit(solution)/shard_map/ppermute | solution.py:28
  86.0 8.3 %collective-permute-start.20 = (f32[192,128]{1,0:T(8,128)S(1)}, f32[192,128]{1,0:T(8,128)S(1)}, u32[]{:S(2)}, u32[]{:S(2)}) collective-permute-start(f32[192,128]{1,0:T(8,128)S(1)} %add.244), channel_id=1, source_target_pairs={{0,16},{4,20},{8,24},{12,28},{16,0},{20,4},{24,8},{28,12},{1,17},{... | collective-permute-start | bytes 294920 | tf_op jit(solution)/shard_map/ppermute | solution.py:33
  94.2 13.1 %collective-permute-start.27 = (bf16[192,1152]{1,0:T(8,128)(2,1)S(1)}, bf16[192,1152]{1,0:T(8,128)(2,1)S(1)}, u32[]{:S(2)}, u32[]{:S(2)}) collective-permute-start(bf16[192,1152]{1,0:T(8,128)(2,1)S(1)} %get-tuple-element.221), channel_id=1, source_target_pairs={{0,4},{4,0},{8,12},{12,8},{16,20},{20,16},{24,28},{28,24},{1,5},{5... | collective-permute-start | bytes 1327112 | tf_op jit(solution)/shard_map/ppermute | solution.py:33
  95.8 6.3 %collective-permute-start.22 = (bf16[256,384]{1,0:T(8,128)(2,1)S(1)}, bf16[256,384]{1,0:T(8,128)(2,1)S(1)}, u32[]{:S(2)}, u32[]{:S(2)}) collective-permute-start(bf16[256,384]{1,0:T(8,128)(2,1)S(1)} %bitcast.93), channel_id=1, source_target_pairs={{0,2},{1,3},{2,0},{3,1},{4,6},{5,7},{6,4},{7,5},{8,10},{9,11},{10,... | collective-permute-start | bytes 589832 | tf_op jit(solution)/shard_map/ppermute | solution.py:28
  97.4 9.9 %collective-permute-start.26 = (bf16[96,1152]{1,0:T(8,128)(2,1)S(1)}, bf16[96,1152]{1,0:T(8,128)(2,1)S(1)}, u32[]{:S(2)}, u32[]{:S(2)}) collective-permute-start(bf16[96,1152]{1,0:T(8,128)(2,1)S(1)} %get-tuple-element.220), channel_id=1, source_target_pairs={{0,8},{4,12},{8,0},{12,4},{16,24},{20,28},{24,16},{28,20},{1,9},{5... | collective-permute-start | bytes 663560 | tf_op jit(solution)/shard_map/ppermute | solution.py:33
  102.1 13.4 %collective-permute-start.31 = (bf16[192,1152]{1,0:T(8,128)(2,1)S(1)}, bf16[192,1152]{1,0:T(8,128)(2,1)S(1)}, u32[]{:S(2)}, u32[]{:S(2)}) collective-permute-start(bf16[192,1152]{1,0:T(8,128)(2,1)S(1)} %get-tuple-element.233), channel_id=1, source_target_pairs={{0,4},{4,0},{8,12},{12,8},{16,20},{20,16},{24,28},{28,24},{1,5},{5... | collective-permute-start | bytes 1327112 | tf_op jit(solution)/shard_map/ppermute | solution.py:33
  111.7 6.4 %collective-permute-start.29 = (bf16[256,384]{1,0:T(8,128)(2,1)S(1)}, bf16[256,384]{1,0:T(8,128)(2,1)S(1)}, u32[]{:S(2)}, u32[]{:S(2)}) collective-permute-start(bf16[256,384]{1,0:T(8,128)(2,1)S(1)} %bitcast.94), channel_id=1, source_target_pairs={{0,2},{1,3},{2,0},{3,1},{4,6},{5,7},{6,4},{7,5},{8,10},{9,11},{10,... | collective-permute-start | bytes 589832 | tf_op jit(solution)/shard_map/ppermute | solution.py:28
  112.3 12.7 %collective-permute-start.37 = (bf16[192,1152]{1,0:T(8,128)(2,1)S(1)}, bf16[192,1152]{1,0:T(8,128)(2,1)S(1)}, u32[]{:S(2)}, u32[]{:S(2)}) collective-permute-start(bf16[192,1152]{1,0:T(8,128)(2,1)S(1)} %get-tuple-element.254), channel_id=1, source_target_pairs={{0,4},{4,0},{8,12},{12,8},{16,20},{20,16},{24,28},{28,24},{1,5},{5... | collective-permute-start | bytes 1327112 | tf_op jit(solution)/shard_map/ppermute | solution.py:33
  118.9 7.9 %collective-permute-start.36 = (bf16[96,1152]{1,0:T(8,128)(2,1)S(1)}, bf16[96,1152]{1,0:T(8,128)(2,1)S(1)}, u32[]{:S(2)}, u32[]{:S(2)}) collective-permute-start(bf16[96,1152]{1,0:T(8,128)(2,1)S(1)} %get-tuple-element.253), channel_id=1, source_target_pairs={{0,8},{4,12},{8,0},{12,4},{16,24},{20,28},{24,16},{28,20},{1,9},{5... | collective-permute-start | bytes 663560 | tf_op jit(solution)/shard_map/ppermute | solution.py:33
  127.5 18.7 %all-to-all-start.2 = ((bf16[8,24,512]{2,1,0:T(8,128)(2,1)}), bf16[8,24,512]{2,1,0:T(8,128)(2,1)}, u32[]{:S(2)}, u32[]{:S(2)}) async-start(bf16[8,24,512]{2,1,0:T(8,128)(2,1)} %bitcast.36), calls=%async_computation.2 | async-start | bytes 393216 | tf_op jit(solution)/shard_map/all_to_all | solution.py:597
  132.5 20.6 %collective-permute-start.33 = (bf16[192,1152]{1,0:T(8,128)(2,1)}, bf16[192,1152]{1,0:T(8,128)(2,1)}, u32[]{:S(2)}, u32[]{:S(2)}) collective-permute-start(bf16[192,1152]{1,0:T(8,128)(2,1)} %get-tuple-element.240), channel_id=1, source_target_pairs={{0,4},{4,0},{8,12},{12,8},{16,20},{20,16},{24,28},{28,24},{1,5},{5... | collective-permute-start | bytes 1327112 | tf_op jit(solution)/shard_map/ppermute | solution.py:33
  135.6 10.6 %collective-permute-start.38 = (bf16[96,1152]{1,0:T(8,128)(2,1)S(1)}, bf16[96,1152]{1,0:T(8,128)(2,1)S(1)}, u32[]{:S(2)}, u32[]{:S(2)}) collective-permute-start(bf16[96,1152]{1,0:T(8,128)(2,1)S(1)} %get-tuple-element.258), channel_id=1, source_target_pairs={{0,8},{4,12},{8,0},{12,4},{16,24},{20,28},{24,16},{28,20},{1,9},{5... | collective-permute-start | bytes 663560 | tf_op jit(solution)/shard_map/ppermute | solution.py:33
  138.9 33.3 %collective-permute-start.43 = (bf16[96,576]{1,0:T(8,128)(2,1)S(1)}, bf16[96,576]{1,0:T(8,128)(2,1)S(1)}, u32[]{:S(2)}, u32[]{:S(2)}) collective-permute-start(bf16[96,576]{1,0:T(8,128)(2,1)S(1)} %get-tuple-element.274), channel_id=1, source_target_pairs={{0,16},{4,20},{8,24},{12,28},{16,0},{20,4},{24,8},{28,12},{1,17},{... | collective-permute-start | bytes 331784 | tf_op jit(solution)/shard_map/ppermute | solution.py:33
  143.0 29.8 %collective-permute-start.42 = (bf16[96,576]{1,0:T(8,128)(2,1)S(1)}, bf16[96,576]{1,0:T(8,128)(2,1)S(1)}, u32[]{:S(2)}, u32[]{:S(2)}) collective-permute-start(bf16[96,576]{1,0:T(8,128)(2,1)S(1)} %get-tuple-element.273), channel_id=1, source_target_pairs={{0,16},{4,20},{8,24},{12,28},{16,0},{20,4},{24,8},{28,12},{1,17},{... | collective-permute-start | bytes 331784 | tf_op jit(solution)/shard_map/ppermute | solution.py:33
  147.9 34.1 %all-to-all-start.3 = ((f32[8,24,512]{2,1,0:T(8,128)}), f32[8,24,512]{2,1,0:T(8,128)}, u32[]{:S(2)}, u32[]{:S(2)}) async-start(f32[8,24,512]{2,1,0:T(8,128)} %broadcast_in_dim.11), calls=%async_computation.3 | async-start | bytes 786432 | tf_op jit(solution)/shard_map/all_to_all | solution.py:600
  154.2 14.6 %collective-permute-start.34 = (bf16[96,1152]{1,0:T(8,128)(2,1)S(1)}, bf16[96,1152]{1,0:T(8,128)(2,1)S(1)}, u32[]{:S(2)}, u32[]{:S(2)}) collective-permute-start(bf16[96,1152]{1,0:T(8,128)(2,1)S(1)} %get-tuple-element.242), channel_id=1, source_target_pairs={{0,8},{4,12},{8,0},{12,4},{16,24},{20,28},{24,16},{28,20},{1,9},{5... | collective-permute-start | bytes 663560 | tf_op jit(solution)/shard_map/ppermute | solution.py:33
  156.4 18.5 %collective-permute-start.41 = (bf16[96,576]{1,0:T(8,128)(2,1)S(1)}, bf16[96,576]{1,0:T(8,128)(2,1)S(1)}, u32[]{:S(2)}, u32[]{:S(2)}) collective-permute-start(bf16[96,576]{1,0:T(8,128)(2,1)S(1)} %get-tuple-element.272), channel_id=1, source_target_pairs={{0,16},{4,20},{8,24},{12,28},{16,0},{20,4},{24,8},{28,12},{1,17},{... | collective-permute-start | bytes 331784 | tf_op jit(solution)/shard_map/ppermute | solution.py:33
  158.9 18.2 %collective-permute-start.40 = (bf16[96,576]{1,0:T(8,128)(2,1)S(1)}, bf16[96,576]{1,0:T(8,128)(2,1)S(1)}, u32[]{:S(2)}, u32[]{:S(2)}) collective-permute-start(bf16[96,576]{1,0:T(8,128)(2,1)S(1)} %get-tuple-element.271), channel_id=1, source_target_pairs={{0,16},{4,20},{8,24},{12,28},{16,0},{20,4},{24,8},{28,12},{1,17},{... | collective-permute-start | bytes 331784 | tf_op jit(solution)/shard_map/ppermute | solution.py:33
  169.0 9.5 %collective-permute-start.39 = (bf16[96,576]{1,0:T(8,128)(2,1)S(1)}, bf16[96,576]{1,0:T(8,128)(2,1)S(1)}, u32[]{:S(2)}, u32[]{:S(2)}) collective-permute-start(bf16[96,576]{1,0:T(8,128)(2,1)S(1)} %get-tuple-element.270), channel_id=1, source_target_pairs={{0,16},{4,20},{8,24},{12,28},{16,0},{20,4},{24,8},{28,12},{1,17},{... | collective-permute-start | bytes 331784 | tf_op jit(solution)/shard_map/ppermute | solution.py:33
  (86 other events, 472.6 us)

commit v2 on v1

--- a/solution.py
+++ b/solution.py
@@ -9,6 +9,9 @@
 WIN = 16
 CORES = 2
 VMEM = 12 << 20
+DUE = (("middle2", "middle3", "end4"), ("middle3", "middle4", "summed"), ("middle4", "end4", "summed"), ("end4", "summed", "needed"), ("summed", "needed", "needed"))
+POOLED_DUE = ("sent", "summed")
+HIGH_FIRST = (1, 0, 0, 0, 0)
 
 bf16 = jnp.bfloat16
 f32 = jnp.float32
@@ -289,9 +292,8 @@
     return [jnp.where(late, 0.0, taps).astype(bf16), jnp.where(late, taps, 0.0).astype(bf16)]
 
 
-def filter_product(strand, active, upstream, active_sibling, upstream_sibling, reach, quarter):
+def filter_product(strand, active, upstream, active_sibling, upstream_sibling, reach, quarter, parts):
     half = active.shape[0] // 2
-    rows = half // 2
 
     def body(roll, strand, active, upstream, active_sibling, upstream_sibling):
         fields = [active[:half], active[half:], active_sibling[:half], active_sibling[half:]]
@@ -300,12 +302,12 @@
         total = jnp.dot(
             jnp.concatenate(fields, axis=1), jnp.concatenate(taps), preferred_element_type=f32
         )
-        return total[:rows], total[rows:].astype(bf16)
-
-    shape = (rows, 6 * quarter)
+        return parted(total, parts)
+
+    shape = (half // parts, 6 * quarter)
     return run(
         body,
-        [(shape, f32), (shape, bf16)],
+        [(shape, f32)] + [(shape, bf16)] * (parts - 1),
         strand,
         active,
         upstream,
@@ -328,59 +330,81 @@
 
 
 class BlockSum:
-    def __init__(self, kept, sent, slot):
-        self.kept, self.sent, self.slot = kept, sent, slot
-        self.bit = 1
-        self.received = None
-
-    def start(self):
-        if self.sent is not None and self.received is None:
-            self.received = seq_swap(self.sent, self.bit)
+    def __init__(self, kept, sends, slot, stages):
+        self.kept, self.slot, self.stages = kept, slot, stages
+        self.received = self.sent(sends)
+        self.done = False
+
+    def sent(self, sends):
+        return [seq_swap(part, away) for part, away in zip(sends, distances(self.stages[0])[1:])]
 
     def last(self):
-        return 2 * self.bit >= lax.axis_size("seq")
+        return len(self.stages) == 1
+
+    def due(self):
+        step = 3 - min(3, len(self.stages))
+        return None if self.done else DUE[self.slot][step]
 
     def join(self):
+        self.stages = self.stages[1:]
+        parts = len(distances(self.stages[0]))
         rows, width = self.kept.shape
-        axis = 1 if 4 * self.bit >= lax.axis_size("seq") else 0
-        half = (rows, width // 2) if axis else (rows // 2, width)
-
-        def body(roll, kept, received):
-            total = kept + received.astype(f32)
-            if axis:
-                return total[:, : half[1]], total[:, half[1] :].astype(bf16)
-            return total[: half[0]], total[half[0] :].astype(bf16)
-
-        self.kept, self.sent = run(body, [(half, f32), (half, bf16)], self.kept, self.received)
-        self.bit *= 2
-        self.received = None
-
-
-def settle(sums, value):
-    value, received = tied(value, [s.received for s in sums])
-    for s, got in zip(sums, received):
+        rows //= parts
+
+        def body(roll, kept, *received):
+            total = kept
+            for part in received:
+                total = total + part.astype(f32)
+            return parted(total, parts)
+
+        outs = [((rows, width), f32)] + [((rows, width), bf16)] * (parts - 1)
+        self.kept, *sends = run(body, outs, self.kept, *self.received)
+        self.received = self.sent(sends)
+
+
+def distances(bits):
+    return [sum(bit for place, bit in enumerate(bits) if (i >> place) & 1) for i in range(1 << len(bits))]
+
+
+def parted(total, parts):
+    rows = total.shape[0] // parts
+    pieces_of = [total[i * rows : (i + 1) * rows] for i in range(parts)]
+    return [pieces_of[0]] + [piece.astype(bf16) for piece in pieces_of[1:]]
+
+
+def settle(sums, value, point):
+    due = [s for s in sums if s.due() == point]
+    value, received = tied(value, [s.received for s in due])
+    for s, got in zip(due, received):
         s.received = got
-        s.join()
-        s.start()
+        if s.last():
+            s.done = True
+        else:
+            s.join()
     return value
 
 
 def assemble(sums, quarter):
-    block = sums[0].kept.shape[0]
-    taps = sums[0].kept.shape[1] // quarter
     count = len(sums)
+    each = 1 + len(sums[0].received)
+    half, width = sums[0].kept.shape
+    shape = (3, quarter, 2 * half)
 
     def kernel(*refs):
         out = refs[-1]
         for layer in range(count):
-            total = refs[layer][...] + refs[count + layer][...].astype(f32)
-            out[layer] = total.T.reshape(taps, quarter, block)
+            total = refs[each * layer][...]
+            for part in range(1, each):
+                total = total + refs[each * layer + part][...].astype(f32)
+            total = jnp.concatenate([total[:, : width // 2], total[:, width // 2 :]])
+            out[layer] = total.T.reshape(shape)
 
     return pl.pallas_call(
         kernel,
-        out_shape=jax.ShapeDtypeStruct((count, taps, quarter, block), f32),
+        out_shape=jax.ShapeDtypeStruct((count,) + shape, f32),
         compiler_params=pltpu.CompilerParams(vmem_limit_bytes=VMEM),
-    )(*[s.kept for s in sums], *[s.received for s in sums])
+        cost_estimate=pl.CostEstimate(flops=1, bytes_accessed=1, transcendentals=0),
+    )(*[value for s in sums for value in [s.kept, *s.received]])
 
 
 def shards(
@@ -440,15 +464,20 @@
         jnp.arange(tracks, dtype=jnp.int32)[None, :] == window_track[:, None]
     ).astype(bf16)
 
-    bits = seqs.bit_length() - 1
-    slot = jnp.arange(channels, dtype=jnp.int32) // block
-    away = (slot >> (bits - 1)) << (bits - 1)
-    for b in range(bits - 1):
-        away = away + (((slot >> (bits - 2 - b)) & 1) << b)
-    wanted = (seq ^ away) * block + jnp.arange(channels, dtype=jnp.int32) % block
-    by_distance = (
-        wanted[:, None] == jnp.arange(channels, dtype=jnp.int32)[None, :]
-    ).astype(bf16)
+    low_first = [(1 << b,) for b in range(seqs.bit_length() - 1)]
+    orders = [low_first, low_first[1:] + low_first[:1]]
+    place = jnp.arange(channels, dtype=jnp.int32)
+    later, local = place // (channels // 2), place % (channels // 2)
+    by_distance = []
+    for order in orders:
+        aways = [0]
+        for stage in order:
+            aways = [away + far for away in aways for far in distances(stage)]
+        away = choose(local // (block // 2), [jnp.full_like(place, away) for away in aways])
+        wanted = (seq ^ away) * block + later * (block // 2) + local % (block // 2)
+        by_distance.append(
+            (wanted[:, None] == jnp.arange(channels, dtype=jnp.int32)[None, :]).astype(bf16)
+        )
 
     filters = [filter_of(0)]
     streams = []
@@ -471,7 +500,7 @@
             parts = [chip_shift(own, by) for by in range(1, chips)]
             beside = [
                 filter_of(layer + 1),
-                placed(by_distance, active),
+                placed(by_distance[HIGH_FIRST[LAYERS - 1 - layer]], active),
             ]
             if layer == 1:
                 columns = lax.dot_general(
@@ -510,9 +539,9 @@
     pooled_own = pooled_own + core_swap(pooled_sent)
     pooled_bit = 1
     if pooled_bit < seqs:
-        pooled_own = pooled_own + seq_swap(pooled_own, pooled_bit)
+        pooled_own = pooled_own + seq_swap(pooled_own.astype(bf16), pooled_bit).astype(f32)
         pooled_bit *= 2
-    last_active = placed(by_distance, active)
+    last_active = placed(by_distance[HIGH_FIRST[0]], active)
     sibling_active = core_swap(actives[-1])
     scores, pooled_own, last_active, sibling_active = tied(
         scores, pooled_own, last_active, sibling_active
@@ -522,6 +551,22 @@
     sibling_actives.append(core_swap(last_active))
 
     sums = []
+
+    def pooled_step(pooled, value, point):
+        total, received, bit, due = pooled
+        if not due or due[0] != point:
+            return value, pooled
+        value, received = tied(value, received)
+        total = total + received.astype(f32)
+        bit *= 2
+        return value, (total, seq_swap(total.astype(bf16), bit) if bit < seqs else None, bit, due[1:])
+
+    pooled = (
+        pooled_own,
+        seq_swap(pooled_own.astype(bf16), pooled_bit) if pooled_bit < seqs else None,
+        pooled_bit,
+        POOLED_DUE,
+    )
     aligned = (channels // chips) % 128 == 0
     shape = (shard_rows, channels // chips)
     back_outs = [
@@ -559,15 +604,9 @@
                 inside=aligned,
             )
         received = jnp.stack([chip_shift(sends[by - 1], by) for by in range(1, chips)])
-        upstream = settle(
-            [s for s in sums if not s.last() and s.slot < LAYERS - 2 - layer], upstream
-        )
-        if pooled_bit < seqs:
-            pooled_received = seq_swap(pooled_own, pooled_bit)
-            pooled_bit *= 2
-        else:
-            pooled_received = jnp.zeros_like(pooled_own)
-        keep, send = filter_product(
+        slot = LAYERS - 1 - layer
+        upstream = settle(sums, upstream, f"middle{slot}")
+        kept, *parts = filter_product(
             strand_word,
             actives[layer],
             upstream,
@@ -575,11 +614,12 @@
             core_swap(theirs),
             reach[layer],
             quarter,
-        )
-        received, pooled_received, keep, send = tied(received, pooled_received, keep, send)
-        pooled_own = pooled_own + pooled_received
-        sums.append(BlockSum(keep, send, LAYERS - 1 - layer))
-        sums[-1].start()
+            2,
+        )
+        received, kept = tied(received, kept)
+        received = settle(sums, received, f"end{slot}")
+        received, pooled = pooled_step(pooled, received, f"end{slot}")
+        sums.append(BlockSum(kept, parts, slot, orders[HIGH_FIRST[slot]]))
         state = (grad, mine, received, streams[layer])
 
     stem_shape = (quarter, letters.shape[1])
@@ -593,16 +633,21 @@
     )
     stem_own = stem_keep + core_swap(stem_away).astype(f32)
     stem_send = stem_own.astype(bf16).reshape(seqs, quarter // seqs, -1)
-    stem_send = settle([s for s in sums if not s.last() and s.slot < LAYERS - 1], stem_send)
+    stem_send = settle(sums, stem_send, "sent")
+    stem_send, pooled = pooled_step(pooled, stem_send, "sent")
     stem_blocks = lax.all_to_all(stem_send, "seq", 0, 0, tiled=True)
-    stem_blocks = settle([s for s in sums if not s.last() and s.slot < LAYERS - 1], stem_blocks)
-    stem_block = jnp.sum(stem_blocks.astype(f32), axis=0)
+    stem_blocks = settle(sums, stem_blocks, "summed")
+    stem_blocks, pooled = pooled_step(pooled, stem_blocks, "summed")
+    stem_block = jnp.sum(stem_blocks.astype(f32), axis=0).astype(bf16)
     stem_grad = lax.all_to_all(
         jnp.broadcast_to(stem_block, (seqs,) + stem_block.shape), "seq", 0, 0, tiled=True
-    ).reshape(quarter, -1)
-    while pooled_bit < seqs:
-        pooled_own = pooled_own + seq_swap(pooled_own, pooled_bit)
-        pooled_bit *= 2
+    )
+    stem_grad = stem_grad.reshape(quarter, -1).astype(f32)
+    pooled_own, received, bit, _ = pooled
+    while received is not None:
+        pooled_own = pooled_own + received.astype(f32)
+        bit *= 2
+        received = seq_swap(pooled_own.astype(bf16), bit) if bit < seqs else None
     head_grad = lax.dot_general(
         jnp.concatenate(pieces(0.5 * loss_slope * pooled_own), axis=1),
         jnp.concatenate([at_track] * 3),
@@ -613,7 +658,6 @@
         for s in sums:
             if not s.last():
                 s.join()
-                s.start()
     conv_grad = assemble(sums[::-1], quarter)
     return (window_score[0], conv_grad, stem_grad, head_grad)
 

time: 185 us -> 177 us (0.957)
  local copies, waits for them, and re-layouts: 21.9 us -> 10.2 us
  other arithmetic: 8.09 us -> 11.8 us
  waiting for transfers between devices: 54 us -> 56.4 us
  starting transfers between devices: 54.2 us -> 52.2 us
    ppermute x18, waiting for transfers between devices: 30.5 us -> 14.3 us  [seq_swap(): return lax.ppermute(value, 'seq', [(i, i ^ bit) for i in range(count)])]
    unnamed x141 -> x106, local copies, waits for them, and re-layouts: 21 us -> 9.46 us
    ppermute x10, waiting for transfers between devices: 16.3 us -> 26.8 us  [chip_shift(): lax.ppermute(value, 'ch', [(i, (i + CORES * by) % count) for i in range(c...]
    all_to_all x1, waiting for transfers between devices: 0.01 us -> 4.74 us  [shards(): stem_blocks = lax.all_to_all(stem_send, 'seq', 0, 0, tiled=True)]
    convert_element_type x1 -> x6, other arithmetic: 0.26 us -> 3.97 us  [the longest x2 1.57 us: shards(): (wanted[:, None] == jnp.arange(channels, dtype=jnp.int32)[None, :]).astyp...]
    all_to_all x1, waiting for transfers between devices: 1.18 us -> 4.09 us  [shards(): lax.all_to_all(partial_score[:, None], ('seq', 'ch'), 0, 0, tiled=True)]
    ppermute x16, waiting for transfers between devices: 1.57 us -> 3.45 us  [core_swap(): return lax.ppermute(value, 'ch', [(i, i ^ 1) for i in range(count)])]
  transfers between devices with their start and end apart: 48 -> 48, of which waited for: 23 -> 21; matrix products, arithmetic and copies ran while one was open for 8% -> 9% of each run, Pallas kernels for 18% -> 18%
where the time goes in v2:
time: 177 us; the launch traced here: 176 us
  waiting for transfers between devices  56.4 us (32%)
  starting transfers between devices  52.2 us (29%)
  Pallas kernels  34.2 us (19%)
  other arithmetic  11.8 us (7%)
  local copies, waits for them, and re-layouts  10.2 us (6%)
  matrix products  9.57 us (5%)
    ppermute x10, waiting for transfers between devices, chip_shift(): lax.ppermute(value, 'ch', [(i, (i + CORES * by) % count) for i in range(c...  26.8 us
    pallas_call x28, Pallas kernels, run(): pl.pallas_call(kernel, out_shape=[jax.ShapeDtypeStruct(shape, kind) for s...  24 us
    ppermute x18, starting transfers between devices, seq_swap(): return lax.ppermute(value, 'seq', [(i, i ^ bit) for i in range(count)])  22.4 us
    ppermute x18, waiting for transfers between devices, seq_swap(): return lax.ppermute(value, 'seq', [(i, i ^ bit) for i in range(count)])  14.3 us
    ppermute x10, starting transfers between devices, chip_shift(): lax.ppermute(value, 'ch', [(i, (i + CORES * by) % count) for i in range(c...  9.53 us
    unnamed x106, local copies, waits for them, and re-layouts  9.46 us
    pallas_call x5, Pallas kernels, join_filters(): pl.pallas_call(kernel, out_shape=jax.ShapeDtypeStruct((taps, CORES * quar...  6.6 us
    dot_general x15, matrix products, shards(): lax.dot_general(rolled(active, (tap - 1) * reach[layer]), filters[layer][...  6.12 us
  transfers between devices with their start and end apart: 48, of which 21 were waited for; matrix products, arithmetic and copies ran while one was open for 9% of the time, Pallas kernels for 18%

profile of v2, /device:TPU:0, one launch (start us, length us, event | category | flops | bytes accessed | tf_op | source)
XLA Modules:
  0.0 176.2 jit_solution(16529526757696092212)
XLA Ops:
  1.2 2.6 %collective-permute-start.1 = (bf16[192,512]{1,0:T(8,128)(2,1)}, bf16[192,512]{1,0:T(8,128)(2,1)}, u32[]{:S(2)}, u32[]{:S(2)}) collective-permute-start(bf16[192,512]{1,0:T(8,128)(2,1)} %refs_0_.3), channel_id=1, source_target_pairs={{0,2},{1,3},{2,0},{3,1},{4,6},{5,7},{6,4},{7,5},{8,10},{9,11},{10,... | collective-permute-start | bytes 589832 | tf_op jit(solution)/shard_map/ppermute | solution.py:31
  5.6 5.8 %all-to-all-start = ((bf16[8,32,128]{2,1,0:T(8,128)(2,1)}), bf16[8,32,128]{2,1,0:T(8,128)(2,1)S(1)}, u32[]{:S(2)}, u32[]{:S(2)}) async-start(bf16[8,32,128]{2,1,0:T(8,128)(2,1)} %bitcast.2), calls=%async_computation | async-start | bytes 131072 | tf_op jit(solution)/shard_map/all_to_all | solution.py:438
  11.5 2.1 %fusion.6 = bf16[128,5313]{1,0:T(8,128)(2,1)} fusion(s32[128]{0:T(128)} %param.12), kind=kLoop, calls=%fused_computation.7 | loop fusion | flops 1360128 | bytes 1360640 | tf_op jit(solution)/shard_map/convert_element_type | solution.py:465
  15.3 3.1 %all-to-all-done = bf16[8,32,128]{2,1,0:T(8,128)(2,1)S(1)} async-done(((bf16[8,32,128]{2,1,0:T(8,128)(2,1)}), bf16[8,32,128]{2,1,0:T(8,128)(2,1)S(1)}, u32[]{:S(2)}, u32[]{:S(2)}) %all-to-all-start) | async-done | bytes 65568 | tf_op jit(solution)/shard_map/all_to_all | solution.py:438
  18.4 1.9 %shard_map.103 = (bf16[256,512]{1,0:T(8,128)(2,1)S(1)}, bf16[256,768]{1,0:T(8,128)(2,1)S(1)}, f32[256,384]{1,0:T(8,128)S(1)}) custom-call(s32[1,1]{1,0:T(1,128)} %bitcast.1.strand_ref.refs_0_.refs_1_, s32[1,1]{1,0:T(1,128)} %bitcast.chip_ref.refs_0_, bf16[256,128]{1,0:T(8,128)(2,1)S(1)} %bitcast.85, bf16[192,512]{1,0:T(8,128)(2,1)S(1)} %copy-done.43, ...), custom_call_target="tpu_custom_call" | custom-call | flops 1 | bytes 1 | tf_op jit(solution)/shard_map/pallas_call | solution.py:220
  21.1 2.3 %copy-done.2 = bf16[5,3,192,768]{3,2,1,0:T(8,128)(2,1)S(1)} copy-done((bf16[5,3,192,768]{3,2,1,0:T(8,128)(2,1)S(1)}, bf16[5,3,192,768]{3,2,1,0:T(8,128)(2,1)}, u32[]{:S(2)}) %copy-start.2) | copy-done | bytes 4423704
  29.2 2.6 %collective-permute-done.4 = bf16[256,384]{1,0:T(8,128)(2,1)S(1)} collective-permute-done((bf16[256,384]{1,0:T(8,128)(2,1)S(1)}, bf16[256,384]{1,0:T(8,128)(2,1)S(1)}, u32[]{:S(2)}, u32[]{:S(2)}) %collective-permute-start.4) | collective-permute-done | bytes 196640 | tf_op jit(solution)/shard_map/ppermute | solution.py:31
  36.7 2.1 %collective-permute-done.5 = bf16[256,384]{1,0:T(8,128)(2,1)S(1)} collective-permute-done((bf16[256,384]{1,0:T(8,128)(2,1)S(1)}, bf16[256,384]{1,0:T(8,128)(2,1)S(1)}, u32[]{:S(2)}, u32[]{:S(2)}) %collective-permute-start.5) | collective-permute-done | bytes 196640 | tf_op jit(solution)/shard_map/ppermute | solution.py:31
  43.4 4.6 %collective-permute-done.7 = bf16[256,384]{1,0:T(8,128)(2,1)S(1)} collective-permute-done((bf16[256,384]{1,0:T(8,128)(2,1)S(1)}, bf16[256,384]{1,0:T(8,128)(2,1)S(1)}, u32[]{:S(2)}, u32[]{:S(2)}) %collective-permute-start.7) | collective-permute-done | bytes 196640 | tf_op jit(solution)/shard_map/ppermute | solution.py:31
  52.7 4.1 %collective-permute-done.10 = bf16[256,384]{1,0:T(8,128)(2,1)S(1)} collective-permute-done((bf16[256,384]{1,0:T(8,128)(2,1)S(1)}, bf16[256,384]{1,0:T(8,128)(2,1)S(1)}, u32[]{:S(2)}, u32[]{:S(2)}) %collective-permute-start.10) | collective-permute-done | bytes 196640 | tf_op jit(solution)/shard_map/ppermute | solution.py:31
  62.0 4.1 %all-to-all-start.1 = ((f32[32,1,128]{2,1,0:T(1,128)}), f32[32,1,128]{2,1,0:T(1,128)S(1)}, u32[]{:S(2)}, u32[]{:S(2)}) async-start(f32[32,1,128]{2,1,0:T(1,128)} %bitcast.21), calls=%async_computation.1 | async-start | bytes 32768 | tf_op jit(solution)/shard_map/all_to_all | solution.py:538
  69.0 4.1 %all-to-all-done.1 = f32[32,1,128]{2,1,0:T(1,128)S(1)} async-done(((f32[32,1,128]{2,1,0:T(1,128)}), f32[32,1,128]{2,1,0:T(1,128)S(1)}, u32[]{:S(2)}, u32[]{:S(2)}) %all-to-all-start.1) | async-done | bytes 16416 | tf_op jit(solution)/shard_map/all_to_all | solution.py:538
  80.4 1.8 %shard_map.116 = (f32[192,1152]{1,0:T(8,128)S(1)}, bf16[192,1152]{1,0:T(8,128)(2,1)S(1)}) custom-call(s32[1,1]{1,0:T(1,128)} %bitcast.1.strand_ref.refs_0_.refs_1_, bf16[768,256]{1,0:T(8,128)(2,1)S(1)} %copy-done.30, bf16[256,384]{1,0:T(8,128)(2,1)S(1)} %get-tuple-element.193.refs_2_, bf16[768,256]{1,0:T(8,128)(2,1)S(1)} %collective-permute-done.16.refs_3_, ...), custom_call_target="tpu_custom_call" | custom-call | flops 1 | bytes 1 | tf_op jit(solution)/shard_map/pallas_call | solution.py:79
  82.8 2.4 %collective-permute-done.15 = bf16[256,384]{1,0:T(8,128)(2,1)S(1)} collective-permute-done((bf16[256,384]{1,0:T(8,128)(2,1)S(1)}, bf16[256,384]{1,0:T(8,128)(2,1)S(1)}, u32[]{:S(2)}, u32[]{:S(2)}) %collective-permute-start.15) | collective-permute-done | bytes 196640 | tf_op jit(solution)/shard_map/ppermute | solution.py:31
  87.6 2.9 %shard_map.118 = (f32[192,1152]{1,0:T(8,128)S(1)}, bf16[192,1152]{1,0:T(8,128)(2,1)S(1)}) custom-call(s32[1,1]{1,0:T(1,128)} %bitcast.1.strand_ref.refs_0_.refs_1_, bf16[768,256]{1,0:T(8,128)(2,1)} %shard_map.112.refs_1_, bf16[256,384]{1,0:T(8,128)(2,1)S(1)} %get-tuple-element.200.refs_2_, bf16[768,256]{1,0:T(8,128)(2,1)} %collective-permute-done.14.refs_3_, ...), custom_call_target="tpu_custom_call" | custom-call | flops 1 | bytes 1 | tf_op jit(solution)/shard_map/pallas_call | solution.py:79
  91.1 2.5 %collective-permute-done.18 = bf16[256,384]{1,0:T(8,128)(2,1)S(1)} collective-permute-done((bf16[256,384]{1,0:T(8,128)(2,1)S(1)}, bf16[256,384]{1,0:T(8,128)(2,1)S(1)}, u32[]{:S(2)}, u32[]{:S(2)}) %collective-permute-start.18) | collective-permute-done | bytes 196640 | tf_op jit(solution)/shard_map/ppermute | solution.py:31
  96.1 1.8 %shard_map.120 = (f32[192,1152]{1,0:T(8,128)S(1)}, bf16[192,1152]{1,0:T(8,128)(2,1)S(1)}) custom-call(s32[1,1]{1,0:T(1,128)} %bitcast.1.strand_ref.refs_0_.refs_1_, bf16[768,256]{1,0:T(8,128)(2,1)S(1)} %copy-done.24, bf16[256,384]{1,0:T(8,128)(2,1)S(1)} %get-tuple-element.210.refs_2_, bf16[768,256]{1,0:T(8,128)(2,1)S(1)} %copy-done.40, ...), custom_call_target="tpu_custom_call" | custom-call | flops 1 | bytes 1 | tf_op jit(solution)/shard_map/pallas_call | solution.py:79
  98.6 3.4 %collective-permute-done.20 = bf16[256,384]{1,0:T(8,128)(2,1)S(1)} collective-permute-done((bf16[256,384]{1,0:T(8,128)(2,1)S(1)}, bf16[256,384]{1,0:T(8,128)(2,1)S(1)}, u32[]{:S(2)}, u32[]{:S(2)}) %collective-permute-start.20) | collective-permute-done | bytes 196640 | tf_op jit(solution)/shard_map/ppermute | solution.py:31
  103.6 5.0 %collective-permute-done.24.refs_1_ = bf16[96,1152]{1,0:T(8,128)(2,1)S(1)} collective-permute-done((bf16[96,1152]{1,0:T(8,128)(2,1)S(1)}, bf16[96,1152]{1,0:T(8,128)(2,1)S(1)}, u32[]{:S(2)}, u32[]{:S(2)}) %collective-permute-start.24) | collective-permute-done | bytes 221216 | tf_op jit(solution)/shard_map/ppermute | solution.py:36
  108.8 1.8 %shard_map.123 = (f32[192,1152]{1,0:T(8,128)S(1)}, bf16[192,1152]{1,0:T(8,128)(2,1)S(1)}) custom-call(s32[1,1]{1,0:T(1,128)} %bitcast.1.strand_ref.refs_0_.refs_1_, bf16[768,256]{1,0:T(8,128)(2,1)S(1)} %copy-done.20, bf16[256,384]{1,0:T(8,128)(2,1)S(1)} %get-tuple-element.223.refs_2_, bf16[768,256]{1,0:T(8,128)(2,1)S(1)} %copy-done.38, ...), custom_call_target="tpu_custom_call" | custom-call | flops 1 | bytes 1 | tf_op jit(solution)/shard_map/pallas_call | solution.py:79
  112.7 5.1 %collective-permute-done.23 = bf16[256,384]{1,0:T(8,128)(2,1)S(1)} collective-permute-done((bf16[256,384]{1,0:T(8,128)(2,1)S(1)}, bf16[256,384]{1,0:T(8,128)(2,1)S(1)}, u32[]{:S(2)}, u32[]{:S(2)}) %collective-permute-start.23) | collective-permute-done | bytes 196640 | tf_op jit(solution)/shard_map/ppermute | solution.py:31
  125.4 1.8 %shard_map.126 = (f32[192,1152]{1,0:T(8,128)S(1)}, bf16[192,1152]{1,0:T(8,128)(2,1)S(1)}) custom-call(s32[1,1]{1,0:T(1,128)} %bitcast.1.strand_ref.refs_0_.refs_1_, bf16[768,256]{1,0:T(8,128)(2,1)S(1)} %copy-done.18, bf16[256,384]{1,0:T(8,128)(2,1)S(1)} %get-tuple-element.234.refs_2_, bf16[768,256]{1,0:T(8,128)(2,1)S(1)} %copy-done.36, ...), custom_call_target="tpu_custom_call" | custom-call | flops 1 | bytes 1 | tf_op jit(solution)/shard_map/pallas_call | solution.py:79
  133.6 2.9 %collective-permute-start.37 = (bf16[48,1152]{1,0:T(8,128)(2,1)}, bf16[48,1152]{1,0:T(8,128)(2,1)S(1)}, u32[]{:S(2)}, u32[]{:S(2)}) collective-permute-start(bf16[48,1152]{1,0:T(8,128)(2,1)} %get-tuple-element.260), channel_id=1, source_target_pairs={{0,16},{4,20},{8,24},{12,28},{16,0},{20,4},{24,8},{28,12},{1,17},{... | collective-permute-start | bytes 331784 | tf_op jit(solution)/shard_map/ppermute | solution.py:36
  137.3 4.0 %all-to-all-start.2 = ((bf16[8,24,512]{2,1,0:T(8,128)(2,1)}), bf16[8,24,512]{2,1,0:T(8,128)(2,1)}, u32[]{:S(2)}, u32[]{:S(2)}) async-start(bf16[8,24,512]{2,1,0:T(8,128)(2,1)} %bitcast.99), calls=%async_computation.2 | async-start | bytes 393216 | tf_op jit(solution)/shard_map/all_to_all | solution.py:638
  142.2 2.9 %collective-permute-start.43 = (bf16[192,128]{1,0:T(8,128)(2,1)S(1)}, bf16[192,128]{1,0:T(8,128)(2,1)}, u32[]{:S(2)}, u32[]{:S(2)}) collective-permute-start(bf16[192,128]{1,0:T(8,128)(2,1)S(1)} %fusion.93), channel_id=1, source_target_pairs={{0,16},{4,20},{8,24},{12,28},{16,0},{20,4},{24,8},{28,12},{1,17},{... | collective-permute-start | bytes 147464 | tf_op jit(solution)/shard_map/ppermute | solution.py:36
  145.1 4.7 %all-to-all-done.2 = bf16[8,24,512]{2,1,0:T(8,128)(2,1)} async-done(((bf16[8,24,512]{2,1,0:T(8,128)(2,1)}), bf16[8,24,512]{2,1,0:T(8,128)(2,1)}, u32[]{:S(2)}, u32[]{:S(2)}) %all-to-all-start.2) | async-done | bytes 196640 | tf_op jit(solution)/shard_map/all_to_all | solution.py:638
  152.1 3.6 %all-to-all-start.3 = ((bf16[8,24,512]{2,1,0:T(8,128)(2,1)}), bf16[8,24,512]{2,1,0:T(8,128)(2,1)S(1)}, u32[]{:S(2)}, u32[]{:S(2)}) async-start(bf16[8,24,512]{2,1,0:T(8,128)(2,1)} %broadcast_in_dim.11), calls=%async_computation.3 | async-start | bytes 393216 | tf_op jit(solution)/shard_map/all_to_all | solution.py:642
  155.8 2.1 %collective-permute-start.40 = (bf16[96,1152]{1,0:T(8,128)(2,1)S(1)}, bf16[96,1152]{1,0:T(8,128)(2,1)S(1)}, u32[]{:S(2)}, u32[]{:S(2)}) collective-permute-start(bf16[96,1152]{1,0:T(8,128)(2,1)S(1)} %get-tuple-element.267), channel_id=1, source_target_pairs={{0,8},{4,12},{8,0},{12,4},{16,24},{20,28},{24,16},{28,20},{1,9},{5... | collective-permute-start | bytes 663560 | tf_op jit(solution)/shard_map/ppermute | solution.py:36
  158.9 2.4 %collective-permute-start.42 = (bf16[48,1152]{1,0:T(8,128)(2,1)S(1)}, bf16[48,1152]{1,0:T(8,128)(2,1)S(1)}, u32[]{:S(2)}, u32[]{:S(2)}) collective-permute-start(bf16[48,1152]{1,0:T(8,128)(2,1)S(1)} %get-tuple-element.273), channel_id=1, source_target_pairs={{0,16},{4,20},{8,24},{12,28},{16,0},{20,4},{24,8},{28,12},{1,17},{... | collective-permute-start | bytes 331784 | tf_op jit(solution)/shard_map/ppermute | solution.py:36
  161.3 5.7 %collective-permute-done.40.refs_1_ = bf16[96,1152]{1,0:T(8,128)(2,1)S(1)} collective-permute-done((bf16[96,1152]{1,0:T(8,128)(2,1)S(1)}, bf16[96,1152]{1,0:T(8,128)(2,1)S(1)}, u32[]{:S(2)}, u32[]{:S(2)}) %collective-permute-start.40) | collective-permute-done | bytes 221216 | tf_op jit(solution)/shard_map/ppermute | solution.py:36
  168.3 2.8 %fusion = f32[192,5313]{1,0:T(8,128)} fusion(bf16[128,5313]{1,0:T(8,128)(2,1)S(1)} %copy-done.49, bf16[192,128]{1,0:T(8,128)(2,1)S(1)} %get-tuple-element.309, bf16[192,128]{1,0:T(8,128)(2,1)S(1)} %get-tuple-element.308, bf16[192,128]{1,0:T(8,128)(2,1)S(1)} %get-tuple-element.286), kind=kOutput, calls=%fused_computation | convolution fusion | flops 796117248 | bytes 5587968 | tf_op jit(solution)/shard_map/dot_general | solution.py:651
  171.1 2.5 %collective-permute-done.41.refs_1_ = bf16[48,1152]{1,0:T(8,128)(2,1)S(1)} collective-permute-done((bf16[48,1152]{1,0:T(8,128)(2,1)S(1)}, bf16[48,1152]{1,0:T(8,128)(2,1)S(1)}, u32[]{:S(2)}, u32[]{:S(2)}) %collective-permute-start.41) | collective-permute-done | bytes 110624 | tf_op jit(solution)/shard_map/ppermute | solution.py:36
  (256 shorter events, 73.0 us)
Async XLA Ops:
  0.6 20.4 %collective-permute-start.3 = (bf16[5,3,192,768]{3,2,1,0:T(8,128)(2,1)}, bf16[5,3,192,768]{3,2,1,0:T(8,128)(2,1)}, u32[]{:S(2)}, u32[]{:S(2)}) collective-permute-start(bf16[5,3,192,768]{3,2,1,0:T(8,128)(2,1)} %own_ref.5), channel_id=1, source_target_pairs={{0,1},{1,0},{2,3},{3,2},{4,5},{5,4},{6,7},{7,6},{8,9},{9,8},{10,11... | collective-permute-start | bytes 13271048 | tf_op jit(solution)/shard_map/ppermute | solution.py:26
  1.2 12.7 %collective-permute-start.1 = (bf16[192,512]{1,0:T(8,128)(2,1)}, bf16[192,512]{1,0:T(8,128)(2,1)}, u32[]{:S(2)}, u32[]{:S(2)}) collective-permute-start(bf16[192,512]{1,0:T(8,128)(2,1)} %refs_0_.3), channel_id=1, source_target_pairs={{0,2},{1,3},{2,0},{3,1},{4,6},{5,7},{6,4},{7,5},{8,10},{9,11},{10,... | collective-permute-start | bytes 589832 | tf_op jit(solution)/shard_map/ppermute | solution.py:31
  3.7 14.6 %collective-permute-start = (bf16[192,512]{1,0:T(8,128)(2,1)}, bf16[192,512]{1,0:T(8,128)(2,1)}, u32[]{:S(2)}, u32[]{:S(2)}) collective-permute-start(bf16[192,512]{1,0:T(8,128)(2,1)} %refs_0_.3), channel_id=1, source_target_pairs={{0,1},{1,0},{2,3},{3,2},{4,5},{5,4},{6,7},{7,6},{8,9},{9,8},{10,11... | collective-permute-start | bytes 589832 | tf_op jit(solution)/shard_map/ppermute | solution.py:26
  5.6 12.7 %all-to-all-start = ((bf16[8,32,128]{2,1,0:T(8,128)(2,1)}), bf16[8,32,128]{2,1,0:T(8,128)(2,1)S(1)}, u32[]{:S(2)}, u32[]{:S(2)}) async-start(bf16[8,32,128]{2,1,0:T(8,128)(2,1)} %bitcast.2), calls=%async_computation | async-start | bytes 131072 | tf_op jit(solution)/shard_map/all_to_all | solution.py:438
  40.0 8.0 %collective-permute-start.9 = (bf16[768,256]{1,0:T(8,128)(2,1)S(1)}, bf16[768,256]{1,0:T(8,128)(2,1)S(1)}, u32[]{:S(2)}, u32[]{:S(2)}) collective-permute-start(bf16[768,256]{1,0:T(8,128)(2,1)S(1)} %shard_map.108.refs_1_), channel_id=1, source_target_pairs={{0,1},{1,0},{2,3},{3,2},{4,5},{5,4},{6,7},{7,6},{8,9},{9,8},{10,11... | collective-permute-start | bytes 1179656 | tf_op jit(solution)/shard_map/ppermute | solution.py:26
  40.9 7.1 %collective-permute-start.7 = (bf16[256,384]{1,0:T(8,128)(2,1)S(1)}, bf16[256,384]{1,0:T(8,128)(2,1)S(1)}, u32[]{:S(2)}, u32[]{:S(2)}) collective-permute-start(bf16[256,384]{1,0:T(8,128)(2,1)S(1)} %get-tuple-element.164), channel_id=1, source_target_pairs={{0,2},{1,3},{2,0},{3,1},{4,6},{5,7},{6,4},{7,5},{8,10},{9,11},{10,... | collective-permute-start | bytes 589832 | tf_op jit(solution)/shard_map/ppermute | solution.py:31
  48.9 7.9 %collective-permute-start.11 = (bf16[768,256]{1,0:T(8,128)(2,1)S(1)}, bf16[768,256]{1,0:T(8,128)(2,1)S(1)}, u32[]{:S(2)}, u32[]{:S(2)}) collective-permute-start(bf16[768,256]{1,0:T(8,128)(2,1)S(1)} %shard_map.110.refs_1_), channel_id=1, source_target_pairs={{0,1},{1,0},{2,3},{3,2},{4,5},{5,4},{6,7},{7,6},{8,9},{9,8},{10,11... | collective-permute-start | bytes 1179656 | tf_op jit(solution)/shard_map/ppermute | solution.py:26
  49.5 7.4 %collective-permute-start.10 = (bf16[256,384]{1,0:T(8,128)(2,1)S(1)}, bf16[256,384]{1,0:T(8,128)(2,1)S(1)}, u32[]{:S(2)}, u32[]{:S(2)}) collective-permute-start(bf16[256,384]{1,0:T(8,128)(2,1)S(1)} %get-tuple-element.174), channel_id=1, source_target_pairs={{0,2},{1,3},{2,0},{3,1},{4,6},{5,7},{6,4},{7,5},{8,10},{9,11},{10,... | collective-permute-start | bytes 589832 | tf_op jit(solution)/shard_map/ppermute | solution.py:31
  59.2 13.9 %collective-permute-start.14 = (bf16[768,256]{1,0:T(8,128)(2,1)}, bf16[768,256]{1,0:T(8,128)(2,1)}, u32[]{:S(2)}, u32[]{:S(2)}) collective-permute-start(bf16[768,256]{1,0:T(8,128)(2,1)} %shard_map.112.refs_1_), channel_id=1, source_target_pairs={{0,1},{1,0},{2,3},{3,2},{4,5},{5,4},{6,7},{7,6},{8,9},{9,8},{10,11... | collective-permute-start | bytes 1179656 | tf_op jit(solution)/shard_map/ppermute | solution.py:26
  62.0 11.1 %all-to-all-start.1 = ((f32[32,1,128]{2,1,0:T(1,128)}), f32[32,1,128]{2,1,0:T(1,128)S(1)}, u32[]{:S(2)}, u32[]{:S(2)}) async-start(f32[32,1,128]{2,1,0:T(1,128)} %bitcast.21), calls=%async_computation.1 | async-start | bytes 32768 | tf_op jit(solution)/shard_map/all_to_all | solution.py:538
  78.4 6.8 %collective-permute-start.15 = (bf16[256,384]{1,0:T(8,128)(2,1)S(1)}, bf16[256,384]{1,0:T(8,128)(2,1)S(1)}, u32[]{:S(2)}, u32[]{:S(2)}) collective-permute-start(bf16[256,384]{1,0:T(8,128)(2,1)S(1)} %bitcast.97), channel_id=1, source_target_pairs={{0,2},{1,3},{2,0},{3,1},{4,6},{5,7},{6,4},{7,5},{8,10},{9,11},{10,... | collective-permute-start | bytes 589832 | tf_op jit(solution)/shard_map/ppermute | solution.py:31
  82.2 13.1 %collective-permute-start.21 = (bf16[192,1152]{1,0:T(8,128)(2,1)S(1)}, bf16[192,1152]{1,0:T(8,128)(2,1)S(1)}, u32[]{:S(2)}, u32[]{:S(2)}) collective-permute-start(bf16[192,1152]{1,0:T(8,128)(2,1)S(1)} %get-tuple-element.209), channel_id=1, source_target_pairs={{0,8},{4,12},{8,0},{12,4},{16,24},{20,28},{24,16},{28,20},{1,9},{5... | collective-permute-start | bytes 1327112 | tf_op jit(solution)/shard_map/ppermute | solution.py:36
  86.3 7.3 %collective-permute-start.18 = (bf16[256,384]{1,0:T(8,128)(2,1)S(1)}, bf16[256,384]{1,0:T(8,128)(2,1)S(1)}, u32[]{:S(2)}, u32[]{:S(2)}) collective-permute-start(bf16[256,384]{1,0:T(8,128)(2,1)S(1)} %bitcast.98), channel_id=1, source_target_pairs={{0,2},{1,3},{2,0},{3,1},{4,6},{5,7},{6,4},{7,5},{8,10},{9,11},{10,... | collective-permute-start | bytes 589832 | tf_op jit(solution)/shard_map/ppermute | solution.py:31
  90.5 13.1 %collective-permute-start.25 = (bf16[192,1152]{1,0:T(8,128)(2,1)S(1)}, bf16[192,1152]{1,0:T(8,128)(2,1)S(1)}, u32[]{:S(2)}, u32[]{:S(2)}) collective-permute-start(bf16[192,1152]{1,0:T(8,128)(2,1)S(1)} %get-tuple-element.222), channel_id=1, source_target_pairs={{0,4},{4,0},{8,12},{12,8},{16,20},{20,16},{24,28},{28,24},{1,5},{5... | collective-permute-start | bytes 1327112 | tf_op jit(solution)/shard_map/ppermute | solution.py:36
  94.7 7.3 %collective-permute-start.20 = (bf16[256,384]{1,0:T(8,128)(2,1)S(1)}, bf16[256,384]{1,0:T(8,128)(2,1)S(1)}, u32[]{:S(2)}, u32[]{:S(2)}) collective-permute-start(bf16[256,384]{1,0:T(8,128)(2,1)S(1)} %bitcast.96), channel_id=1, source_target_pairs={{0,2},{1,3},{2,0},{3,1},{4,6},{5,7},{6,4},{7,5},{8,10},{9,11},{10,... | collective-permute-start | bytes 589832 | tf_op jit(solution)/shard_map/ppermute | solution.py:31
  95.4 13.2 %collective-permute-start.24 = (bf16[96,1152]{1,0:T(8,128)(2,1)S(1)}, bf16[96,1152]{1,0:T(8,128)(2,1)S(1)}, u32[]{:S(2)}, u32[]{:S(2)}) collective-permute-start(bf16[96,1152]{1,0:T(8,128)(2,1)S(1)} %get-tuple-element.221), channel_id=1, source_target_pairs={{0,16},{4,20},{8,24},{12,28},{16,0},{20,4},{24,8},{28,12},{1,17},{... | collective-permute-start | bytes 663560 | tf_op jit(solution)/shard_map/ppermute | solution.py:36
  97.9 21.2 %collective-permute-start.29 = (bf16[192,1152]{1,0:T(8,128)(2,1)S(1)}, bf16[192,1152]{1,0:T(8,128)(2,1)S(1)}, u32[]{:S(2)}, u32[]{:S(2)}) collective-permute-start(bf16[192,1152]{1,0:T(8,128)(2,1)S(1)} %get-tuple-element.233), channel_id=1, source_target_pairs={{0,4},{4,0},{8,12},{12,8},{16,20},{20,16},{24,28},{28,24},{1,5},{5... | collective-permute-start | bytes 1327112 | tf_op jit(solution)/shard_map/ppermute | solution.py:36
  108.7 10.4 %collective-permute-start.28 = (bf16[96,1152]{1,0:T(8,128)(2,1)S(1)}, bf16[96,1152]{1,0:T(8,128)(2,1)S(1)}, u32[]{:S(2)}, u32[]{:S(2)}) collective-permute-start(bf16[96,1152]{1,0:T(8,128)(2,1)S(1)} %get-tuple-element.232), channel_id=1, source_target_pairs={{0,8},{4,12},{8,0},{12,4},{16,24},{20,28},{24,16},{28,20},{1,9},{5... | collective-permute-start | bytes 663560 | tf_op jit(solution)/shard_map/ppermute | solution.py:36
  110.6 16.7 %collective-permute-start.33 = (bf16[192,1152]{1,0:T(8,128)(2,1)S(1)}, bf16[192,1152]{1,0:T(8,128)(2,1)S(1)}, u32[]{:S(2)}, u32[]{:S(2)}) collective-permute-start(bf16[192,1152]{1,0:T(8,128)(2,1)S(1)} %get-tuple-element.248), channel_id=1, source_target_pairs={{0,4},{4,0},{8,12},{12,8},{16,20},{20,16},{24,28},{28,24},{1,5},{5... | collective-permute-start | bytes 1327112 | tf_op jit(solution)/shard_map/ppermute | solution.py:36
  111.3 6.5 %collective-permute-start.23 = (bf16[256,384]{1,0:T(8,128)(2,1)S(1)}, bf16[256,384]{1,0:T(8,128)(2,1)S(1)}, u32[]{:S(2)}, u32[]{:S(2)}) collective-permute-start(bf16[256,384]{1,0:T(8,128)(2,1)S(1)} %bitcast.95), channel_id=1, source_target_pairs={{0,2},{1,3},{2,0},{3,1},{4,6},{5,7},{6,4},{7,5},{8,10},{9,11},{10,... | collective-permute-start | bytes 589832 | tf_op jit(solution)/shard_map/ppermute | solution.py:31
  119.2 8.0 %collective-permute-start.32 = (bf16[96,1152]{1,0:T(8,128)(2,1)S(1)}, bf16[96,1152]{1,0:T(8,128)(2,1)S(1)}, u32[]{:S(2)}, u32[]{:S(2)}) collective-permute-start(bf16[96,1152]{1,0:T(8,128)(2,1)S(1)} %get-tuple-element.247), channel_id=1, source_target_pairs={{0,8},{4,12},{8,0},{12,4},{16,24},{20,28},{24,16},{28,20},{1,9},{5... | collective-permute-start | bytes 663560 | tf_op jit(solution)/shard_map/ppermute | solution.py:36
  128.0 9.2 %collective-permute-start.35 = (bf16[192,128]{1,0:T(8,128)(2,1)S(1)}, bf16[192,128]{1,0:T(8,128)(2,1)S(1)}, u32[]{:S(2)}, u32[]{:S(2)}) collective-permute-start(bf16[192,128]{1,0:T(8,128)(2,1)S(1)} %convert_element_type.95), channel_id=1, source_target_pairs={{0,8},{4,12},{8,0},{12,4},{16,24},{20,28},{24,16},{28,20},{1,9},{5... | collective-permute-start | bytes 147464 | tf_op jit(solution)/shard_map/ppermute | solution.py:36
  129.1 16.0 %collective-permute-start.36 = (bf16[48,1152]{1,0:T(8,128)(2,1)}, bf16[48,1152]{1,0:T(8,128)(2,1)S(1)}, u32[]{:S(2)}, u32[]{:S(2)}) collective-permute-start(bf16[48,1152]{1,0:T(8,128)(2,1)} %get-tuple-element.257), channel_id=1, source_target_pairs={{0,16},{4,20},{8,24},{12,28},{16,0},{20,4},{24,8},{28,12},{1,17},{... | collective-permute-start | bytes 331784 | tf_op jit(solution)/shard_map/ppermute | solution.py:36
  130.2 14.9 %collective-permute-start.39 = (bf16[192,1152]{1,0:T(8,128)(2,1)S(1)}, bf16[192,1152]{1,0:T(8,128)(2,1)S(1)}, u32[]{:S(2)}, u32[]{:S(2)}) collective-permute-start(bf16[192,1152]{1,0:T(8,128)(2,1)S(1)} %get-tuple-element.264), channel_id=1, source_target_pairs={{0,4},{4,0},{8,12},{12,8},{16,20},{20,16},{24,28},{28,24},{1,5},{5... | collective-permute-start | bytes 1327112 | tf_op jit(solution)/shard_map/ppermute | solution.py:36
  131.4 13.7 %collective-permute-start.38 = (bf16[96,1152]{1,0:T(8,128)(2,1)}, bf16[96,1152]{1,0:T(8,128)(2,1)S(1)}, u32[]{:S(2)}, u32[]{:S(2)}) collective-permute-start(bf16[96,1152]{1,0:T(8,128)(2,1)} %get-tuple-element.263), channel_id=1, source_target_pairs={{0,8},{4,12},{8,0},{12,4},{16,24},{20,28},{24,16},{28,20},{1,9},{5... | collective-permute-start | bytes 663560 | tf_op jit(solution)/shard_map/ppermute | solution.py:36
  133.6 11.5 %collective-permute-start.37 = (bf16[48,1152]{1,0:T(8,128)(2,1)}, bf16[48,1152]{1,0:T(8,128)(2,1)S(1)}, u32[]{:S(2)}, u32[]{:S(2)}) collective-permute-start(bf16[48,1152]{1,0:T(8,128)(2,1)} %get-tuple-element.260), channel_id=1, source_target_pairs={{0,16},{4,20},{8,24},{12,28},{16,0},{20,4},{24,8},{28,12},{1,17},{... | collective-permute-start | bytes 331784 | tf_op jit(solution)/shard_map/ppermute | solution.py:36
  137.3 12.6 %all-to-all-start.2 = ((bf16[8,24,512]{2,1,0:T(8,128)(2,1)}), bf16[8,24,512]{2,1,0:T(8,128)(2,1)}, u32[]{:S(2)}, u32[]{:S(2)}) async-start(bf16[8,24,512]{2,1,0:T(8,128)(2,1)} %bitcast.99), calls=%async_computation.2 | async-start | bytes 393216 | tf_op jit(solution)/shard_map/all_to_all | solution.py:638
  142.2 8.2 %collective-permute-start.43 = (bf16[192,128]{1,0:T(8,128)(2,1)S(1)}, bf16[192,128]{1,0:T(8,128)(2,1)}, u32[]{:S(2)}, u32[]{:S(2)}) collective-permute-start(bf16[192,128]{1,0:T(8,128)(2,1)S(1)} %fusion.93), channel_id=1, source_target_pairs={{0,16},{4,20},{8,24},{12,28},{16,0},{20,4},{24,8},{28,12},{1,17},{... | collective-permute-start | bytes 147464 | tf_op jit(solution)/shard_map/ppermute | solution.py:36
  152.1 23.3 %all-to-all-start.3 = ((bf16[8,24,512]{2,1,0:T(8,128)(2,1)}), bf16[8,24,512]{2,1,0:T(8,128)(2,1)S(1)}, u32[]{:S(2)}, u32[]{:S(2)}) async-start(bf16[8,24,512]{2,1,0:T(8,128)(2,1)} %broadcast_in_dim.11), calls=%async_computation.3 | async-start | bytes 393216 | tf_op jit(solution)/shard_map/all_to_all | solution.py:642
  155.8 11.3 %collective-permute-start.40 = (bf16[96,1152]{1,0:T(8,128)(2,1)S(1)}, bf16[96,1152]{1,0:T(8,128)(2,1)S(1)}, u32[]{:S(2)}, u32[]{:S(2)}) collective-permute-start(bf16[96,1152]{1,0:T(8,128)(2,1)S(1)} %get-tuple-element.267), channel_id=1, source_target_pairs={{0,8},{4,12},{8,0},{12,4},{16,24},{20,28},{24,16},{28,20},{1,9},{5... | collective-permute-start | bytes 663560 | tf_op jit(solution)/shard_map/ppermute | solution.py:36
  158.9 12.2 %collective-permute-start.42 = (bf16[48,1152]{1,0:T(8,128)(2,1)S(1)}, bf16[48,1152]{1,0:T(8,128)(2,1)S(1)}, u32[]{:S(2)}, u32[]{:S(2)}) collective-permute-start(bf16[48,1152]{1,0:T(8,128)(2,1)S(1)} %get-tuple-element.273), channel_id=1, source_target_pairs={{0,16},{4,20},{8,24},{12,28},{16,0},{20,4},{24,8},{28,12},{1,17},{... | collective-permute-start | bytes 331784 | tf_op jit(solution)/shard_map/ppermute | solution.py:36
  167.1 6.5 %collective-permute-start.41 = (bf16[48,1152]{1,0:T(8,128)(2,1)S(1)}, bf16[48,1152]{1,0:T(8,128)(2,1)S(1)}, u32[]{:S(2)}, u32[]{:S(2)}) collective-permute-start(bf16[48,1152]{1,0:T(8,128)(2,1)S(1)} %get-tuple-element.269), channel_id=1, source_target_pairs={{0,16},{4,20},{8,24},{12,28},{16,0},{20,4},{24,8},{28,12},{1,17},{... | collective-permute-start | bytes 331784 | tf_op jit(solution)/shard_map/ppermute | solution.py:36
  (69 other events, 408.9 us)

commit v3 on v2

--- a/solution.py
+++ b/solution.py
@@ -9,7 +9,7 @@
 WIN = 16
 CORES = 2
 VMEM = 12 << 20
-DUE = (("middle2", "middle3", "end4"), ("middle3", "middle4", "summed"), ("middle4", "end4", "summed"), ("end4", "summed", "needed"), ("summed", "needed", "needed"))
+DUE = (("middle2", "middle3", "end4"), ("middle3", "middle4", "summed"), ("middle4", "end4", "summed"), ("end4", "summed", "needed"), ("end4", "summed", "needed"))
 POOLED_DUE = ("sent", "summed")
 HIGH_FIRST = (1, 0, 0, 0, 0)
 
@@ -254,8 +254,8 @@
         out_shape=jax.ShapeDtypeStruct((taps, CORES * quarter, channels), bf16),
         in_specs=[
             pl.BlockSpec(memory_space=pltpu.SMEM),
-            pl.BlockSpec(memory_space=pl.ANY),
-            pl.BlockSpec(memory_space=pl.ANY),
+            pl.BlockSpec(memory_space=pltpu.HBM),
+            pl.BlockSpec(memory_space=pltpu.HBM),
         ],
         out_specs=pl.BlockSpec(memory_space=pl.ANY),
         scratch_shapes=[pltpu.SemaphoreType.DMA((CORES,))],

time: 177 us -> 176 us (level)
  waiting for transfers between devices: 56.4 us -> 52.7 us
  matrix products: 9.57 us -> 12.4 us
    all_to_all x1, waiting for transfers between devices: 4.74 us -> 0.01 us  [shards(): stem_blocks = lax.all_to_all(stem_send, 'seq', 0, 0, tiled=True)]
    dot_general x1, matrix products: 2.76 us -> 5.62 us  [shards(): lax.dot_general(jnp.concatenate(pieces(0.5 * loss_slope * pooled_own), ax...]
    unnamed x106 -> x104, local copies, waits for them, and re-layouts: 9.46 us -> 9.47 us
  transfers between devices with their start and end apart: 48 -> 48, of which waited for: 21 -> 18; matrix products, arithmetic and copies ran while one was open for 9% -> 11% of each run, Pallas kernels for 18% -> 18%
where the time goes in v3:
time: 176 us; the launch traced here: 175 us
  waiting for transfers between devices  52.7 us (30%)
  starting transfers between devices  51.6 us (29%)
  Pallas kernels  34.3 us (19%)
  matrix products  12.4 us (7%)
  other arithmetic  11.8 us (7%)
  local copies, waits for them, and re-layouts  10.3 us (6%)
    ppermute x10, waiting for transfers between devices, chip_shift(): lax.ppermute(value, 'ch', [(i, (i + CORES * by) % count) for i in range(c...  26.8 us
    pallas_call x28, Pallas kernels, run(): pl.pallas_call(kernel, out_shape=[jax.ShapeDtypeStruct(shape, kind) for s...  24.1 us
    ppermute x18, starting transfers between devices, seq_swap(): return lax.ppermute(value, 'seq', [(i, i ^ bit) for i in range(count)])  20.8 us
    ppermute x18, waiting for transfers between devices, seq_swap(): return lax.ppermute(value, 'seq', [(i, i ^ bit) for i in range(count)])  15.3 us
    ppermute x10, starting transfers between devices, chip_shift(): lax.ppermute(value, 'ch', [(i, (i + CORES * by) % count) for i in range(c...  9.51 us
    unnamed x104, local copies, waits for them, and re-layouts  9.47 us
    pallas_call x5, Pallas kernels, join_filters(): pl.pallas_call(kernel, out_shape=jax.ShapeDtypeStruct((taps, CORES * quar...  6.6 us
    dot_general x15, matrix products, shards(): lax.dot_general(rolled(active, (tap - 1) * reach[layer]), filters[layer][...  6.13 us
  transfers between devices with their start and end apart: 48, of which 18 were waited for; matrix products, arithmetic and copies ran while one was open for 11% of the time, Pallas kernels for 18%

profile of v3, /device:TPU:0, one launch (start us, length us, event | category | flops | bytes accessed | tf_op | source)
XLA Modules:
  0.0 174.9 jit_solution(8039395784735736603)
XLA Ops:
  1.2 2.6 %collective-permute-start.1 = (bf16[192,512]{1,0:T(8,128)(2,1)}, bf16[192,512]{1,0:T(8,128)(2,1)}, u32[]{:S(2)}, u32[]{:S(2)}) collective-permute-start(bf16[192,512]{1,0:T(8,128)(2,1)} %refs_0_.3), channel_id=1, source_target_pairs={{0,2},{1,3},{2,0},{3,1},{4,6},{5,7},{6,4},{7,5},{8,10},{9,11},{10,... | collective-permute-start | bytes 589832 | tf_op jit(solution)/shard_map/ppermute | solution.py:31
  5.6 5.8 %all-to-all-start = ((bf16[8,32,128]{2,1,0:T(8,128)(2,1)}), bf16[8,32,128]{2,1,0:T(8,128)(2,1)S(1)}, u32[]{:S(2)}, u32[]{:S(2)}) async-start(bf16[8,32,128]{2,1,0:T(8,128)(2,1)} %bitcast.2), calls=%async_computation | async-start | bytes 131072 | tf_op jit(solution)/shard_map/all_to_all | solution.py:438
  11.5 2.1 %fusion.6 = bf16[128,5313]{1,0:T(8,128)(2,1)} fusion(s32[128]{0:T(128)} %param.12), kind=kLoop, calls=%fused_computation.7 | loop fusion | flops 1360128 | bytes 1360640 | tf_op jit(solution)/shard_map/convert_element_type | solution.py:465
  15.3 3.1 %all-to-all-done = bf16[8,32,128]{2,1,0:T(8,128)(2,1)S(1)} async-done(((bf16[8,32,128]{2,1,0:T(8,128)(2,1)}), bf16[8,32,128]{2,1,0:T(8,128)(2,1)S(1)}, u32[]{:S(2)}, u32[]{:S(2)}) %all-to-all-start) | async-done | bytes 65568 | tf_op jit(solution)/shard_map/all_to_all | solution.py:438
  18.4 1.9 %shard_map.103 = (bf16[256,512]{1,0:T(8,128)(2,1)S(1)}, bf16[256,768]{1,0:T(8,128)(2,1)S(1)}, f32[256,384]{1,0:T(8,128)S(1)}) custom-call(s32[1,1]{1,0:T(1,128)} %bitcast.1.strand_ref.refs_0_.refs_1_, s32[1,1]{1,0:T(1,128)} %bitcast.chip_ref.refs_0_, bf16[256,128]{1,0:T(8,128)(2,1)S(1)} %bitcast.85, bf16[192,512]{1,0:T(8,128)(2,1)S(1)} %copy-done.43, ...), custom_call_target="tpu_custom_call" | custom-call | flops 1 | bytes 1 | tf_op jit(solution)/shard_map/pallas_call | solution.py:220
  21.1 2.3 %copy-done.2 = bf16[5,3,192,768]{3,2,1,0:T(8,128)(2,1)S(1)} copy-done((bf16[5,3,192,768]{3,2,1,0:T(8,128)(2,1)S(1)}, bf16[5,3,192,768]{3,2,1,0:T(8,128)(2,1)}, u32[]{:S(2)}) %copy-start.2) | copy-done | bytes 4423704
  29.2 2.6 %collective-permute-done.4 = bf16[256,384]{1,0:T(8,128)(2,1)S(1)} collective-permute-done((bf16[256,384]{1,0:T(8,128)(2,1)S(1)}, bf16[256,384]{1,0:T(8,128)(2,1)S(1)}, u32[]{:S(2)}, u32[]{:S(2)}) %collective-permute-start.4) | collective-permute-done | bytes 196640 | tf_op jit(solution)/shard_map/ppermute | solution.py:31
  36.7 2.1 %collective-permute-done.5 = bf16[256,384]{1,0:T(8,128)(2,1)S(1)} collective-permute-done((bf16[256,384]{1,0:T(8,128)(2,1)S(1)}, bf16[256,384]{1,0:T(8,128)(2,1)S(1)}, u32[]{:S(2)}, u32[]{:S(2)}) %collective-permute-start.5) | collective-permute-done | bytes 196640 | tf_op jit(solution)/shard_map/ppermute | solution.py:31
  43.4 4.6 %collective-permute-done.7 = bf16[256,384]{1,0:T(8,128)(2,1)S(1)} collective-permute-done((bf16[256,384]{1,0:T(8,128)(2,1)S(1)}, bf16[256,384]{1,0:T(8,128)(2,1)S(1)}, u32[]{:S(2)}, u32[]{:S(2)}) %collective-permute-start.7) | collective-permute-done | bytes 196640 | tf_op jit(solution)/shard_map/ppermute | solution.py:31
  52.8 4.1 %collective-permute-done.10 = bf16[256,384]{1,0:T(8,128)(2,1)S(1)} collective-permute-done((bf16[256,384]{1,0:T(8,128)(2,1)S(1)}, bf16[256,384]{1,0:T(8,128)(2,1)S(1)}, u32[]{:S(2)}, u32[]{:S(2)}) %collective-permute-start.10) | collective-permute-done | bytes 196640 | tf_op jit(solution)/shard_map/ppermute | solution.py:31
  62.0 4.1 %all-to-all-start.1 = ((f32[32,1,128]{2,1,0:T(1,128)}), f32[32,1,128]{2,1,0:T(1,128)S(1)}, u32[]{:S(2)}, u32[]{:S(2)}) async-start(f32[32,1,128]{2,1,0:T(1,128)} %bitcast.21), calls=%async_computation.1 | async-start | bytes 32768 | tf_op jit(solution)/shard_map/all_to_all | solution.py:538
  69.0 4.1 %all-to-all-done.1 = f32[32,1,128]{2,1,0:T(1,128)S(1)} async-done(((f32[32,1,128]{2,1,0:T(1,128)}), f32[32,1,128]{2,1,0:T(1,128)S(1)}, u32[]{:S(2)}, u32[]{:S(2)}) %all-to-all-start.1) | async-done | bytes 16416 | tf_op jit(solution)/shard_map/all_to_all | solution.py:538
  80.4 1.8 %shard_map.116 = (f32[192,1152]{1,0:T(8,128)S(1)}, bf16[192,1152]{1,0:T(8,128)(2,1)S(1)}) custom-call(s32[1,1]{1,0:T(1,128)} %bitcast.1.strand_ref.refs_0_.refs_1_, bf16[768,256]{1,0:T(8,128)(2,1)S(1)} %copy-done.30, bf16[256,384]{1,0:T(8,128)(2,1)S(1)} %get-tuple-element.192.refs_2_, bf16[768,256]{1,0:T(8,128)(2,1)S(1)} %collective-permute-done.16.refs_3_, ...), custom_call_target="tpu_custom_call" | custom-call | flops 1 | bytes 1 | tf_op jit(solution)/shard_map/pallas_call | solution.py:79
  82.9 2.4 %collective-permute-done.15 = bf16[256,384]{1,0:T(8,128)(2,1)S(1)} collective-permute-done((bf16[256,384]{1,0:T(8,128)(2,1)S(1)}, bf16[256,384]{1,0:T(8,128)(2,1)S(1)}, u32[]{:S(2)}, u32[]{:S(2)}) %collective-permute-start.15) | collective-permute-done | bytes 196640 | tf_op jit(solution)/shard_map/ppermute | solution.py:31
  87.7 2.9 %shard_map.118 = (f32[192,1152]{1,0:T(8,128)S(1)}, bf16[192,1152]{1,0:T(8,128)(2,1)S(1)}) custom-call(s32[1,1]{1,0:T(1,128)} %bitcast.1.strand_ref.refs_0_.refs_1_, bf16[768,256]{1,0:T(8,128)(2,1)} %shard_map.112.refs_1_, bf16[256,384]{1,0:T(8,128)(2,1)S(1)} %get-tuple-element.199.refs_2_, bf16[768,256]{1,0:T(8,128)(2,1)} %collective-permute-done.14.refs_3_, ...), custom_call_target="tpu_custom_call" | custom-call | flops 1 | bytes 1 | tf_op jit(solution)/shard_map/pallas_call | solution.py:79
  91.2 2.5 %collective-permute-done.18 = bf16[256,384]{1,0:T(8,128)(2,1)S(1)} collective-permute-done((bf16[256,384]{1,0:T(8,128)(2,1)S(1)}, bf16[256,384]{1,0:T(8,128)(2,1)S(1)}, u32[]{:S(2)}, u32[]{:S(2)}) %collective-permute-start.18) | collective-permute-done | bytes 196640 | tf_op jit(solution)/shard_map/ppermute | solution.py:31
  96.1 1.8 %shard_map.120 = (f32[192,1152]{1,0:T(8,128)S(1)}, bf16[192,1152]{1,0:T(8,128)(2,1)S(1)}) custom-call(s32[1,1]{1,0:T(1,128)} %bitcast.1.strand_ref.refs_0_.refs_1_, bf16[768,256]{1,0:T(8,128)(2,1)S(1)} %copy-done.24, bf16[256,384]{1,0:T(8,128)(2,1)S(1)} %get-tuple-element.209.refs_2_, bf16[768,256]{1,0:T(8,128)(2,1)S(1)} %copy-done.40, ...), custom_call_target="tpu_custom_call" | custom-call | flops 1 | bytes 1 | tf_op jit(solution)/shard_map/pallas_call | solution.py:79
  98.6 3.5 %collective-permute-done.20 = bf16[256,384]{1,0:T(8,128)(2,1)S(1)} collective-permute-done((bf16[256,384]{1,0:T(8,128)(2,1)S(1)}, bf16[256,384]{1,0:T(8,128)(2,1)S(1)}, u32[]{:S(2)}, u32[]{:S(2)}) %collective-permute-start.20) | collective-permute-done | bytes 196640 | tf_op jit(solution)/shard_map/ppermute | solution.py:31
  103.6 5.0 %collective-permute-done.24.refs_1_ = bf16[96,1152]{1,0:T(8,128)(2,1)S(1)} collective-permute-done((bf16[96,1152]{1,0:T(8,128)(2,1)S(1)}, bf16[96,1152]{1,0:T(8,128)(2,1)S(1)}, u32[]{:S(2)}, u32[]{:S(2)}) %collective-permute-start.24) | collective-permute-done | bytes 221216 | tf_op jit(solution)/shard_map/ppermute | solution.py:36
  108.8 1.8 %shard_map.123 = (f32[192,1152]{1,0:T(8,128)S(1)}, bf16[192,1152]{1,0:T(8,128)(2,1)S(1)}) custom-call(s32[1,1]{1,0:T(1,128)} %bitcast.1.strand_ref.refs_0_.refs_1_, bf16[768,256]{1,0:T(8,128)(2,1)S(1)} %copy-done.20, bf16[256,384]{1,0:T(8,128)(2,1)S(1)} %get-tuple-element.222.refs_2_, bf16[768,256]{1,0:T(8,128)(2,1)S(1)} %copy-done.38, ...), custom_call_target="tpu_custom_call" | custom-call | flops 1 | bytes 1 | tf_op jit(solution)/shard_map/pallas_call | solution.py:79
  112.7 5.1 %collective-permute-done.23 = bf16[256,384]{1,0:T(8,128)(2,1)S(1)} collective-permute-done((bf16[256,384]{1,0:T(8,128)(2,1)S(1)}, bf16[256,384]{1,0:T(8,128)(2,1)S(1)}, u32[]{:S(2)}, u32[]{:S(2)}) %collective-permute-start.23) | collective-permute-done | bytes 196640 | tf_op jit(solution)/shard_map/ppermute | solution.py:31
  119.3 1.8 %collective-permute-start.35 = (bf16[96,1152]{1,0:T(8,128)(2,1)S(1)}, bf16[96,1152]{1,0:T(8,128)(2,1)S(1)}, u32[]{:S(2)}, u32[]{:S(2)}) collective-permute-start(bf16[96,1152]{1,0:T(8,128)(2,1)S(1)} %get-tuple-element.250), channel_id=1, source_target_pairs={{0,8},{4,12},{8,0},{12,4},{16,24},{20,28},{24,16},{28,20},{1,9},{5... | collective-permute-start | bytes 663560 | tf_op jit(solution)/shard_map/ppermute | solution.py:36
  125.4 2.6 %shard_map.126 = (f32[192,1152]{1,0:T(8,128)S(1)}, bf16[192,1152]{1,0:T(8,128)(2,1)}) custom-call(s32[1,1]{1,0:T(1,128)} %bitcast.1.strand_ref.refs_0_.refs_1_, bf16[768,256]{1,0:T(8,128)(2,1)S(1)} %copy-done.18, bf16[256,384]{1,0:T(8,128)(2,1)S(1)} %get-tuple-element.233.refs_2_, bf16[768,256]{1,0:T(8,128)(2,1)S(1)} %copy-done.36, ...), custom_call_target="tpu_custom_call" | custom-call | flops 1 | bytes 1 | tf_op jit(solution)/shard_map/pallas_call | solution.py:79
  131.1 2.4 %collective-permute-start.40 = (bf16[48,1152]{1,0:T(8,128)(2,1)}, bf16[48,1152]{1,0:T(8,128)(2,1)S(1)}, u32[]{:S(2)}, u32[]{:S(2)}) collective-permute-start(bf16[48,1152]{1,0:T(8,128)(2,1)} %get-tuple-element.267), channel_id=1, source_target_pairs={{0,16},{4,20},{8,24},{12,28},{16,0},{20,4},{24,8},{28,12},{1,17},{... | collective-permute-start | bytes 331784 | tf_op jit(solution)/shard_map/ppermute | solution.py:36
  136.8 4.0 %all-to-all-start.2 = ((bf16[8,24,512]{2,1,0:T(8,128)(2,1)}), bf16[8,24,512]{2,1,0:T(8,128)(2,1)}, u32[]{:S(2)}, u32[]{:S(2)}) async-start(bf16[8,24,512]{2,1,0:T(8,128)(2,1)} %bitcast.36), calls=%async_computation.2 | async-start | bytes 393216 | tf_op jit(solution)/shard_map/all_to_all | solution.py:638
  140.8 2.9 %collective-permute-start.43 = (bf16[192,128]{1,0:T(8,128)(2,1)S(1)}, bf16[192,128]{1,0:T(8,128)(2,1)}, u32[]{:S(2)}, u32[]{:S(2)}) collective-permute-start(bf16[192,128]{1,0:T(8,128)(2,1)S(1)} %fusion.93), channel_id=1, source_target_pairs={{0,16},{4,20},{8,24},{12,28},{16,0},{20,4},{24,8},{28,12},{1,17},{... | collective-permute-start | bytes 147464 | tf_op jit(solution)/shard_map/ppermute | solution.py:36
  145.3 8.4 %collective-permute-done.32.refs_1_ = bf16[96,1152]{1,0:T(8,128)(2,1)S(1)} collective-permute-done((bf16[96,1152]{1,0:T(8,128)(2,1)S(1)}, bf16[96,1152]{1,0:T(8,128)(2,1)S(1)}, u32[]{:S(2)}, u32[]{:S(2)}) %collective-permute-start.32) | collective-permute-done | bytes 221216 | tf_op jit(solution)/shard_map/ppermute | solution.py:36
  155.7 4.7 %all-to-all-start.3 = ((bf16[8,24,512]{2,1,0:T(8,128)(2,1)}), bf16[8,24,512]{2,1,0:T(8,128)(2,1)}, u32[]{:S(2)}, u32[]{:S(2)}) async-start(bf16[8,24,512]{2,1,0:T(8,128)(2,1)} %broadcast_in_dim.11), calls=%async_computation.3 | async-start | bytes 393216 | tf_op jit(solution)/shard_map/all_to_all | solution.py:642
  161.4 3.0 %collective-permute-start.42 = (bf16[48,1152]{1,0:T(8,128)(2,1)S(1)}, bf16[48,1152]{1,0:T(8,128)(2,1)S(1)}, u32[]{:S(2)}, u32[]{:S(2)}) collective-permute-start(bf16[48,1152]{1,0:T(8,128)(2,1)S(1)} %get-tuple-element.271), channel_id=1, source_target_pairs={{0,16},{4,20},{8,24},{12,28},{16,0},{20,4},{24,8},{28,12},{1,17},{... | collective-permute-start | bytes 331784 | tf_op jit(solution)/shard_map/ppermute | solution.py:36
  164.4 5.6 %fusion = f32[192,5313]{1,0:T(8,128)} fusion(bf16[128,5313]{1,0:T(8,128)(2,1)} %fusion.6, bf16[192,128]{1,0:T(8,128)(2,1)S(1)} %get-tuple-element.307, bf16[192,128]{1,0:T(8,128)(2,1)S(1)} %get-tuple-element.306, bf16[192,128]{1,0:T(8,128)(2,1)S(1)} %get-tuple-element.284), kind=kOutput, calls=%fused_computation | convolution fusion | flops 796117248 | bytes 5587968 | tf_op jit(solution)/shard_map/dot_general | solution.py:651
  171.4 1.8 %shard_map.136 = f32[5,3,192,96]{3,2,1,0:T(8,128)} custom-call(f32[48,1152]{1,0:T(8,128)S(1)} %get-tuple-element.241.refs_0_, bf16[48,1152]{1,0:T(8,128)(2,1)S(1)} %collective-permute-done.33.refs_1_, f32[48,1152]{1,0:T(8,128)S(1)} %get-tuple-element.270.refs_2_, bf16[48,1152]{1,0:T(8,128)(2,1)S(1)} %collective-permute-done.42.refs_3_, ...), custom_call_target="tpu_custom_call" | custom-call | flops 1 | bytes 1 | tf_op jit(solution)/shard_map/pallas_call | solution.py:402
  173.1 1.7 bitcast_convert_fusion
  (254 shorter events, 68.3 us)
Async XLA Ops:
  0.6 20.4 %collective-permute-start.3 = (bf16[5,3,192,768]{3,2,1,0:T(8,128)(2,1)}, bf16[5,3,192,768]{3,2,1,0:T(8,128)(2,1)}, u32[]{:S(2)}, u32[]{:S(2)}) collective-permute-start(bf16[5,3,192,768]{3,2,1,0:T(8,128)(2,1)} %own_ref.5), channel_id=1, source_target_pairs={{0,1},{1,0},{2,3},{3,2},{4,5},{5,4},{6,7},{7,6},{8,9},{9,8},{10,11... | collective-permute-start | bytes 13271048 | tf_op jit(solution)/shard_map/ppermute | solution.py:26
  1.2 12.7 %collective-permute-start.1 = (bf16[192,512]{1,0:T(8,128)(2,1)}, bf16[192,512]{1,0:T(8,128)(2,1)}, u32[]{:S(2)}, u32[]{:S(2)}) collective-permute-start(bf16[192,512]{1,0:T(8,128)(2,1)} %refs_0_.3), channel_id=1, source_target_pairs={{0,2},{1,3},{2,0},{3,1},{4,6},{5,7},{6,4},{7,5},{8,10},{9,11},{10,... | collective-permute-start | bytes 589832 | tf_op jit(solution)/shard_map/ppermute | solution.py:31
  3.7 14.6 %collective-permute-start = (bf16[192,512]{1,0:T(8,128)(2,1)}, bf16[192,512]{1,0:T(8,128)(2,1)}, u32[]{:S(2)}, u32[]{:S(2)}) collective-permute-start(bf16[192,512]{1,0:T(8,128)(2,1)} %refs_0_.3), channel_id=1, source_target_pairs={{0,1},{1,0},{2,3},{3,2},{4,5},{5,4},{6,7},{7,6},{8,9},{9,8},{10,11... | collective-permute-start | bytes 589832 | tf_op jit(solution)/shard_map/ppermute | solution.py:26
  5.6 12.7 %all-to-all-start = ((bf16[8,32,128]{2,1,0:T(8,128)(2,1)}), bf16[8,32,128]{2,1,0:T(8,128)(2,1)S(1)}, u32[]{:S(2)}, u32[]{:S(2)}) async-start(bf16[8,32,128]{2,1,0:T(8,128)(2,1)} %bitcast.2), calls=%async_computation | async-start | bytes 131072 | tf_op jit(solution)/shard_map/all_to_all | solution.py:438
  40.0 8.0 %collective-permute-start.9 = (bf16[768,256]{1,0:T(8,128)(2,1)S(1)}, bf16[768,256]{1,0:T(8,128)(2,1)S(1)}, u32[]{:S(2)}, u32[]{:S(2)}) collective-permute-start(bf16[768,256]{1,0:T(8,128)(2,1)S(1)} %shard_map.108.refs_1_), channel_id=1, source_target_pairs={{0,1},{1,0},{2,3},{3,2},{4,5},{5,4},{6,7},{7,6},{8,9},{9,8},{10,11... | collective-permute-start | bytes 1179656 | tf_op jit(solution)/shard_map/ppermute | solution.py:26
  40.9 7.1 %collective-permute-start.7 = (bf16[256,384]{1,0:T(8,128)(2,1)S(1)}, bf16[256,384]{1,0:T(8,128)(2,1)S(1)}, u32[]{:S(2)}, u32[]{:S(2)}) collective-permute-start(bf16[256,384]{1,0:T(8,128)(2,1)S(1)} %get-tuple-element.163), channel_id=1, source_target_pairs={{0,2},{1,3},{2,0},{3,1},{4,6},{5,7},{6,4},{7,5},{8,10},{9,11},{10,... | collective-permute-start | bytes 589832 | tf_op jit(solution)/shard_map/ppermute | solution.py:31
  48.9 7.9 %collective-permute-start.11 = (bf16[768,256]{1,0:T(8,128)(2,1)S(1)}, bf16[768,256]{1,0:T(8,128)(2,1)S(1)}, u32[]{:S(2)}, u32[]{:S(2)}) collective-permute-start(bf16[768,256]{1,0:T(8,128)(2,1)S(1)} %shard_map.110.refs_1_), channel_id=1, source_target_pairs={{0,1},{1,0},{2,3},{3,2},{4,5},{5,4},{6,7},{7,6},{8,9},{9,8},{10,11... | collective-permute-start | bytes 1179656 | tf_op jit(solution)/shard_map/ppermute | solution.py:26
  49.5 7.4 %collective-permute-start.10 = (bf16[256,384]{1,0:T(8,128)(2,1)S(1)}, bf16[256,384]{1,0:T(8,128)(2,1)S(1)}, u32[]{:S(2)}, u32[]{:S(2)}) collective-permute-start(bf16[256,384]{1,0:T(8,128)(2,1)S(1)} %get-tuple-element.173), channel_id=1, source_target_pairs={{0,2},{1,3},{2,0},{3,1},{4,6},{5,7},{6,4},{7,5},{8,10},{9,11},{10,... | collective-permute-start | bytes 589832 | tf_op jit(solution)/shard_map/ppermute | solution.py:31
  59.2 13.9 %collective-permute-start.14 = (bf16[768,256]{1,0:T(8,128)(2,1)}, bf16[768,256]{1,0:T(8,128)(2,1)}, u32[]{:S(2)}, u32[]{:S(2)}) collective-permute-start(bf16[768,256]{1,0:T(8,128)(2,1)} %shard_map.112.refs_1_), channel_id=1, source_target_pairs={{0,1},{1,0},{2,3},{3,2},{4,5},{5,4},{6,7},{7,6},{8,9},{9,8},{10,11... | collective-permute-start | bytes 1179656 | tf_op jit(solution)/shard_map/ppermute | solution.py:26
  62.0 11.1 %all-to-all-start.1 = ((f32[32,1,128]{2,1,0:T(1,128)}), f32[32,1,128]{2,1,0:T(1,128)S(1)}, u32[]{:S(2)}, u32[]{:S(2)}) async-start(f32[32,1,128]{2,1,0:T(1,128)} %bitcast.21), calls=%async_computation.1 | async-start | bytes 32768 | tf_op jit(solution)/shard_map/all_to_all | solution.py:538
  78.4 6.8 %collective-permute-start.15 = (bf16[256,384]{1,0:T(8,128)(2,1)S(1)}, bf16[256,384]{1,0:T(8,128)(2,1)S(1)}, u32[]{:S(2)}, u32[]{:S(2)}) collective-permute-start(bf16[256,384]{1,0:T(8,128)(2,1)S(1)} %bitcast.97), channel_id=1, source_target_pairs={{0,2},{1,3},{2,0},{3,1},{4,6},{5,7},{6,4},{7,5},{8,10},{9,11},{10,... | collective-permute-start | bytes 589832 | tf_op jit(solution)/shard_map/ppermute | solution.py:31
  82.2 13.1 %collective-permute-start.21 = (bf16[192,1152]{1,0:T(8,128)(2,1)S(1)}, bf16[192,1152]{1,0:T(8,128)(2,1)S(1)}, u32[]{:S(2)}, u32[]{:S(2)}) collective-permute-start(bf16[192,1152]{1,0:T(8,128)(2,1)S(1)} %get-tuple-element.208), channel_id=1, source_target_pairs={{0,8},{4,12},{8,0},{12,4},{16,24},{20,28},{24,16},{28,20},{1,9},{5... | collective-permute-start | bytes 1327112 | tf_op jit(solution)/shard_map/ppermute | solution.py:36
  86.3 7.3 %collective-permute-start.18 = (bf16[256,384]{1,0:T(8,128)(2,1)S(1)}, bf16[256,384]{1,0:T(8,128)(2,1)S(1)}, u32[]{:S(2)}, u32[]{:S(2)}) collective-permute-start(bf16[256,384]{1,0:T(8,128)(2,1)S(1)} %bitcast.98), channel_id=1, source_target_pairs={{0,2},{1,3},{2,0},{3,1},{4,6},{5,7},{6,4},{7,5},{8,10},{9,11},{10,... | collective-permute-start | bytes 589832 | tf_op jit(solution)/shard_map/ppermute | solution.py:31
  90.6 13.1 %collective-permute-start.25 = (bf16[192,1152]{1,0:T(8,128)(2,1)S(1)}, bf16[192,1152]{1,0:T(8,128)(2,1)S(1)}, u32[]{:S(2)}, u32[]{:S(2)}) collective-permute-start(bf16[192,1152]{1,0:T(8,128)(2,1)S(1)} %get-tuple-element.221), channel_id=1, source_target_pairs={{0,4},{4,0},{8,12},{12,8},{16,20},{20,16},{24,28},{28,24},{1,5},{5... | collective-permute-start | bytes 1327112 | tf_op jit(solution)/shard_map/ppermute | solution.py:36
  94.7 7.3 %collective-permute-start.20 = (bf16[256,384]{1,0:T(8,128)(2,1)S(1)}, bf16[256,384]{1,0:T(8,128)(2,1)S(1)}, u32[]{:S(2)}, u32[]{:S(2)}) collective-permute-start(bf16[256,384]{1,0:T(8,128)(2,1)S(1)} %bitcast.96), channel_id=1, source_target_pairs={{0,2},{1,3},{2,0},{3,1},{4,6},{5,7},{6,4},{7,5},{8,10},{9,11},{10,... | collective-permute-start | bytes 589832 | tf_op jit(solution)/shard_map/ppermute | solution.py:31
  95.4 13.2 %collective-permute-start.24 = (bf16[96,1152]{1,0:T(8,128)(2,1)S(1)}, bf16[96,1152]{1,0:T(8,128)(2,1)S(1)}, u32[]{:S(2)}, u32[]{:S(2)}) collective-permute-start(bf16[96,1152]{1,0:T(8,128)(2,1)S(1)} %get-tuple-element.220), channel_id=1, source_target_pairs={{0,16},{4,20},{8,24},{12,28},{16,0},{20,4},{24,8},{28,12},{1,17},{... | collective-permute-start | bytes 663560 | tf_op jit(solution)/shard_map/ppermute | solution.py:36
  97.9 21.2 %collective-permute-start.29 = (bf16[192,1152]{1,0:T(8,128)(2,1)S(1)}, bf16[192,1152]{1,0:T(8,128)(2,1)S(1)}, u32[]{:S(2)}, u32[]{:S(2)}) collective-permute-start(bf16[192,1152]{1,0:T(8,128)(2,1)S(1)} %get-tuple-element.232), channel_id=1, source_target_pairs={{0,4},{4,0},{8,12},{12,8},{16,20},{20,16},{24,28},{28,24},{1,5},{5... | collective-permute-start | bytes 1327112 | tf_op jit(solution)/shard_map/ppermute | solution.py:36
  108.7 10.4 %collective-permute-start.28 = (bf16[96,1152]{1,0:T(8,128)(2,1)S(1)}, bf16[96,1152]{1,0:T(8,128)(2,1)S(1)}, u32[]{:S(2)}, u32[]{:S(2)}) collective-permute-start(bf16[96,1152]{1,0:T(8,128)(2,1)S(1)} %get-tuple-element.231), channel_id=1, source_target_pairs={{0,8},{4,12},{8,0},{12,4},{16,24},{20,28},{24,16},{28,20},{1,9},{5... | collective-permute-start | bytes 663560 | tf_op jit(solution)/shard_map/ppermute | solution.py:36
  110.6 17.4 %collective-permute-start.36 = (bf16[192,1152]{1,0:T(8,128)(2,1)S(1)}, bf16[192,1152]{1,0:T(8,128)(2,1)S(1)}, u32[]{:S(2)}, u32[]{:S(2)}) collective-permute-start(bf16[192,1152]{1,0:T(8,128)(2,1)S(1)} %get-tuple-element.251), channel_id=1, source_target_pairs={{0,4},{4,0},{8,12},{12,8},{16,20},{20,16},{24,28},{28,24},{1,5},{5... | collective-permute-start | bytes 1327112 | tf_op jit(solution)/shard_map/ppermute | solution.py:36
  119.3 8.8 %collective-permute-start.35 = (bf16[96,1152]{1,0:T(8,128)(2,1)S(1)}, bf16[96,1152]{1,0:T(8,128)(2,1)S(1)}, u32[]{:S(2)}, u32[]{:S(2)}) collective-permute-start(bf16[96,1152]{1,0:T(8,128)(2,1)S(1)} %get-tuple-element.250), channel_id=1, source_target_pairs={{0,8},{4,12},{8,0},{12,4},{16,24},{20,28},{24,16},{28,20},{1,9},{5... | collective-permute-start | bytes 663560 | tf_op jit(solution)/shard_map/ppermute | solution.py:36
  121.0 7.0 %collective-permute-start.27 = (bf16[256,384]{1,0:T(8,128)(2,1)S(1)}, bf16[256,384]{1,0:T(8,128)(2,1)S(1)}, u32[]{:S(2)}, u32[]{:S(2)}) collective-permute-start(bf16[256,384]{1,0:T(8,128)(2,1)S(1)} %bitcast.94), channel_id=1, source_target_pairs={{0,2},{1,3},{2,0},{3,1},{4,6},{5,7},{6,4},{7,5},{8,10},{9,11},{10,... | collective-permute-start | bytes 589832 | tf_op jit(solution)/shard_map/ppermute | solution.py:31
  128.8 7.9 %collective-permute-start.38 = (bf16[192,128]{1,0:T(8,128)(2,1)S(1)}, bf16[192,128]{1,0:T(8,128)(2,1)S(1)}, u32[]{:S(2)}, u32[]{:S(2)}) collective-permute-start(bf16[192,128]{1,0:T(8,128)(2,1)S(1)} %convert_element_type.95), channel_id=1, source_target_pairs={{0,8},{4,12},{8,0},{12,4},{16,24},{20,28},{24,16},{28,20},{1,9},{5... | collective-permute-start | bytes 147464 | tf_op jit(solution)/shard_map/ppermute | solution.py:36
  129.3 24.7 %collective-permute-start.39 = (bf16[48,1152]{1,0:T(8,128)(2,1)S(1)}, bf16[48,1152]{1,0:T(8,128)(2,1)S(1)}, u32[]{:S(2)}, u32[]{:S(2)}) collective-permute-start(bf16[48,1152]{1,0:T(8,128)(2,1)S(1)} %get-tuple-element.264), channel_id=1, source_target_pairs={{0,16},{4,20},{8,24},{12,28},{16,0},{20,4},{24,8},{28,12},{1,17},{... | collective-permute-start | bytes 331784 | tf_op jit(solution)/shard_map/ppermute | solution.py:36
  129.6 14.1 %collective-permute-start.31 = (bf16[192,1152]{1,0:T(8,128)(2,1)}, bf16[192,1152]{1,0:T(8,128)(2,1)S(1)}, u32[]{:S(2)}, u32[]{:S(2)}) collective-permute-start(bf16[192,1152]{1,0:T(8,128)(2,1)} %get-tuple-element.238), channel_id=1, source_target_pairs={{0,4},{4,0},{8,12},{12,8},{16,20},{20,16},{24,28},{28,24},{1,5},{5... | collective-permute-start | bytes 1327112 | tf_op jit(solution)/shard_map/ppermute | solution.py:36
  131.1 22.9 %collective-permute-start.40 = (bf16[48,1152]{1,0:T(8,128)(2,1)}, bf16[48,1152]{1,0:T(8,128)(2,1)S(1)}, u32[]{:S(2)}, u32[]{:S(2)}) collective-permute-start(bf16[48,1152]{1,0:T(8,128)(2,1)} %get-tuple-element.267), channel_id=1, source_target_pairs={{0,16},{4,20},{8,24},{12,28},{16,0},{20,4},{24,8},{28,12},{1,17},{... | collective-permute-start | bytes 331784 | tf_op jit(solution)/shard_map/ppermute | solution.py:36
  134.3 19.7 %collective-permute-start.41 = (bf16[96,1152]{1,0:T(8,128)(2,1)}, bf16[96,1152]{1,0:T(8,128)(2,1)S(1)}, u32[]{:S(2)}, u32[]{:S(2)}) collective-permute-start(bf16[96,1152]{1,0:T(8,128)(2,1)} %get-tuple-element.268), channel_id=1, source_target_pairs={{0,8},{4,12},{8,0},{12,4},{16,24},{20,28},{24,16},{28,20},{1,9},{5... | collective-permute-start | bytes 663560 | tf_op jit(solution)/shard_map/ppermute | solution.py:36
  136.8 17.3 %all-to-all-start.2 = ((bf16[8,24,512]{2,1,0:T(8,128)(2,1)}), bf16[8,24,512]{2,1,0:T(8,128)(2,1)}, u32[]{:S(2)}, u32[]{:S(2)}) async-start(bf16[8,24,512]{2,1,0:T(8,128)(2,1)} %bitcast.36), calls=%async_computation.2 | async-start | bytes 393216 | tf_op jit(solution)/shard_map/all_to_all | solution.py:638
  140.8 13.2 %collective-permute-start.43 = (bf16[192,128]{1,0:T(8,128)(2,1)S(1)}, bf16[192,128]{1,0:T(8,128)(2,1)}, u32[]{:S(2)}, u32[]{:S(2)}) collective-permute-start(bf16[192,128]{1,0:T(8,128)(2,1)S(1)} %fusion.93), channel_id=1, source_target_pairs={{0,16},{4,20},{8,24},{12,28},{16,0},{20,4},{24,8},{28,12},{1,17},{... | collective-permute-start | bytes 147464 | tf_op jit(solution)/shard_map/ppermute | solution.py:36
  143.8 10.0 %collective-permute-start.32 = (bf16[96,1152]{1,0:T(8,128)(2,1)S(1)}, bf16[96,1152]{1,0:T(8,128)(2,1)S(1)}, u32[]{:S(2)}, u32[]{:S(2)}) collective-permute-start(bf16[96,1152]{1,0:T(8,128)(2,1)S(1)} %get-tuple-element.240), channel_id=1, source_target_pairs={{0,8},{4,12},{8,0},{12,4},{16,24},{20,28},{24,16},{28,20},{1,9},{5... | collective-permute-start | bytes 663560 | tf_op jit(solution)/shard_map/ppermute | solution.py:36
  153.8 16.2 %collective-permute-start.33 = (bf16[48,1152]{1,0:T(8,128)(2,1)S(1)}, bf16[48,1152]{1,0:T(8,128)(2,1)S(1)}, u32[]{:S(2)}, u32[]{:S(2)}) collective-permute-start(bf16[48,1152]{1,0:T(8,128)(2,1)S(1)} %get-tuple-element.242), channel_id=1, source_target_pairs={{0,16},{4,20},{8,24},{12,28},{16,0},{20,4},{24,8},{28,12},{1,17},{... | collective-permute-start | bytes 331784 | tf_op jit(solution)/shard_map/ppermute | solution.py:36
  155.7 17.4 %all-to-all-start.3 = ((bf16[8,24,512]{2,1,0:T(8,128)(2,1)}), bf16[8,24,512]{2,1,0:T(8,128)(2,1)}, u32[]{:S(2)}, u32[]{:S(2)}) async-start(bf16[8,24,512]{2,1,0:T(8,128)(2,1)} %broadcast_in_dim.11), calls=%async_computation.3 | async-start | bytes 393216 | tf_op jit(solution)/shard_map/all_to_all | solution.py:642
  161.4 9.9 %collective-permute-start.42 = (bf16[48,1152]{1,0:T(8,128)(2,1)S(1)}, bf16[48,1152]{1,0:T(8,128)(2,1)S(1)}, u32[]{:S(2)}, u32[]{:S(2)}) collective-permute-start(bf16[48,1152]{1,0:T(8,128)(2,1)S(1)} %get-tuple-element.271), channel_id=1, source_target_pairs={{0,16},{4,20},{8,24},{12,28},{16,0},{20,4},{24,8},{28,12},{1,17},{... | collective-permute-start | bytes 331784 | tf_op jit(solution)/shard_map/ppermute | solution.py:36
  (68 other events, 398.7 us)

commit v4 on v3

--- a/solution.py
+++ b/solution.py
@@ -9,7 +9,7 @@
 WIN = 16
 CORES = 2
 VMEM = 12 << 20
-DUE = (("middle2", "middle3", "end4"), ("middle3", "middle4", "summed"), ("middle4", "end4", "summed"), ("end4", "summed", "needed"), ("end4", "summed", "needed"))
+DUE = (("middle2", "middle3", "end4"), ("middle3", "middle4", "summed"), ("middle4", "end4", "summed"), ("end4", "summed", "needed"), ("end4", "sent", "needed"))
 POOLED_DUE = ("sent", "summed")
 HIGH_FIRST = (1, 0, 0, 0, 0)
 
@@ -154,7 +154,10 @@
 def loss_body(reach, chips, quarter):
     back = back_body(reach, chips, quarter, True)
 
-    def body(roll, chip, strand, scores, targets, counts, member, columns, taps):
+    def body(roll, chip, strand, scores, facts, packed, taps):
+        targets, counts = facts[:1], facts[1:]
+        rows = packed.shape[0] - CORES * quarter
+        member, columns = packed[:rows], packed[rows:]
         score = jnp.sum(scores, axis=0, keepdims=True)
         slope = (jnp.exp(score) - targets) / counts
         grad = sum(
@@ -525,6 +528,9 @@
                 [choose((chip - p) % chips, parts) for p in range(chips)], axis=1
             )
 
+    facts = jnp.stack([targets, counts])
+    packed = jnp.concatenate([member, half_columns])
+    stream, facts, packed = tied(stream, facts, packed)
     windows = window_start.shape[0]
     everyone = seqs * chips * CORES
     partial_score, pooled_own, pooled_sent = run(
@@ -586,10 +592,8 @@
                 chip_word,
                 strand_word,
                 scores[:, 0],
-                targets[None],
-                counts[None],
-                member,
-                half_columns,
+                facts,
+                packed,
                 filters[layer],
                 inside=aligned,
             )

time: 176 us -> 176 us (level)
    unnamed x104 -> x102, local copies, waits for them, and re-layouts: 9.47 us -> 8.58 us
where the time goes in v4:
time: 176 us; the launch traced here: 175 us
  starting transfers between devices  53 us (30%)
  waiting for transfers between devices  51.5 us (29%)
  Pallas kernels  34.3 us (19%)
  other arithmetic  12.4 us (7%)
  matrix products  12.4 us (7%)
  local copies, waits for them, and re-layouts  9.37 us (5%)
    ppermute x10, waiting for transfers between devices, chip_shift(): lax.ppermute(value, 'ch', [(i, (i + CORES * by) % count) for i in range(c...  26.4 us
    pallas_call x28, Pallas kernels, run(): pl.pallas_call(kernel, out_shape=[jax.ShapeDtypeStruct(shape, kind) for s...  24.1 us
    ppermute x18, starting transfers between devices, seq_swap(): return lax.ppermute(value, 'seq', [(i, i ^ bit) for i in range(count)])  22.5 us
    ppermute x18, waiting for transfers between devices, seq_swap(): return lax.ppermute(value, 'seq', [(i, i ^ bit) for i in range(count)])  15.3 us
    ppermute x10, starting transfers between devices, chip_shift(): lax.ppermute(value, 'ch', [(i, (i + CORES * by) % count) for i in range(c...  9.5 us
    unnamed x102, local copies, waits for them, and re-layouts  8.58 us
    pallas_call x5, Pallas kernels, join_filters(): pl.pallas_call(kernel, out_shape=jax.ShapeDtypeStruct((taps, CORES * quar...  6.6 us
    dot_general x15, matrix products, shards(): lax.dot_general(rolled(active, (tap - 1) * reach[layer]), filters[layer][...  6.13 us
  transfers between devices with their start and end apart: 48, of which 18 were waited for; matrix products, arithmetic and copies ran while one was open for 11% of the time, Pallas kernels for 18%

profile of v4, /device:TPU:0, one launch (start us, length us, event | category | flops | bytes accessed | tf_op | source)
XLA Modules:
  0.0 174.7 jit_solution(3967714434614685140)
XLA Ops:
  1.2 2.6 %collective-permute-start.1 = (bf16[192,512]{1,0:T(8,128)(2,1)}, bf16[192,512]{1,0:T(8,128)(2,1)}, u32[]{:S(2)}, u32[]{:S(2)}) collective-permute-start(bf16[192,512]{1,0:T(8,128)(2,1)} %refs_0_.3), channel_id=1, source_target_pairs={{0,2},{1,3},{2,0},{3,1},{4,6},{5,7},{6,4},{7,5},{8,10},{9,11},{10,... | collective-permute-start | bytes 589832 | tf_op jit(solution)/shard_map/ppermute | solution.py:31
  5.6 5.8 %all-to-all-start = ((bf16[8,32,128]{2,1,0:T(8,128)(2,1)}), bf16[8,32,128]{2,1,0:T(8,128)(2,1)S(1)}, u32[]{:S(2)}, u32[]{:S(2)}) async-start(bf16[8,32,128]{2,1,0:T(8,128)(2,1)} %bitcast.2), calls=%async_computation | async-start | bytes 131072 | tf_op jit(solution)/shard_map/all_to_all | solution.py:441
  16.1 2.2 %all-to-all-done = bf16[8,32,128]{2,1,0:T(8,128)(2,1)S(1)} async-done(((bf16[8,32,128]{2,1,0:T(8,128)(2,1)}), bf16[8,32,128]{2,1,0:T(8,128)(2,1)S(1)}, u32[]{:S(2)}, u32[]{:S(2)}) %all-to-all-start) | async-done | bytes 65568 | tf_op jit(solution)/shard_map/all_to_all | solution.py:441
  18.4 1.9 %shard_map.103 = (bf16[256,512]{1,0:T(8,128)(2,1)S(1)}, bf16[256,768]{1,0:T(8,128)(2,1)S(1)}, f32[256,384]{1,0:T(8,128)S(1)}) custom-call(s32[1,1]{1,0:T(1,128)} %bitcast.1.strand_ref.refs_0_.refs_1_, s32[1,1]{1,0:T(1,128)} %bitcast.chip_ref.refs_0_, bf16[256,128]{1,0:T(8,128)(2,1)S(1)} %bitcast.85, bf16[192,512]{1,0:T(8,128)(2,1)S(1)} %copy-done.40, ...), custom_call_target="tpu_custom_call" | custom-call | flops 1 | bytes 1 | tf_op jit(solution)/shard_map/pallas_call | solution.py:223
  21.1 2.3 %copy-done.2 = bf16[5,3,192,768]{3,2,1,0:T(8,128)(2,1)S(1)} copy-done((bf16[5,3,192,768]{3,2,1,0:T(8,128)(2,1)S(1)}, bf16[5,3,192,768]{3,2,1,0:T(8,128)(2,1)}, u32[]{:S(2)}) %copy-start.2) | copy-done | bytes 4423704
  29.2 2.7 %collective-permute-done.4 = bf16[256,384]{1,0:T(8,128)(2,1)S(1)} collective-permute-done((bf16[256,384]{1,0:T(8,128)(2,1)S(1)}, bf16[256,384]{1,0:T(8,128)(2,1)S(1)}, u32[]{:S(2)}, u32[]{:S(2)}) %collective-permute-start.4) | collective-permute-done | bytes 196640 | tf_op jit(solution)/shard_map/ppermute | solution.py:31
  36.8 2.1 %collective-permute-done.5 = bf16[256,384]{1,0:T(8,128)(2,1)S(1)} collective-permute-done((bf16[256,384]{1,0:T(8,128)(2,1)S(1)}, bf16[256,384]{1,0:T(8,128)(2,1)S(1)}, u32[]{:S(2)}, u32[]{:S(2)}) %collective-permute-start.5) | collective-permute-done | bytes 196640 | tf_op jit(solution)/shard_map/ppermute | solution.py:31
  43.5 4.6 %collective-permute-done.7 = bf16[256,384]{1,0:T(8,128)(2,1)S(1)} collective-permute-done((bf16[256,384]{1,0:T(8,128)(2,1)S(1)}, bf16[256,384]{1,0:T(8,128)(2,1)S(1)}, u32[]{:S(2)}, u32[]{:S(2)}) %collective-permute-start.7) | collective-permute-done | bytes 196640 | tf_op jit(solution)/shard_map/ppermute | solution.py:31
  53.4 3.5 %collective-permute-done.10 = bf16[256,384]{1,0:T(8,128)(2,1)S(1)} collective-permute-done((bf16[256,384]{1,0:T(8,128)(2,1)S(1)}, bf16[256,384]{1,0:T(8,128)(2,1)S(1)}, u32[]{:S(2)}, u32[]{:S(2)}) %collective-permute-start.10) | collective-permute-done | bytes 196640 | tf_op jit(solution)/shard_map/ppermute | solution.py:31
  61.3 2.5 %collective-permute-start.13 = (bf16[192,128]{1,0:T(8,128)(2,1)}, bf16[192,128]{1,0:T(8,128)(2,1)}, u32[]{:S(2)}, u32[]{:S(2)}) collective-permute-start(bf16[192,128]{1,0:T(8,128)(2,1)} %get-tuple-element.292), channel_id=1, source_target_pairs={{0,4},{4,0},{8,12},{12,8},{16,20},{20,16},{24,28},{28,24},{1,5},{5... | collective-permute-start | bytes 147464 | tf_op jit(solution)/shard_map/ppermute | solution.py:36
  63.8 3.8 %all-to-all-start.1 = ((f32[32,1,128]{2,1,0:T(1,128)}), f32[32,1,128]{2,1,0:T(1,128)S(1)}, u32[]{:S(2)}, u32[]{:S(2)}) async-start(f32[32,1,128]{2,1,0:T(1,128)} %bitcast.23), calls=%async_computation.1 | async-start | bytes 32768 | tf_op jit(solution)/shard_map/all_to_all | solution.py:544
  70.5 4.1 %all-to-all-done.1 = f32[32,1,128]{2,1,0:T(1,128)S(1)} async-done(((f32[32,1,128]{2,1,0:T(1,128)}), f32[32,1,128]{2,1,0:T(1,128)S(1)}, u32[]{:S(2)}, u32[]{:S(2)}) %all-to-all-start.1) | async-done | bytes 16416 | tf_op jit(solution)/shard_map/all_to_all | solution.py:544
  80.2 1.8 %shard_map.116 = (f32[192,1152]{1,0:T(8,128)S(1)}, bf16[192,1152]{1,0:T(8,128)(2,1)S(1)}) custom-call(s32[1,1]{1,0:T(1,128)} %bitcast.1.strand_ref.refs_0_.refs_1_, bf16[768,256]{1,0:T(8,128)(2,1)S(1)} %copy-done.30, bf16[256,384]{1,0:T(8,128)(2,1)S(1)} %get-tuple-element.198.refs_2_, bf16[768,256]{1,0:T(8,128)(2,1)S(1)} %collective-permute-done.16.refs_3_, ...), custom_call_target="tpu_custom_call" | custom-call | flops 1 | bytes 1 | tf_op jit(solution)/shard_map/pallas_call | solution.py:79
  82.6 2.4 %collective-permute-done.15 = bf16[256,384]{1,0:T(8,128)(2,1)S(1)} collective-permute-done((bf16[256,384]{1,0:T(8,128)(2,1)S(1)}, bf16[256,384]{1,0:T(8,128)(2,1)S(1)}, u32[]{:S(2)}, u32[]{:S(2)}) %collective-permute-start.15) | collective-permute-done | bytes 196640 | tf_op jit(solution)/shard_map/ppermute | solution.py:31
  87.5 2.9 %shard_map.118 = (f32[192,1152]{1,0:T(8,128)S(1)}, bf16[192,1152]{1,0:T(8,128)(2,1)S(1)}) custom-call(s32[1,1]{1,0:T(1,128)} %bitcast.1.strand_ref.refs_0_.refs_1_, bf16[768,256]{1,0:T(8,128)(2,1)} %shard_map.112.refs_1_, bf16[256,384]{1,0:T(8,128)(2,1)S(1)} %get-tuple-element.205.refs_2_, bf16[768,256]{1,0:T(8,128)(2,1)} %collective-permute-done.14.refs_3_, ...), custom_call_target="tpu_custom_call" | custom-call | flops 1 | bytes 1 | tf_op jit(solution)/shard_map/pallas_call | solution.py:79
  91.0 2.5 %collective-permute-done.18 = bf16[256,384]{1,0:T(8,128)(2,1)S(1)} collective-permute-done((bf16[256,384]{1,0:T(8,128)(2,1)S(1)}, bf16[256,384]{1,0:T(8,128)(2,1)S(1)}, u32[]{:S(2)}, u32[]{:S(2)}) %collective-permute-start.18) | collective-permute-done | bytes 196640 | tf_op jit(solution)/shard_map/ppermute | solution.py:31
  95.9 1.8 %shard_map.120 = (f32[192,1152]{1,0:T(8,128)S(1)}, bf16[192,1152]{1,0:T(8,128)(2,1)S(1)}) custom-call(s32[1,1]{1,0:T(1,128)} %bitcast.1.strand_ref.refs_0_.refs_1_, bf16[768,256]{1,0:T(8,128)(2,1)S(1)} %copy-done.24, bf16[256,384]{1,0:T(8,128)(2,1)S(1)} %get-tuple-element.215.refs_2_, bf16[768,256]{1,0:T(8,128)(2,1)S(1)} %copy-done.37, ...), custom_call_target="tpu_custom_call" | custom-call | flops 1 | bytes 1 | tf_op jit(solution)/shard_map/pallas_call | solution.py:79
  98.4 3.4 %collective-permute-done.20 = bf16[256,384]{1,0:T(8,128)(2,1)S(1)} collective-permute-done((bf16[256,384]{1,0:T(8,128)(2,1)S(1)}, bf16[256,384]{1,0:T(8,128)(2,1)S(1)}, u32[]{:S(2)}, u32[]{:S(2)}) %collective-permute-start.20) | collective-permute-done | bytes 196640 | tf_op jit(solution)/shard_map/ppermute | solution.py:31
  103.5 5.0 %collective-permute-done.24.refs_1_ = bf16[96,1152]{1,0:T(8,128)(2,1)S(1)} collective-permute-done((bf16[96,1152]{1,0:T(8,128)(2,1)S(1)}, bf16[96,1152]{1,0:T(8,128)(2,1)S(1)}, u32[]{:S(2)}, u32[]{:S(2)}) %collective-permute-start.24) | collective-permute-done | bytes 221216 | tf_op jit(solution)/shard_map/ppermute | solution.py:36
  108.7 1.8 %shard_map.123 = (f32[192,1152]{1,0:T(8,128)S(1)}, bf16[192,1152]{1,0:T(8,128)(2,1)S(1)}) custom-call(s32[1,1]{1,0:T(1,128)} %bitcast.1.strand_ref.refs_0_.refs_1_, bf16[768,256]{1,0:T(8,128)(2,1)S(1)} %copy-done.20, bf16[256,384]{1,0:T(8,128)(2,1)S(1)} %get-tuple-element.228.refs_2_, bf16[768,256]{1,0:T(8,128)(2,1)S(1)} %copy-done.35, ...), custom_call_target="tpu_custom_call" | custom-call | flops 1 | bytes 1 | tf_op jit(solution)/shard_map/pallas_call | solution.py:79
  112.6 5.1 %collective-permute-done.23 = bf16[256,384]{1,0:T(8,128)(2,1)S(1)} collective-permute-done((bf16[256,384]{1,0:T(8,128)(2,1)S(1)}, bf16[256,384]{1,0:T(8,128)(2,1)S(1)}, u32[]{:S(2)}, u32[]{:S(2)}) %collective-permute-start.23) | collective-permute-done | bytes 196640 | tf_op jit(solution)/shard_map/ppermute | solution.py:31
  119.1 1.8 %collective-permute-start.35 = (bf16[96,1152]{1,0:T(8,128)(2,1)S(1)}, bf16[96,1152]{1,0:T(8,128)(2,1)S(1)}, u32[]{:S(2)}, u32[]{:S(2)}) collective-permute-start(bf16[96,1152]{1,0:T(8,128)(2,1)S(1)} %get-tuple-element.256), channel_id=1, source_target_pairs={{0,8},{4,12},{8,0},{12,4},{16,24},{20,28},{24,16},{28,20},{1,9},{5... | collective-permute-start | bytes 663560 | tf_op jit(solution)/shard_map/ppermute | solution.py:36
  125.3 2.6 %shard_map.126 = (f32[192,1152]{1,0:T(8,128)S(1)}, bf16[192,1152]{1,0:T(8,128)(2,1)}) custom-call(s32[1,1]{1,0:T(1,128)} %bitcast.1.strand_ref.refs_0_.refs_1_, bf16[768,256]{1,0:T(8,128)(2,1)S(1)} %copy-done.18, bf16[256,384]{1,0:T(8,128)(2,1)S(1)} %get-tuple-element.239.refs_2_, bf16[768,256]{1,0:T(8,128)(2,1)S(1)} %copy-done.33, ...), custom_call_target="tpu_custom_call" | custom-call | flops 1 | bytes 1 | tf_op jit(solution)/shard_map/pallas_call | solution.py:79
  131.0 2.4 %collective-permute-start.40 = (bf16[48,1152]{1,0:T(8,128)(2,1)}, bf16[48,1152]{1,0:T(8,128)(2,1)S(1)}, u32[]{:S(2)}, u32[]{:S(2)}) collective-permute-start(bf16[48,1152]{1,0:T(8,128)(2,1)} %get-tuple-element.273), channel_id=1, source_target_pairs={{0,16},{4,20},{8,24},{12,28},{16,0},{20,4},{24,8},{28,12},{1,17},{... | collective-permute-start | bytes 331784 | tf_op jit(solution)/shard_map/ppermute | solution.py:36
  136.6 4.0 %all-to-all-start.2 = ((bf16[8,24,512]{2,1,0:T(8,128)(2,1)}), bf16[8,24,512]{2,1,0:T(8,128)(2,1)}, u32[]{:S(2)}, u32[]{:S(2)}) async-start(bf16[8,24,512]{2,1,0:T(8,128)(2,1)} %bitcast.36), calls=%async_computation.2 | async-start | bytes 393216 | tf_op jit(solution)/shard_map/all_to_all | solution.py:642
  140.7 2.9 %collective-permute-start.43 = (bf16[192,128]{1,0:T(8,128)(2,1)S(1)}, bf16[192,128]{1,0:T(8,128)(2,1)}, u32[]{:S(2)}, u32[]{:S(2)}) collective-permute-start(bf16[192,128]{1,0:T(8,128)(2,1)S(1)} %fusion.93), channel_id=1, source_target_pairs={{0,16},{4,20},{8,24},{12,28},{16,0},{20,4},{24,8},{28,12},{1,17},{... | collective-permute-start | bytes 147464 | tf_op jit(solution)/shard_map/ppermute | solution.py:36
  145.2 8.4 %collective-permute-done.32.refs_1_ = bf16[96,1152]{1,0:T(8,128)(2,1)S(1)} collective-permute-done((bf16[96,1152]{1,0:T(8,128)(2,1)S(1)}, bf16[96,1152]{1,0:T(8,128)(2,1)S(1)}, u32[]{:S(2)}, u32[]{:S(2)}) %collective-permute-start.32) | collective-permute-done | bytes 221216 | tf_op jit(solution)/shard_map/ppermute | solution.py:36
  155.5 4.7 %all-to-all-start.3 = ((bf16[8,24,512]{2,1,0:T(8,128)(2,1)}), bf16[8,24,512]{2,1,0:T(8,128)(2,1)}, u32[]{:S(2)}, u32[]{:S(2)}) async-start(bf16[8,24,512]{2,1,0:T(8,128)(2,1)} %broadcast_in_dim.5), calls=%async_computation.3 | async-start | bytes 393216 | tf_op jit(solution)/shard_map/all_to_all | solution.py:646
  161.2 3.0 %collective-permute-start.42 = (bf16[48,1152]{1,0:T(8,128)(2,1)S(1)}, bf16[48,1152]{1,0:T(8,128)(2,1)S(1)}, u32[]{:S(2)}, u32[]{:S(2)}) collective-permute-start(bf16[48,1152]{1,0:T(8,128)(2,1)S(1)} %get-tuple-element.277), channel_id=1, source_target_pairs={{0,16},{4,20},{8,24},{12,28},{16,0},{20,4},{24,8},{28,12},{1,17},{... | collective-permute-start | bytes 331784 | tf_op jit(solution)/shard_map/ppermute | solution.py:36
  164.2 5.6 %fusion = f32[192,5313]{1,0:T(8,128)} fusion(bf16[128,5313]{1,0:T(8,128)(2,1)} %fusion.6, bf16[192,128]{1,0:T(8,128)(2,1)S(1)} %get-tuple-element.313, bf16[192,128]{1,0:T(8,128)(2,1)S(1)} %get-tuple-element.312, bf16[192,128]{1,0:T(8,128)(2,1)S(1)} %get-tuple-element.290), kind=kOutput, calls=%fused_computation | convolution fusion | flops 796117248 | bytes 5587968 | tf_op jit(solution)/shard_map/dot_general | solution.py:655
  171.2 1.8 %shard_map.136 = f32[5,3,192,96]{3,2,1,0:T(8,128)} custom-call(f32[48,1152]{1,0:T(8,128)S(1)} %get-tuple-element.247.refs_0_, bf16[48,1152]{1,0:T(8,128)(2,1)S(1)} %collective-permute-done.33.refs_1_, f32[48,1152]{1,0:T(8,128)S(1)} %get-tuple-element.276.refs_2_, bf16[48,1152]{1,0:T(8,128)(2,1)S(1)} %collective-permute-done.42.refs_3_, ...), custom_call_target="tpu_custom_call" | custom-call | flops 1 | bytes 1 | tf_op jit(solution)/shard_map/pallas_call | solution.py:405
  173.0 1.7 bitcast_convert_fusion
  (254 shorter events, 69.4 us)
Async XLA Ops:
  0.6 20.4 %collective-permute-start.3 = (bf16[5,3,192,768]{3,2,1,0:T(8,128)(2,1)}, bf16[5,3,192,768]{3,2,1,0:T(8,128)(2,1)}, u32[]{:S(2)}, u32[]{:S(2)}) collective-permute-start(bf16[5,3,192,768]{3,2,1,0:T(8,128)(2,1)} %own_ref.5), channel_id=1, source_target_pairs={{0,1},{1,0},{2,3},{3,2},{4,5},{5,4},{6,7},{7,6},{8,9},{9,8},{10,11... | collective-permute-start | bytes 13271048 | tf_op jit(solution)/shard_map/ppermute | solution.py:26
  1.2 14.2 %collective-permute-start.1 = (bf16[192,512]{1,0:T(8,128)(2,1)}, bf16[192,512]{1,0:T(8,128)(2,1)}, u32[]{:S(2)}, u32[]{:S(2)}) collective-permute-start(bf16[192,512]{1,0:T(8,128)(2,1)} %refs_0_.3), channel_id=1, source_target_pairs={{0,2},{1,3},{2,0},{3,1},{4,6},{5,7},{6,4},{7,5},{8,10},{9,11},{10,... | collective-permute-start | bytes 589832 | tf_op jit(solution)/shard_map/ppermute | solution.py:31
  3.7 14.6 %collective-permute-start = (bf16[192,512]{1,0:T(8,128)(2,1)}, bf16[192,512]{1,0:T(8,128)(2,1)}, u32[]{:S(2)}, u32[]{:S(2)}) collective-permute-start(bf16[192,512]{1,0:T(8,128)(2,1)} %refs_0_.3), channel_id=1, source_target_pairs={{0,1},{1,0},{2,3},{3,2},{4,5},{5,4},{6,7},{7,6},{8,9},{9,8},{10,11... | collective-permute-start | bytes 589832 | tf_op jit(solution)/shard_map/ppermute | solution.py:26
  5.6 12.7 %all-to-all-start = ((bf16[8,32,128]{2,1,0:T(8,128)(2,1)}), bf16[8,32,128]{2,1,0:T(8,128)(2,1)S(1)}, u32[]{:S(2)}, u32[]{:S(2)}) async-start(bf16[8,32,128]{2,1,0:T(8,128)(2,1)} %bitcast.2), calls=%async_computation | async-start | bytes 131072 | tf_op jit(solution)/shard_map/all_to_all | solution.py:441
  40.1 8.0 %collective-permute-start.9 = (bf16[768,256]{1,0:T(8,128)(2,1)S(1)}, bf16[768,256]{1,0:T(8,128)(2,1)S(1)}, u32[]{:S(2)}, u32[]{:S(2)}) collective-permute-start(bf16[768,256]{1,0:T(8,128)(2,1)S(1)} %shard_map.108.refs_1_), channel_id=1, source_target_pairs={{0,1},{1,0},{2,3},{3,2},{4,5},{5,4},{6,7},{7,6},{8,9},{9,8},{10,11... | collective-permute-start | bytes 1179656 | tf_op jit(solution)/shard_map/ppermute | solution.py:26
  41.0 7.1 %collective-permute-start.7 = (bf16[256,384]{1,0:T(8,128)(2,1)S(1)}, bf16[256,384]{1,0:T(8,128)(2,1)S(1)}, u32[]{:S(2)}, u32[]{:S(2)}) collective-permute-start(bf16[256,384]{1,0:T(8,128)(2,1)S(1)} %get-tuple-element.166), channel_id=1, source_target_pairs={{0,2},{1,3},{2,0},{3,1},{4,6},{5,7},{6,4},{7,5},{8,10},{9,11},{10,... | collective-permute-start | bytes 589832 | tf_op jit(solution)/shard_map/ppermute | solution.py:31
  49.0 7.9 %collective-permute-start.11 = (bf16[768,256]{1,0:T(8,128)(2,1)S(1)}, bf16[768,256]{1,0:T(8,128)(2,1)S(1)}, u32[]{:S(2)}, u32[]{:S(2)}) collective-permute-start(bf16[768,256]{1,0:T(8,128)(2,1)S(1)} %shard_map.110.refs_1_), channel_id=1, source_target_pairs={{0,1},{1,0},{2,3},{3,2},{4,5},{5,4},{6,7},{7,6},{8,9},{9,8},{10,11... | collective-permute-start | bytes 1179656 | tf_op jit(solution)/shard_map/ppermute | solution.py:26
  49.6 7.4 %collective-permute-start.10 = (bf16[256,384]{1,0:T(8,128)(2,1)S(1)}, bf16[256,384]{1,0:T(8,128)(2,1)S(1)}, u32[]{:S(2)}, u32[]{:S(2)}) collective-permute-start(bf16[256,384]{1,0:T(8,128)(2,1)S(1)} %get-tuple-element.176), channel_id=1, source_target_pairs={{0,2},{1,3},{2,0},{3,1},{4,6},{5,7},{6,4},{7,5},{8,10},{9,11},{10,... | collective-permute-start | bytes 589832 | tf_op jit(solution)/shard_map/ppermute | solution.py:31
  59.2 15.4 %collective-permute-start.14 = (bf16[768,256]{1,0:T(8,128)(2,1)}, bf16[768,256]{1,0:T(8,128)(2,1)}, u32[]{:S(2)}, u32[]{:S(2)}) collective-permute-start(bf16[768,256]{1,0:T(8,128)(2,1)} %shard_map.112.refs_1_), channel_id=1, source_target_pairs={{0,1},{1,0},{2,3},{3,2},{4,5},{5,4},{6,7},{7,6},{8,9},{9,8},{10,11... | collective-permute-start | bytes 1179656 | tf_op jit(solution)/shard_map/ppermute | solution.py:26
  61.3 7.6 %collective-permute-start.13 = (bf16[192,128]{1,0:T(8,128)(2,1)}, bf16[192,128]{1,0:T(8,128)(2,1)}, u32[]{:S(2)}, u32[]{:S(2)}) collective-permute-start(bf16[192,128]{1,0:T(8,128)(2,1)} %get-tuple-element.292), channel_id=1, source_target_pairs={{0,4},{4,0},{8,12},{12,8},{16,20},{20,16},{24,28},{28,24},{1,5},{5... | collective-permute-start | bytes 147464 | tf_op jit(solution)/shard_map/ppermute | solution.py:36
  63.8 10.8 %all-to-all-start.1 = ((f32[32,1,128]{2,1,0:T(1,128)}), f32[32,1,128]{2,1,0:T(1,128)S(1)}, u32[]{:S(2)}, u32[]{:S(2)}) async-start(f32[32,1,128]{2,1,0:T(1,128)} %bitcast.23), calls=%async_computation.1 | async-start | bytes 32768 | tf_op jit(solution)/shard_map/all_to_all | solution.py:544
  82.0 13.2 %collective-permute-start.21 = (bf16[192,1152]{1,0:T(8,128)(2,1)S(1)}, bf16[192,1152]{1,0:T(8,128)(2,1)S(1)}, u32[]{:S(2)}, u32[]{:S(2)}) collective-permute-start(bf16[192,1152]{1,0:T(8,128)(2,1)S(1)} %get-tuple-element.214), channel_id=1, source_target_pairs={{0,8},{4,12},{8,0},{12,4},{16,24},{20,28},{24,16},{28,20},{1,9},{5... | collective-permute-start | bytes 1327112 | tf_op jit(solution)/shard_map/ppermute | solution.py:36
  86.2 7.3 %collective-permute-start.18 = (bf16[256,384]{1,0:T(8,128)(2,1)S(1)}, bf16[256,384]{1,0:T(8,128)(2,1)S(1)}, u32[]{:S(2)}, u32[]{:S(2)}) collective-permute-start(bf16[256,384]{1,0:T(8,128)(2,1)S(1)} %bitcast.96), channel_id=1, source_target_pairs={{0,2},{1,3},{2,0},{3,1},{4,6},{5,7},{6,4},{7,5},{8,10},{9,11},{10,... | collective-permute-start | bytes 589832 | tf_op jit(solution)/shard_map/ppermute | solution.py:31
  90.4 13.1 %collective-permute-start.25 = (bf16[192,1152]{1,0:T(8,128)(2,1)S(1)}, bf16[192,1152]{1,0:T(8,128)(2,1)S(1)}, u32[]{:S(2)}, u32[]{:S(2)}) collective-permute-start(bf16[192,1152]{1,0:T(8,128)(2,1)S(1)} %get-tuple-element.227), channel_id=1, source_target_pairs={{0,4},{4,0},{8,12},{12,8},{16,20},{20,16},{24,28},{28,24},{1,5},{5... | collective-permute-start | bytes 1327112 | tf_op jit(solution)/shard_map/ppermute | solution.py:36
  94.6 7.3 %collective-permute-start.20 = (bf16[256,384]{1,0:T(8,128)(2,1)S(1)}, bf16[256,384]{1,0:T(8,128)(2,1)S(1)}, u32[]{:S(2)}, u32[]{:S(2)}) collective-permute-start(bf16[256,384]{1,0:T(8,128)(2,1)S(1)} %bitcast.94), channel_id=1, source_target_pairs={{0,2},{1,3},{2,0},{3,1},{4,6},{5,7},{6,4},{7,5},{8,10},{9,11},{10,... | collective-permute-start | bytes 589832 | tf_op jit(solution)/shard_map/ppermute | solution.py:31
  95.3 13.2 %collective-permute-start.24 = (bf16[96,1152]{1,0:T(8,128)(2,1)S(1)}, bf16[96,1152]{1,0:T(8,128)(2,1)S(1)}, u32[]{:S(2)}, u32[]{:S(2)}) collective-permute-start(bf16[96,1152]{1,0:T(8,128)(2,1)S(1)} %get-tuple-element.226), channel_id=1, source_target_pairs={{0,16},{4,20},{8,24},{12,28},{16,0},{20,4},{24,8},{28,12},{1,17},{... | collective-permute-start | bytes 663560 | tf_op jit(solution)/shard_map/ppermute | solution.py:36
  97.8 21.2 %collective-permute-start.29 = (bf16[192,1152]{1,0:T(8,128)(2,1)S(1)}, bf16[192,1152]{1,0:T(8,128)(2,1)S(1)}, u32[]{:S(2)}, u32[]{:S(2)}) collective-permute-start(bf16[192,1152]{1,0:T(8,128)(2,1)S(1)} %get-tuple-element.238), channel_id=1, source_target_pairs={{0,4},{4,0},{8,12},{12,8},{16,20},{20,16},{24,28},{28,24},{1,5},{5... | collective-permute-start | bytes 1327112 | tf_op jit(solution)/shard_map/ppermute | solution.py:36
  108.6 10.4 %collective-permute-start.28 = (bf16[96,1152]{1,0:T(8,128)(2,1)S(1)}, bf16[96,1152]{1,0:T(8,128)(2,1)S(1)}, u32[]{:S(2)}, u32[]{:S(2)}) collective-permute-start(bf16[96,1152]{1,0:T(8,128)(2,1)S(1)} %get-tuple-element.237), channel_id=1, source_target_pairs={{0,8},{4,12},{8,0},{12,4},{16,24},{20,28},{24,16},{28,20},{1,9},{5... | collective-permute-start | bytes 663560 | tf_op jit(solution)/shard_map/ppermute | solution.py:36
  110.5 17.4 %collective-permute-start.36 = (bf16[192,1152]{1,0:T(8,128)(2,1)S(1)}, bf16[192,1152]{1,0:T(8,128)(2,1)S(1)}, u32[]{:S(2)}, u32[]{:S(2)}) collective-permute-start(bf16[192,1152]{1,0:T(8,128)(2,1)S(1)} %get-tuple-element.257), channel_id=1, source_target_pairs={{0,4},{4,0},{8,12},{12,8},{16,20},{20,16},{24,28},{28,24},{1,5},{5... | collective-permute-start | bytes 1327112 | tf_op jit(solution)/shard_map/ppermute | solution.py:36
  119.1 8.8 %collective-permute-start.35 = (bf16[96,1152]{1,0:T(8,128)(2,1)S(1)}, bf16[96,1152]{1,0:T(8,128)(2,1)S(1)}, u32[]{:S(2)}, u32[]{:S(2)}) collective-permute-start(bf16[96,1152]{1,0:T(8,128)(2,1)S(1)} %get-tuple-element.256), channel_id=1, source_target_pairs={{0,8},{4,12},{8,0},{12,4},{16,24},{20,28},{24,16},{28,20},{1,9},{5... | collective-permute-start | bytes 663560 | tf_op jit(solution)/shard_map/ppermute | solution.py:36
  120.9 7.0 %collective-permute-start.27 = (bf16[256,384]{1,0:T(8,128)(2,1)S(1)}, bf16[256,384]{1,0:T(8,128)(2,1)S(1)}, u32[]{:S(2)}, u32[]{:S(2)}) collective-permute-start(bf16[256,384]{1,0:T(8,128)(2,1)S(1)} %bitcast.92), channel_id=1, source_target_pairs={{0,2},{1,3},{2,0},{3,1},{4,6},{5,7},{6,4},{7,5},{8,10},{9,11},{10,... | collective-permute-start | bytes 589832 | tf_op jit(solution)/shard_map/ppermute | solution.py:31
  128.7 7.9 %collective-permute-start.38 = (bf16[192,128]{1,0:T(8,128)(2,1)S(1)}, bf16[192,128]{1,0:T(8,128)(2,1)S(1)}, u32[]{:S(2)}, u32[]{:S(2)}) collective-permute-start(bf16[192,128]{1,0:T(8,128)(2,1)S(1)} %convert_element_type.95), channel_id=1, source_target_pairs={{0,8},{4,12},{8,0},{12,4},{16,24},{20,28},{24,16},{28,20},{1,9},{5... | collective-permute-start | bytes 147464 | tf_op jit(solution)/shard_map/ppermute | solution.py:36
  129.1 24.7 %collective-permute-start.39 = (bf16[48,1152]{1,0:T(8,128)(2,1)S(1)}, bf16[48,1152]{1,0:T(8,128)(2,1)S(1)}, u32[]{:S(2)}, u32[]{:S(2)}) collective-permute-start(bf16[48,1152]{1,0:T(8,128)(2,1)S(1)} %get-tuple-element.270), channel_id=1, source_target_pairs={{0,16},{4,20},{8,24},{12,28},{16,0},{20,4},{24,8},{28,12},{1,17},{... | collective-permute-start | bytes 331784 | tf_op jit(solution)/shard_map/ppermute | solution.py:36
  129.5 14.0 %collective-permute-start.31 = (bf16[192,1152]{1,0:T(8,128)(2,1)}, bf16[192,1152]{1,0:T(8,128)(2,1)S(1)}, u32[]{:S(2)}, u32[]{:S(2)}) collective-permute-start(bf16[192,1152]{1,0:T(8,128)(2,1)} %get-tuple-element.244), channel_id=1, source_target_pairs={{0,4},{4,0},{8,12},{12,8},{16,20},{20,16},{24,28},{28,24},{1,5},{5... | collective-permute-start | bytes 1327112 | tf_op jit(solution)/shard_map/ppermute | solution.py:36
  131.0 22.8 %collective-permute-start.40 = (bf16[48,1152]{1,0:T(8,128)(2,1)}, bf16[48,1152]{1,0:T(8,128)(2,1)S(1)}, u32[]{:S(2)}, u32[]{:S(2)}) collective-permute-start(bf16[48,1152]{1,0:T(8,128)(2,1)} %get-tuple-element.273), channel_id=1, source_target_pairs={{0,16},{4,20},{8,24},{12,28},{16,0},{20,4},{24,8},{28,12},{1,17},{... | collective-permute-start | bytes 331784 | tf_op jit(solution)/shard_map/ppermute | solution.py:36
  134.2 19.7 %collective-permute-start.41 = (bf16[96,1152]{1,0:T(8,128)(2,1)}, bf16[96,1152]{1,0:T(8,128)(2,1)S(1)}, u32[]{:S(2)}, u32[]{:S(2)}) collective-permute-start(bf16[96,1152]{1,0:T(8,128)(2,1)} %get-tuple-element.274), channel_id=1, source_target_pairs={{0,8},{4,12},{8,0},{12,4},{16,24},{20,28},{24,16},{28,20},{1,9},{5... | collective-permute-start | bytes 663560 | tf_op jit(solution)/shard_map/ppermute | solution.py:36
  136.6 17.3 %all-to-all-start.2 = ((bf16[8,24,512]{2,1,0:T(8,128)(2,1)}), bf16[8,24,512]{2,1,0:T(8,128)(2,1)}, u32[]{:S(2)}, u32[]{:S(2)}) async-start(bf16[8,24,512]{2,1,0:T(8,128)(2,1)} %bitcast.36), calls=%async_computation.2 | async-start | bytes 393216 | tf_op jit(solution)/shard_map/all_to_all | solution.py:642
  140.7 13.2 %collective-permute-start.43 = (bf16[192,128]{1,0:T(8,128)(2,1)S(1)}, bf16[192,128]{1,0:T(8,128)(2,1)}, u32[]{:S(2)}, u32[]{:S(2)}) collective-permute-start(bf16[192,128]{1,0:T(8,128)(2,1)S(1)} %fusion.93), channel_id=1, source_target_pairs={{0,16},{4,20},{8,24},{12,28},{16,0},{20,4},{24,8},{28,12},{1,17},{... | collective-permute-start | bytes 147464 | tf_op jit(solution)/shard_map/ppermute | solution.py:36
  143.6 9.9 %collective-permute-start.32 = (bf16[96,1152]{1,0:T(8,128)(2,1)S(1)}, bf16[96,1152]{1,0:T(8,128)(2,1)S(1)}, u32[]{:S(2)}, u32[]{:S(2)}) collective-permute-start(bf16[96,1152]{1,0:T(8,128)(2,1)S(1)} %get-tuple-element.246), channel_id=1, source_target_pairs={{0,8},{4,12},{8,0},{12,4},{16,24},{20,28},{24,16},{28,20},{1,9},{5... | collective-permute-start | bytes 663560 | tf_op jit(solution)/shard_map/ppermute | solution.py:36
  153.6 16.2 %collective-permute-start.33 = (bf16[48,1152]{1,0:T(8,128)(2,1)S(1)}, bf16[48,1152]{1,0:T(8,128)(2,1)S(1)}, u32[]{:S(2)}, u32[]{:S(2)}) collective-permute-start(bf16[48,1152]{1,0:T(8,128)(2,1)S(1)} %get-tuple-element.248), channel_id=1, source_target_pairs={{0,16},{4,20},{8,24},{12,28},{16,0},{20,4},{24,8},{28,12},{1,17},{... | collective-permute-start | bytes 331784 | tf_op jit(solution)/shard_map/ppermute | solution.py:36
  155.5 17.4 %all-to-all-start.3 = ((bf16[8,24,512]{2,1,0:T(8,128)(2,1)}), bf16[8,24,512]{2,1,0:T(8,128)(2,1)}, u32[]{:S(2)}, u32[]{:S(2)}) async-start(bf16[8,24,512]{2,1,0:T(8,128)(2,1)} %broadcast_in_dim.5), calls=%async_computation.3 | async-start | bytes 393216 | tf_op jit(solution)/shard_map/all_to_all | solution.py:646
  161.2 10.0 %collective-permute-start.42 = (bf16[48,1152]{1,0:T(8,128)(2,1)S(1)}, bf16[48,1152]{1,0:T(8,128)(2,1)S(1)}, u32[]{:S(2)}, u32[]{:S(2)}) collective-permute-start(bf16[48,1152]{1,0:T(8,128)(2,1)S(1)} %get-tuple-element.277), channel_id=1, source_target_pairs={{0,16},{4,20},{8,24},{12,28},{16,0},{20,4},{24,8},{28,12},{1,17},{... | collective-permute-start | bytes 331784 | tf_op jit(solution)/shard_map/ppermute | solution.py:36
  (67 other events, 383.8 us)
